TPU v7x, 32 devices: a whole 2x2x4 slice. The times are simulated.
32 devices in a mesh: tm: 4 (over z), tile: 8 (over y, x, core).
Axes of the slice: x: 2, y: 2, z: 4, core: 2. Of those that a mesh axis runs over, the one named last changes fastest.
Arguments:
- heads: float32 [4, 3, 128, 4096], P('tm', None, 'tile'), may hold values from -6 to 6
- capacity: float32 [128, 4096], P('tile'), may hold values from 0.5 to 2
- cond_row: float32 [128, 4096], P('tile'), may hold values from 0.1 to 1
- cond_col: float32 [128, 4096], P('tile'), may hold values from 0.1 to 1
- terminal: float32 [2, 128, 4096], P(None, 'tile'), may hold values from -6 to 6
- obs_cell: int32 [4, 2, 512], P('tm'), may hold values from 0 to 524287
- obs_weight: float32 [4, 2, 2, 512], P('tm'), may hold values from -8 to 8
- block_mask: int32 [1, 32], replicated, may hold values 0 or 1
Outputs:
- adjoint_start: float32 [4, 2, 128, 4096], P('tm', None, 'tile')
- cond_sens: float32 [128, 4096], P('tile', 'tm')
- storage_sens: float32 [2], replicated
Inputs may be any that keep to these rules, and one draw needn't show every extreme that they name: `obs_cell`: row * 4096 + column of an observed cell; a cell may repeat.
All inputs are finite; a program needn't handle non-finite values.
Results may differ from a plain program's by a relative error of at most 0.0003.
Values sent between devices are 32-bit elements; how exact they have to be, the bound alone decides.
No kernel may reach another device: no remote copies, remote signals or barrier semaphores. Data moves between devices by JAX's collectives and lax.ppermute only.
A program may use at most 64 MiB of HBM per device.

v0:
```python
import jax
import jax.numpy as jnp
from jax import lax
from jax.sharding import PartitionSpec as P

BLOCK = 128
STEPS = 2
SWEEPS = 2


def shifted(value, axis, steps):
    count = lax.axis_size(axis)
    leading, last = (max(0, -steps), min(count, count - steps))
    return lax.ppermute(value, axis, [(source, source + steps) for source in range(leading, last)])


def with_halo(value, sides, width):
    for axis, dim in sides:
        size, length = (lax.axis_size(axis), value.shape[dim])
        up = [(i, (i + 1) % size) for i in range(size - 1)]
        down = [(j, i) for i, j in up]
        last = lax.slice_in_dim(value, length - width, length, axis=dim)
        leading = lax.slice_in_dim(value, 0, width, axis=dim)
        before = lax.ppermute(last, axis, up)
        after = lax.ppermute(leading, axis, down)
        value = jnp.concatenate([before, value, after], axis=dim)
    return value


def shards(heads, capacity, cond_row, cond_col, terminal, obs_cell, obs_weight, block_mask):
    rows_here = capacity.shape[0]
    width = capacity.shape[1]
    members = terminal.shape[0]
    tile_index = lax.axis_index("tile")
    section = lax.axis_index("tm")
    sections = lax.axis_size("tm")
    global_rows = tile_index * rows_here + jnp.arange(rows_here + 1, dtype=jnp.int32)
    block_rows = block_mask.shape[0]
    picker = (
        global_rows[:, None] // BLOCK == jnp.arange(block_rows, dtype=jnp.int32)[None, :]
    ).astype(jnp.float32)
    coarse = jnp.dot(picker, block_mask.astype(jnp.float32), precision=lax.Precision.HIGHEST)
    active_all = jnp.repeat(coarse, BLOCK, axis=1)
    active = active_all[:-1]
    next_active = active_all[1:]
    zero_col = jnp.zeros((rows_here, 1), jnp.float32)
    pair = active * jnp.concatenate([active[:, 1:], zero_col], axis=1)
    east = cond_row * pair
    west = jnp.concatenate([zero_col, east[:, :-1]], axis=1)
    south = cond_col * active * next_active
    upper_rim = shifted(south[-1:], "tile", 1)
    north = jnp.concatenate([upper_rim, south[:-1]], axis=0)
    diagonal = capacity + east + west + south + north
    cell_row = obs_cell[0] // width
    cell_col = obs_cell[0] % width
    local_row = cell_row - tile_index * rows_here
    inside = (local_row >= 0) & (local_row < rows_here)
    local_row = jnp.where(inside, local_row, rows_here)
    row_range = jnp.arange(rows_here, dtype=jnp.int32)
    col_range = jnp.arange(width, dtype=jnp.int32)
    groups = 1
    per_group = members // groups
    rounds = sections + groups - 1
    zero_cols = jnp.zeros((per_group, rows_here, 1), jnp.float32)

    def forcing(step):
        weights = obs_weight[0, step]
        row_hit = (local_row[step][None, :] == row_range[:, None]).astype(jnp.float32)
        col_hit = (cell_col[step][:, None] == col_range[None, :]).astype(jnp.float32)
        weighted_rows = weights[:, None, :] * row_hit[None, :, :]
        return jnp.einsum("gro,oc->grc", weighted_rows, col_hit, precision=lax.Precision.HIGHEST)

    def relax(field, rhs):
        padded = with_halo(field, (("tile", 1),), 1)
        above = padded[:, :-2]
        below = padded[:, 2:]
        left = jnp.concatenate([zero_cols, field[:, :, :-1]], axis=2)
        right = jnp.concatenate([field[:, :, 1:], zero_cols], axis=2)
        return (rhs + east * right + west * left + south * below + north * above) / diagonal

    def one_round(turn, carry):
        incoming, adjoint_out, sens_local, storage_part = carry
        group = turn - (sections - 1 - section)
        valid = (group >= 0) & (group < groups)
        field = jnp.where(section == sections - 1, terminal, incoming)
        sens_add = jnp.zeros((rows_here, width), jnp.float32)
        store_add = jnp.zeros((per_group,), jnp.float32)
        for step in reversed(range(STEPS)):
            rhs = active * (capacity * field + forcing(step))
            for sweep_index in range(SWEEPS):
                field = relax(field, rhs)
            later = heads[0, step + 1]
            earlier = heads[0, step]
            head_step = jnp.concatenate([later[:, 1:] - later[:, :-1], zero_col], axis=1)
            adj_step = jnp.concatenate([field[:, :, 1:] - field[:, :, :-1], zero_cols], axis=2)
            sens_add = sens_add + jnp.sum(adj_step * head_step * pair, axis=0)
            store_add = store_add + jnp.sum(field * capacity * (later - earlier), axis=(1, 2))
        sens_local = sens_local + jnp.where(valid, sens_add, 0.0)
        old_store = storage_part
        storage_part = jnp.where(valid, old_store + store_add, old_store)
        old_field = adjoint_out
        adjoint_out = jnp.where(valid, field, old_field)
        incoming = shifted(field, "tm", -1)
        return (incoming, adjoint_out, sens_local, storage_part)

    start = (
        jnp.zeros((per_group, rows_here, width), jnp.float32),
        jnp.zeros((members, rows_here, width), jnp.float32),
        jnp.zeros((rows_here, width), jnp.float32),
        jnp.zeros((members,), jnp.float32),
    )
    incoming, adjoint_out, sens_local, storage_part = lax.fori_loop(0, rounds, one_round, start)
    storage = lax.psum(storage_part, ("tm", "tile"))
    sens = lax.psum_scatter(sens_local, "tm", scatter_dimension=1, tiled=True)
    return (adjoint_out[None], sens, storage)


def solution(mesh):
    placed = (
        P("tm", None, "tile", None),
        P("tile", None),
        P("tile", None),
        P("tile", None),
        P(None, "tile", None),
        P("tm", None, None),
        P("tm", None, None, None),
        P(),
    )
    return jax.shard_map(
        shards,
        mesh=mesh,
        in_specs=placed,
        out_specs=(P("tm", None, "tile", None), P("tile", "tm"), P()),
        check_vma=False,
    )
```

profile of v0, /device:TPU:0, one launch (start us, length us, event | category | flops | bytes accessed | tf_op | source)
XLA Modules:
  0.0 299.5 jit_solution(6167967518200223891)
XLA Ops:
  10.1 2.4 collective-permute-start.9
  16.0 233.9 %while.23 = (s32[]{:T(128)}, f32[2,16,4096]{2,1,0:T(8,128)S(1)}, f32[2,16,4096]{2,1,0:T(8,128)S(1)}, f32[16,4096]{1,0:T(8,128)}, f32[2]{0:T(128)}, /*index=5*/f3...) while((s32[]{:T(128)}, f32[2,16,4096]{2,1,0:T(8,128)S(1)}, ...), condition=%wide.region_5.6_spmd.clone.clone, body=%wide.region_0.5_spmd.clone.clone.sunk | while | flops 1623785472 | bytes 51633208 | solution.py:112
  16.1 5.1 %collective-permute-start = (f32[2,1,4096]{2,1,0:T(1,128)S(1)}, f32[2,1,4096]{2,1,0:T(1,128)}, u32[]{:S(2)}, u32[]{:S(2)}) collective-permute-start(f32[2,1,4096]{2,1,0:T(1,128)S(1)} %get-tuple-element.903), channel_id=1, source_target_pairs={{0,1},{1,2},{2,3},{3,4},{4,5},{5,6},{6,7},{8,9},{9,10},{10,11},{11... | collective-permute-start | bytes 98312 | tf_op jit(solution)/shard_map/while/body/eval_jaxpr/ppermute | solution.py:24
  26.9 4.4 %fusion.85 = (f32[2,16,4096]{2,1,0:T(8,128)S(1)}, f32[2,16,4096]{2,1,0:T(8,128)S(1)}) fusion(f32[2,16,4096]{2,1,0:T(8,128)S(1)} %broadcast_select_fusion.5, f32[2,1,4096]{2,1,0:T(1,128)} %collective-permute-done, f32[2,1,4096]{2,1,0:T(1,128)} %collective-permute-done.1, f32[2,16,4095]{2,1,0:T(8,128)} %get-tuple-element.905, ...), kind=kOutput, calls=%fused_computation.40.clone.1 | convolution fusion | flops 809254912 | bytes 4560640 | tf_op jit(solution)/shard_map/while/body/eval_jaxpr/gro,oc->grc/dot_general | solution.py:71
  31.4 3.0 %collective-permute-start.2 = (f32[2,1,4096]{2,1,0:T(1,128)S(1)}, f32[2,1,4096]{2,1,0:T(1,128)S(1)}, u32[]{:S(2)}, u32[]{:S(2)}) collective-permute-start(f32[2,1,4096]{2,1,0:T(1,128)S(1)} %get-tuple-element.911), channel_id=1, source_target_pairs={{0,1},{1,2},{2,3},{3,4},{4,5},{5,6},{6,7},{8,9},{9,10},{10,11},{11... | collective-permute-start | bytes 98312 | tf_op jit(solution)/shard_map/while/body/eval_jaxpr/ppermute | solution.py:24
  35.9 2.2 collective-permute-done.3
  38.6 4.5 %collective-permute-start.4 = (f32[2,1,4096]{2,1,0:T(1,128)S(1)}, f32[2,1,4096]{2,1,0:T(1,128)S(1)}, u32[]{:S(2)}, u32[]{:S(2)}) collective-permute-start(f32[2,1,4096]{2,1,0:T(1,128)S(1)} %get-tuple-element.916), channel_id=1, source_target_pairs={{0,1},{1,2},{2,3},{3,4},{4,5},{5,6},{6,7},{8,9},{9,10},{10,11},{11... | collective-permute-start | bytes 98312 | tf_op jit(solution)/shard_map/while/body/eval_jaxpr/ppermute | solution.py:24
  43.2 1.4 collective-permute-start.5
  44.8 1.8 collective-permute-done.5
  46.7 3.2 %fusion.91 = (f32[2,16,4096]{2,1,0:T(8,128)S(1)}, f32[2,16,4096]{2,1,0:T(8,128)S(1)}) fusion(f32[2,16,4096]{2,1,0:T(8,128)S(1)} %fusion.88, f32[2,1,4096]{2,1,0:T(1,128)S(1)} %collective-permute-done.4, f32[2,1,4096]{2,1,0:T(1,128)S(1)} %collective-permute-done.5, f32[2,16,4095]{2,1,0:T(8,128)S(1)} %get-tuple-element.918, ...), kind=kOutput, calls=%fused_computation.26.clone.1 | convolution fusion | flops 809254912 | bytes 4560640 | tf_op jit(solution)/shard_map/while/body/eval_jaxpr/gro,oc->grc/dot_general | solution.py:71
  50.0 6.3 %collective-permute-start.6 = (f32[2,1,4096]{2,1,0:T(1,128)S(1)}, f32[2,1,4096]{2,1,0:T(1,128)S(1)}, u32[]{:S(2)}, u32[]{:S(2)}) collective-permute-start(f32[2,1,4096]{2,1,0:T(1,128)S(1)} %get-tuple-element.924), channel_id=1, source_target_pairs={{0,1},{1,2},{2,3},{3,4},{4,5},{5,6},{6,7},{8,9},{9,10},{10,11},{11... | collective-permute-start | bytes 98312 | tf_op jit(solution)/shard_map/while/body/eval_jaxpr/ppermute | solution.py:24
  56.4 1.4 collective-permute-start.7
  58.0 1.6 collective-permute-done.7
  62.9 12.1 %collective-permute-done.8 = f32[2,16,4096]{2,1,0:T(8,128)S(1)} collective-permute-done((f32[2,16,4096]{2,1,0:T(8,128)S(1)}, f32[2,16,4096]{2,1,0:T(8,128)S(1)}, u32[]{:S(2)}, u32[]{:S(2)}) %collective-permute-start.8) | collective-permute-done | bytes 524320 | tf_op jit(solution)/shard_map/while/body/eval_jaxpr/ppermute | solution.py:14
  75.1 4.5 %collective-permute-start = (f32[2,1,4096]{2,1,0:T(1,128)S(1)}, f32[2,1,4096]{2,1,0:T(1,128)}, u32[]{:S(2)}, u32[]{:S(2)}) collective-permute-start(f32[2,1,4096]{2,1,0:T(1,128)S(1)} %get-tuple-element.903), channel_id=1, source_target_pairs={{0,1},{1,2},{2,3},{3,4},{4,5},{5,6},{6,7},{8,9},{9,10},{10,11},{11... | collective-permute-start | bytes 98312 | tf_op jit(solution)/shard_map/while/body/eval_jaxpr/ppermute | solution.py:24
  85.2 4.4 %fusion.85 = (f32[2,16,4096]{2,1,0:T(8,128)S(1)}, f32[2,16,4096]{2,1,0:T(8,128)S(1)}) fusion(f32[2,16,4096]{2,1,0:T(8,128)S(1)} %broadcast_select_fusion.5, f32[2,1,4096]{2,1,0:T(1,128)} %collective-permute-done, f32[2,1,4096]{2,1,0:T(1,128)} %collective-permute-done.1, f32[2,16,4095]{2,1,0:T(8,128)} %get-tuple-element.905, ...), kind=kOutput, calls=%fused_computation.40.clone.1 | convolution fusion | flops 809254912 | bytes 4560640 | tf_op jit(solution)/shard_map/while/body/eval_jaxpr/gro,oc->grc/dot_general | solution.py:71
  89.7 3.3 %collective-permute-start.2 = (f32[2,1,4096]{2,1,0:T(1,128)S(1)}, f32[2,1,4096]{2,1,0:T(1,128)S(1)}, u32[]{:S(2)}, u32[]{:S(2)}) collective-permute-start(f32[2,1,4096]{2,1,0:T(1,128)S(1)} %get-tuple-element.911), channel_id=1, source_target_pairs={{0,1},{1,2},{2,3},{3,4},{4,5},{5,6},{6,7},{8,9},{9,10},{10,11},{11... | collective-permute-start | bytes 98312 | tf_op jit(solution)/shard_map/while/body/eval_jaxpr/ppermute | solution.py:24
  94.6 2.8 collective-permute-done.3
  97.8 4.5 %collective-permute-start.4 = (f32[2,1,4096]{2,1,0:T(1,128)S(1)}, f32[2,1,4096]{2,1,0:T(1,128)S(1)}, u32[]{:S(2)}, u32[]{:S(2)}) collective-permute-start(f32[2,1,4096]{2,1,0:T(1,128)S(1)} %get-tuple-element.916), channel_id=1, source_target_pairs={{0,1},{1,2},{2,3},{3,4},{4,5},{5,6},{6,7},{8,9},{9,10},{10,11},{11... | collective-permute-start | bytes 98312 | tf_op jit(solution)/shard_map/while/body/eval_jaxpr/ppermute | solution.py:24
  102.4 1.4 collective-permute-start.5
  104.1 1.6 collective-permute-done.5
  105.7 3.2 %fusion.91 = (f32[2,16,4096]{2,1,0:T(8,128)S(1)}, f32[2,16,4096]{2,1,0:T(8,128)S(1)}) fusion(f32[2,16,4096]{2,1,0:T(8,128)S(1)} %fusion.88, f32[2,1,4096]{2,1,0:T(1,128)S(1)} %collective-permute-done.4, f32[2,1,4096]{2,1,0:T(1,128)S(1)} %collective-permute-done.5, f32[2,16,4095]{2,1,0:T(8,128)S(1)} %get-tuple-element.918, ...), kind=kOutput, calls=%fused_computation.26.clone.1 | convolution fusion | flops 809254912 | bytes 4560640 | tf_op jit(solution)/shard_map/while/body/eval_jaxpr/gro,oc->grc/dot_general | solution.py:71
  108.9 5.7 %collective-permute-start.6 = (f32[2,1,4096]{2,1,0:T(1,128)S(1)}, f32[2,1,4096]{2,1,0:T(1,128)S(1)}, u32[]{:S(2)}, u32[]{:S(2)}) collective-permute-start(f32[2,1,4096]{2,1,0:T(1,128)S(1)} %get-tuple-element.924), channel_id=1, source_target_pairs={{0,1},{1,2},{2,3},{3,4},{4,5},{5,6},{6,7},{8,9},{9,10},{10,11},{11... | collective-permute-start | bytes 98312 | tf_op jit(solution)/shard_map/while/body/eval_jaxpr/ppermute | solution.py:24
  114.7 1.4 collective-permute-start.7
  116.3 1.6 collective-permute-done.7
  121.2 12.1 %collective-permute-done.8 = f32[2,16,4096]{2,1,0:T(8,128)S(1)} collective-permute-done((f32[2,16,4096]{2,1,0:T(8,128)S(1)}, f32[2,16,4096]{2,1,0:T(8,128)S(1)}, u32[]{:S(2)}, u32[]{:S(2)}) %collective-permute-start.8) | collective-permute-done | bytes 524320 | tf_op jit(solution)/shard_map/while/body/eval_jaxpr/ppermute | solution.py:14
  133.4 4.5 %collective-permute-start = (f32[2,1,4096]{2,1,0:T(1,128)S(1)}, f32[2,1,4096]{2,1,0:T(1,128)}, u32[]{:S(2)}, u32[]{:S(2)}) collective-permute-start(f32[2,1,4096]{2,1,0:T(1,128)S(1)} %get-tuple-element.903), channel_id=1, source_target_pairs={{0,1},{1,2},{2,3},{3,4},{4,5},{5,6},{6,7},{8,9},{9,10},{10,11},{11... | collective-permute-start | bytes 98312 | tf_op jit(solution)/shard_map/while/body/eval_jaxpr/ppermute | solution.py:24
  143.5 4.4 %fusion.85 = (f32[2,16,4096]{2,1,0:T(8,128)S(1)}, f32[2,16,4096]{2,1,0:T(8,128)S(1)}) fusion(f32[2,16,4096]{2,1,0:T(8,128)S(1)} %broadcast_select_fusion.5, f32[2,1,4096]{2,1,0:T(1,128)} %collective-permute-done, f32[2,1,4096]{2,1,0:T(1,128)} %collective-permute-done.1, f32[2,16,4095]{2,1,0:T(8,128)} %get-tuple-element.905, ...), kind=kOutput, calls=%fused_computation.40.clone.1 | convolution fusion | flops 809254912 | bytes 4560640 | tf_op jit(solution)/shard_map/while/body/eval_jaxpr/gro,oc->grc/dot_general | solution.py:71
  148.0 3.3 %collective-permute-start.2 = (f32[2,1,4096]{2,1,0:T(1,128)S(1)}, f32[2,1,4096]{2,1,0:T(1,128)S(1)}, u32[]{:S(2)}, u32[]{:S(2)}) collective-permute-start(f32[2,1,4096]{2,1,0:T(1,128)S(1)} %get-tuple-element.911), channel_id=1, source_target_pairs={{0,1},{1,2},{2,3},{3,4},{4,5},{5,6},{6,7},{8,9},{9,10},{10,11},{11... | collective-permute-start | bytes 98312 | tf_op jit(solution)/shard_map/while/body/eval_jaxpr/ppermute | solution.py:24
  152.9 2.8 collective-permute-done.3
  156.1 4.5 %collective-permute-start.4 = (f32[2,1,4096]{2,1,0:T(1,128)S(1)}, f32[2,1,4096]{2,1,0:T(1,128)S(1)}, u32[]{:S(2)}, u32[]{:S(2)}) collective-permute-start(f32[2,1,4096]{2,1,0:T(1,128)S(1)} %get-tuple-element.916), channel_id=1, source_target_pairs={{0,1},{1,2},{2,3},{3,4},{4,5},{5,6},{6,7},{8,9},{9,10},{10,11},{11... | collective-permute-start | bytes 98312 | tf_op jit(solution)/shard_map/while/body/eval_jaxpr/ppermute | solution.py:24
  160.7 1.4 collective-permute-start.5
  162.4 1.6 collective-permute-done.5
  164.0 3.2 %fusion.91 = (f32[2,16,4096]{2,1,0:T(8,128)S(1)}, f32[2,16,4096]{2,1,0:T(8,128)S(1)}) fusion(f32[2,16,4096]{2,1,0:T(8,128)S(1)} %fusion.88, f32[2,1,4096]{2,1,0:T(1,128)S(1)} %collective-permute-done.4, f32[2,1,4096]{2,1,0:T(1,128)S(1)} %collective-permute-done.5, f32[2,16,4095]{2,1,0:T(8,128)S(1)} %get-tuple-element.918, ...), kind=kOutput, calls=%fused_computation.26.clone.1 | convolution fusion | flops 809254912 | bytes 4560640 | tf_op jit(solution)/shard_map/while/body/eval_jaxpr/gro,oc->grc/dot_general | solution.py:71
  167.3 5.7 %collective-permute-start.6 = (f32[2,1,4096]{2,1,0:T(1,128)S(1)}, f32[2,1,4096]{2,1,0:T(1,128)S(1)}, u32[]{:S(2)}, u32[]{:S(2)}) collective-permute-start(f32[2,1,4096]{2,1,0:T(1,128)S(1)} %get-tuple-element.924), channel_id=1, source_target_pairs={{0,1},{1,2},{2,3},{3,4},{4,5},{5,6},{6,7},{8,9},{9,10},{10,11},{11... | collective-permute-start | bytes 98312 | tf_op jit(solution)/shard_map/while/body/eval_jaxpr/ppermute | solution.py:24
  174.6 1.6 collective-permute-done.7
  179.5 12.1 %collective-permute-done.8 = f32[2,16,4096]{2,1,0:T(8,128)S(1)} collective-permute-done((f32[2,16,4096]{2,1,0:T(8,128)S(1)}, f32[2,16,4096]{2,1,0:T(8,128)S(1)}, u32[]{:S(2)}, u32[]{:S(2)}) %collective-permute-start.8) | collective-permute-done | bytes 524320 | tf_op jit(solution)/shard_map/while/body/eval_jaxpr/ppermute | solution.py:14
  191.8 4.5 %collective-permute-start = (f32[2,1,4096]{2,1,0:T(1,128)S(1)}, f32[2,1,4096]{2,1,0:T(1,128)}, u32[]{:S(2)}, u32[]{:S(2)}) collective-permute-start(f32[2,1,4096]{2,1,0:T(1,128)S(1)} %get-tuple-element.903), channel_id=1, source_target_pairs={{0,1},{1,2},{2,3},{3,4},{4,5},{5,6},{6,7},{8,9},{9,10},{10,11},{11... | collective-permute-start | bytes 98312 | tf_op jit(solution)/shard_map/while/body/eval_jaxpr/ppermute | solution.py:24
  201.8 4.4 %fusion.85 = (f32[2,16,4096]{2,1,0:T(8,128)S(1)}, f32[2,16,4096]{2,1,0:T(8,128)S(1)}) fusion(f32[2,16,4096]{2,1,0:T(8,128)S(1)} %broadcast_select_fusion.5, f32[2,1,4096]{2,1,0:T(1,128)} %collective-permute-done, f32[2,1,4096]{2,1,0:T(1,128)} %collective-permute-done.1, f32[2,16,4095]{2,1,0:T(8,128)} %get-tuple-element.905, ...), kind=kOutput, calls=%fused_computation.40.clone.1 | convolution fusion | flops 809254912 | bytes 4560640 | tf_op jit(solution)/shard_map/while/body/eval_jaxpr/gro,oc->grc/dot_general | solution.py:71
  206.4 3.3 %collective-permute-start.2 = (f32[2,1,4096]{2,1,0:T(1,128)S(1)}, f32[2,1,4096]{2,1,0:T(1,128)S(1)}, u32[]{:S(2)}, u32[]{:S(2)}) collective-permute-start(f32[2,1,4096]{2,1,0:T(1,128)S(1)} %get-tuple-element.911), channel_id=1, source_target_pairs={{0,1},{1,2},{2,3},{3,4},{4,5},{5,6},{6,7},{8,9},{9,10},{10,11},{11... | collective-permute-start | bytes 98312 | tf_op jit(solution)/shard_map/while/body/eval_jaxpr/ppermute | solution.py:24
  211.2 2.8 collective-permute-done.3
  214.4 4.5 %collective-permute-start.4 = (f32[2,1,4096]{2,1,0:T(1,128)S(1)}, f32[2,1,4096]{2,1,0:T(1,128)S(1)}, u32[]{:S(2)}, u32[]{:S(2)}) collective-permute-start(f32[2,1,4096]{2,1,0:T(1,128)S(1)} %get-tuple-element.916), channel_id=1, source_target_pairs={{0,1},{1,2},{2,3},{3,4},{4,5},{5,6},{6,7},{8,9},{9,10},{10,11},{11... | collective-permute-start | bytes 98312 | tf_op jit(solution)/shard_map/while/body/eval_jaxpr/ppermute | solution.py:24
  220.7 1.6 collective-permute-done.5
  222.3 3.2 %fusion.91 = (f32[2,16,4096]{2,1,0:T(8,128)S(1)}, f32[2,16,4096]{2,1,0:T(8,128)S(1)}) fusion(f32[2,16,4096]{2,1,0:T(8,128)S(1)} %fusion.88, f32[2,1,4096]{2,1,0:T(1,128)S(1)} %collective-permute-done.4, f32[2,1,4096]{2,1,0:T(1,128)S(1)} %collective-permute-done.5, f32[2,16,4095]{2,1,0:T(8,128)S(1)} %get-tuple-element.918, ...), kind=kOutput, calls=%fused_computation.26.clone.1 | convolution fusion | flops 809254912 | bytes 4560640 | tf_op jit(solution)/shard_map/while/body/eval_jaxpr/gro,oc->grc/dot_general | solution.py:71
  225.6 5.7 %collective-permute-start.6 = (f32[2,1,4096]{2,1,0:T(1,128)S(1)}, f32[2,1,4096]{2,1,0:T(1,128)S(1)}, u32[]{:S(2)}, u32[]{:S(2)}) collective-permute-start(f32[2,1,4096]{2,1,0:T(1,128)S(1)} %get-tuple-element.924), channel_id=1, source_target_pairs={{0,1},{1,2},{2,3},{3,4},{4,5},{5,6},{6,7},{8,9},{9,10},{10,11},{11... | collective-permute-start | bytes 98312 | tf_op jit(solution)/shard_map/while/body/eval_jaxpr/ppermute | solution.py:24
  232.9 1.6 collective-permute-done.7
  237.8 12.1 %collective-permute-done.8 = f32[2,16,4096]{2,1,0:T(8,128)S(1)} collective-permute-done((f32[2,16,4096]{2,1,0:T(8,128)S(1)}, f32[2,16,4096]{2,1,0:T(8,128)S(1)}, u32[]{:S(2)}, u32[]{:S(2)}) %collective-permute-start.8) | collective-permute-done | bytes 524320 | tf_op jit(solution)/shard_map/while/body/eval_jaxpr/ppermute | solution.py:14
  250.0 42.7 %psum.7 = f32[2]{0:T(128)} all-reduce(f32[2]{0:T(128)} %get-tuple-element.1021), channel_id=1, replica_groups=mesh['tm'=4,'tile'=8] {'tm','tile'}, use_global_device_ids=true, to_apply=%region_7.8 | all-reduce | flops 2 | bytes 16 | tf_op jit(solution)/shard_map/psum | solution.py:113
  (297 shorter events, 56.2 us)
Async XLA Ops:
  7.2 285.5 %reduce-scatter.2.cloned.1.call-start = ((), (), s32[]{:S(2)}) async-start(), calls=%async_computation.1 | async-start | bytes 327680 | tf_op jit(solution)/shard_map/reduce_scatter | solution.py:114
  10.1 4.9 %collective-permute-start.9 = (f32[1,4096]{1,0:T(1,128)S(1)}, f32[1,4096]{1,0:T(1,128)S(1)}, u32[]{:S(2)}, u32[]{:S(2)}) collective-permute-start(f32[1,4096]{1,0:T(1,128)S(1)} %slice.501), channel_id=1, source_target_pairs={{0,1},{1,2},{2,3},{3,4},{4,5},{5,6},{6,7},{8,9},{9,10},{10,11},{11... | collective-permute-start | bytes 49160 | tf_op jit(solution)/shard_map/ppermute | solution.py:14
  16.1 10.7 %collective-permute-start = (f32[2,1,4096]{2,1,0:T(1,128)S(1)}, f32[2,1,4096]{2,1,0:T(1,128)}, u32[]{:S(2)}, u32[]{:S(2)}) collective-permute-start(f32[2,1,4096]{2,1,0:T(1,128)S(1)} %get-tuple-element.903), channel_id=1, source_target_pairs={{0,1},{1,2},{2,3},{3,4},{4,5},{5,6},{6,7},{8,9},{9,10},{10,11},{11... | collective-permute-start | bytes 98312 | tf_op jit(solution)/shard_map/while/body/eval_jaxpr/ppermute | solution.py:24
  21.2 5.6 %collective-permute-start.1 = (f32[2,1,4096]{2,1,0:T(1,128)S(1)}, f32[2,1,4096]{2,1,0:T(1,128)}, u32[]{:S(2)}, u32[]{:S(2)}) collective-permute-start(f32[2,1,4096]{2,1,0:T(1,128)S(1)} %get-tuple-element.904), channel_id=1, source_target_pairs={{1,0},{2,1},{3,2},{4,3},{5,4},{6,5},{7,6},{9,8},{10,9},{11,10},{12... | collective-permute-start | bytes 98312 | tf_op jit(solution)/shard_map/while/body/eval_jaxpr/ppermute | solution.py:25
  31.4 4.5 %collective-permute-start.2 = (f32[2,1,4096]{2,1,0:T(1,128)S(1)}, f32[2,1,4096]{2,1,0:T(1,128)S(1)}, u32[]{:S(2)}, u32[]{:S(2)}) collective-permute-start(f32[2,1,4096]{2,1,0:T(1,128)S(1)} %get-tuple-element.911), channel_id=1, source_target_pairs={{0,1},{1,2},{2,3},{3,4},{4,5},{5,6},{6,7},{8,9},{9,10},{10,11},{11... | collective-permute-start | bytes 98312 | tf_op jit(solution)/shard_map/while/body/eval_jaxpr/ppermute | solution.py:24
  34.4 3.8 %collective-permute-start.3 = (f32[2,1,4096]{2,1,0:T(1,128)S(1)}, f32[2,1,4096]{2,1,0:T(1,128)S(1)}, u32[]{:S(2)}, u32[]{:S(2)}) collective-permute-start(f32[2,1,4096]{2,1,0:T(1,128)S(1)} %get-tuple-element.912), channel_id=1, source_target_pairs={{1,0},{2,1},{3,2},{4,3},{5,4},{6,5},{7,6},{9,8},{10,9},{11,10},{12... | collective-permute-start | bytes 98312 | tf_op jit(solution)/shard_map/while/body/eval_jaxpr/ppermute | solution.py:25
  38.6 6.2 %collective-permute-start.4 = (f32[2,1,4096]{2,1,0:T(1,128)S(1)}, f32[2,1,4096]{2,1,0:T(1,128)S(1)}, u32[]{:S(2)}, u32[]{:S(2)}) collective-permute-start(f32[2,1,4096]{2,1,0:T(1,128)S(1)} %get-tuple-element.916), channel_id=1, source_target_pairs={{0,1},{1,2},{2,3},{3,4},{4,5},{5,6},{6,7},{8,9},{9,10},{10,11},{11... | collective-permute-start | bytes 98312 | tf_op jit(solution)/shard_map/while/body/eval_jaxpr/ppermute | solution.py:24
  43.2 3.5 %collective-permute-start.5 = (f32[2,1,4096]{2,1,0:T(1,128)S(1)}, f32[2,1,4096]{2,1,0:T(1,128)S(1)}, u32[]{:S(2)}, u32[]{:S(2)}) collective-permute-start(f32[2,1,4096]{2,1,0:T(1,128)S(1)} %get-tuple-element.917), channel_id=1, source_target_pairs={{1,0},{2,1},{3,2},{4,3},{5,4},{6,5},{7,6},{9,8},{10,9},{11,10},{12... | collective-permute-start | bytes 98312 | tf_op jit(solution)/shard_map/while/body/eval_jaxpr/ppermute | solution.py:25
  50.0 8.0 %collective-permute-start.6 = (f32[2,1,4096]{2,1,0:T(1,128)S(1)}, f32[2,1,4096]{2,1,0:T(1,128)S(1)}, u32[]{:S(2)}, u32[]{:S(2)}) collective-permute-start(f32[2,1,4096]{2,1,0:T(1,128)S(1)} %get-tuple-element.924), channel_id=1, source_target_pairs={{0,1},{1,2},{2,3},{3,4},{4,5},{5,6},{6,7},{8,9},{9,10},{10,11},{11... | collective-permute-start | bytes 98312 | tf_op jit(solution)/shard_map/while/body/eval_jaxpr/ppermute | solution.py:24
  56.4 3.2 %collective-permute-start.7 = (f32[2,1,4096]{2,1,0:T(1,128)S(1)}, f32[2,1,4096]{2,1,0:T(1,128)S(1)}, u32[]{:S(2)}, u32[]{:S(2)}) collective-permute-start(f32[2,1,4096]{2,1,0:T(1,128)S(1)} %get-tuple-element.925), channel_id=1, source_target_pairs={{1,0},{2,1},{3,2},{4,3},{5,4},{6,5},{7,6},{9,8},{10,9},{11,10},{12... | collective-permute-start | bytes 98312 | tf_op jit(solution)/shard_map/while/body/eval_jaxpr/ppermute | solution.py:25
  60.4 14.6 %collective-permute-start.8 = (f32[2,16,4096]{2,1,0:T(8,128)S(1)}, f32[2,16,4096]{2,1,0:T(8,128)S(1)}, u32[]{:S(2)}, u32[]{:S(2)}) collective-permute-start(f32[2,16,4096]{2,1,0:T(8,128)S(1)} %get-tuple-element.929), channel_id=1, source_target_pairs={{8,0},{16,8},{24,16},{9,1},{17,9},{25,17},{10,2},{18,10},{26,18},{... | collective-permute-start | bytes 1572872 | tf_op jit(solution)/shard_map/while/body/eval_jaxpr/ppermute | solution.py:14
  62.2 12.8 %copy-start.2 = (f32[2,16,4096]{2,1,0:T(8,128)S(1)}, f32[2,16,4096]{2,1,0:T(8,128)}, u32[]{:S(2)}) copy-start(f32[2,16,4096]{2,1,0:T(8,128)} %get-tuple-element.1043) | copy-start | bytes 1572868 | tf_op jit(solution)/shard_map/while
  62.2 12.8 %copy-start.18 = (s32[2,512]{1,0:T(2,128)S(1)}, s32[2,512]{1,0:T(2,128)}, u32[]{:S(2)}) copy-start(s32[2,512]{1,0:T(2,128)} %copy-done.17) | copy-start | bytes 12292 | tf_op jit(solution)/shard_map/while
  75.1 10.1 %collective-permute-start = (f32[2,1,4096]{2,1,0:T(1,128)S(1)}, f32[2,1,4096]{2,1,0:T(1,128)}, u32[]{:S(2)}, u32[]{:S(2)}) collective-permute-start(f32[2,1,4096]{2,1,0:T(1,128)S(1)} %get-tuple-element.903), channel_id=1, source_target_pairs={{0,1},{1,2},{2,3},{3,4},{4,5},{5,6},{6,7},{8,9},{9,10},{10,11},{11... | collective-permute-start | bytes 98312 | tf_op jit(solution)/shard_map/while/body/eval_jaxpr/ppermute | solution.py:24
  79.6 5.6 %collective-permute-start.1 = (f32[2,1,4096]{2,1,0:T(1,128)S(1)}, f32[2,1,4096]{2,1,0:T(1,128)}, u32[]{:S(2)}, u32[]{:S(2)}) collective-permute-start(f32[2,1,4096]{2,1,0:T(1,128)S(1)} %get-tuple-element.904), channel_id=1, source_target_pairs={{1,0},{2,1},{3,2},{4,3},{5,4},{6,5},{7,6},{9,8},{10,9},{11,10},{12... | collective-permute-start | bytes 98312 | tf_op jit(solution)/shard_map/while/body/eval_jaxpr/ppermute | solution.py:25
  89.7 4.8 %collective-permute-start.2 = (f32[2,1,4096]{2,1,0:T(1,128)S(1)}, f32[2,1,4096]{2,1,0:T(1,128)S(1)}, u32[]{:S(2)}, u32[]{:S(2)}) collective-permute-start(f32[2,1,4096]{2,1,0:T(1,128)S(1)} %get-tuple-element.911), channel_id=1, source_target_pairs={{0,1},{1,2},{2,3},{3,4},{4,5},{5,6},{6,7},{8,9},{9,10},{10,11},{11... | collective-permute-start | bytes 98312 | tf_op jit(solution)/shard_map/while/body/eval_jaxpr/ppermute | solution.py:24
  93.1 4.3 %collective-permute-start.3 = (f32[2,1,4096]{2,1,0:T(1,128)S(1)}, f32[2,1,4096]{2,1,0:T(1,128)S(1)}, u32[]{:S(2)}, u32[]{:S(2)}) collective-permute-start(f32[2,1,4096]{2,1,0:T(1,128)S(1)} %get-tuple-element.912), channel_id=1, source_target_pairs={{1,0},{2,1},{3,2},{4,3},{5,4},{6,5},{7,6},{9,8},{10,9},{11,10},{12... | collective-permute-start | bytes 98312 | tf_op jit(solution)/shard_map/while/body/eval_jaxpr/ppermute | solution.py:25
  97.8 6.2 %collective-permute-start.4 = (f32[2,1,4096]{2,1,0:T(1,128)S(1)}, f32[2,1,4096]{2,1,0:T(1,128)S(1)}, u32[]{:S(2)}, u32[]{:S(2)}) collective-permute-start(f32[2,1,4096]{2,1,0:T(1,128)S(1)} %get-tuple-element.916), channel_id=1, source_target_pairs={{0,1},{1,2},{2,3},{3,4},{4,5},{5,6},{6,7},{8,9},{9,10},{10,11},{11... | collective-permute-start | bytes 98312 | tf_op jit(solution)/shard_map/while/body/eval_jaxpr/ppermute | solution.py:24
  102.4 3.2 %collective-permute-start.5 = (f32[2,1,4096]{2,1,0:T(1,128)S(1)}, f32[2,1,4096]{2,1,0:T(1,128)S(1)}, u32[]{:S(2)}, u32[]{:S(2)}) collective-permute-start(f32[2,1,4096]{2,1,0:T(1,128)S(1)} %get-tuple-element.917), channel_id=1, source_target_pairs={{1,0},{2,1},{3,2},{4,3},{5,4},{6,5},{7,6},{9,8},{10,9},{11,10},{12... | collective-permute-start | bytes 98312 | tf_op jit(solution)/shard_map/while/body/eval_jaxpr/ppermute | solution.py:25
  108.9 7.3 %collective-permute-start.6 = (f32[2,1,4096]{2,1,0:T(1,128)S(1)}, f32[2,1,4096]{2,1,0:T(1,128)S(1)}, u32[]{:S(2)}, u32[]{:S(2)}) collective-permute-start(f32[2,1,4096]{2,1,0:T(1,128)S(1)} %get-tuple-element.924), channel_id=1, source_target_pairs={{0,1},{1,2},{2,3},{3,4},{4,5},{5,6},{6,7},{8,9},{9,10},{10,11},{11... | collective-permute-start | bytes 98312 | tf_op jit(solution)/shard_map/while/body/eval_jaxpr/ppermute | solution.py:24
  114.7 3.2 %collective-permute-start.7 = (f32[2,1,4096]{2,1,0:T(1,128)S(1)}, f32[2,1,4096]{2,1,0:T(1,128)S(1)}, u32[]{:S(2)}, u32[]{:S(2)}) collective-permute-start(f32[2,1,4096]{2,1,0:T(1,128)S(1)} %get-tuple-element.925), channel_id=1, source_target_pairs={{1,0},{2,1},{3,2},{4,3},{5,4},{6,5},{7,6},{9,8},{10,9},{11,10},{12... | collective-permute-start | bytes 98312 | tf_op jit(solution)/shard_map/while/body/eval_jaxpr/ppermute | solution.py:25
  118.7 14.6 %collective-permute-start.8 = (f32[2,16,4096]{2,1,0:T(8,128)S(1)}, f32[2,16,4096]{2,1,0:T(8,128)S(1)}, u32[]{:S(2)}, u32[]{:S(2)}) collective-permute-start(f32[2,16,4096]{2,1,0:T(8,128)S(1)} %get-tuple-element.929), channel_id=1, source_target_pairs={{8,0},{16,8},{24,16},{9,1},{17,9},{25,17},{10,2},{18,10},{26,18},{... | collective-permute-start | bytes 1572872 | tf_op jit(solution)/shard_map/while/body/eval_jaxpr/ppermute | solution.py:14
  120.5 12.8 %copy-start.2 = (f32[2,16,4096]{2,1,0:T(8,128)S(1)}, f32[2,16,4096]{2,1,0:T(8,128)}, u32[]{:S(2)}) copy-start(f32[2,16,4096]{2,1,0:T(8,128)} %get-tuple-element.1043) | copy-start | bytes 1572868 | tf_op jit(solution)/shard_map/while
  120.5 12.8 %copy-start.18 = (s32[2,512]{1,0:T(2,128)S(1)}, s32[2,512]{1,0:T(2,128)}, u32[]{:S(2)}) copy-start(s32[2,512]{1,0:T(2,128)} %copy-done.17) | copy-start | bytes 12292 | tf_op jit(solution)/shard_map/while
  121.1 12.1 %copy-start.6 = (f32[16,4096]{1,0:T(8,128)}, f32[16,4096]{1,0:T(8,128)S(1)}, u32[]{:S(2)}) copy-start(f32[16,4096]{1,0:T(8,128)S(1)} %select_add_fusion.2) | copy-start | bytes 786436 | tf_op jit(solution)/shard_map/while
  133.4 10.1 %collective-permute-start = (f32[2,1,4096]{2,1,0:T(1,128)S(1)}, f32[2,1,4096]{2,1,0:T(1,128)}, u32[]{:S(2)}, u32[]{:S(2)}) collective-permute-start(f32[2,1,4096]{2,1,0:T(1,128)S(1)} %get-tuple-element.903), channel_id=1, source_target_pairs={{0,1},{1,2},{2,3},{3,4},{4,5},{5,6},{6,7},{8,9},{9,10},{10,11},{11... | collective-permute-start | bytes 98312 | tf_op jit(solution)/shard_map/while/body/eval_jaxpr/ppermute | solution.py:24
  137.9 5.6 %collective-permute-start.1 = (f32[2,1,4096]{2,1,0:T(1,128)S(1)}, f32[2,1,4096]{2,1,0:T(1,128)}, u32[]{:S(2)}, u32[]{:S(2)}) collective-permute-start(f32[2,1,4096]{2,1,0:T(1,128)S(1)} %get-tuple-element.904), channel_id=1, source_target_pairs={{1,0},{2,1},{3,2},{4,3},{5,4},{6,5},{7,6},{9,8},{10,9},{11,10},{12... | collective-permute-start | bytes 98312 | tf_op jit(solution)/shard_map/while/body/eval_jaxpr/ppermute | solution.py:25
  148.0 4.8 %collective-permute-start.2 = (f32[2,1,4096]{2,1,0:T(1,128)S(1)}, f32[2,1,4096]{2,1,0:T(1,128)S(1)}, u32[]{:S(2)}, u32[]{:S(2)}) collective-permute-start(f32[2,1,4096]{2,1,0:T(1,128)S(1)} %get-tuple-element.911), channel_id=1, source_target_pairs={{0,1},{1,2},{2,3},{3,4},{4,5},{5,6},{6,7},{8,9},{9,10},{10,11},{11... | collective-permute-start | bytes 98312 | tf_op jit(solution)/shard_map/while/body/eval_jaxpr/ppermute | solution.py:24
  151.4 4.3 %collective-permute-start.3 = (f32[2,1,4096]{2,1,0:T(1,128)S(1)}, f32[2,1,4096]{2,1,0:T(1,128)S(1)}, u32[]{:S(2)}, u32[]{:S(2)}) collective-permute-start(f32[2,1,4096]{2,1,0:T(1,128)S(1)} %get-tuple-element.912), channel_id=1, source_target_pairs={{1,0},{2,1},{3,2},{4,3},{5,4},{6,5},{7,6},{9,8},{10,9},{11,10},{12... | collective-permute-start | bytes 98312 | tf_op jit(solution)/shard_map/while/body/eval_jaxpr/ppermute | solution.py:25
  156.1 6.2 %collective-permute-start.4 = (f32[2,1,4096]{2,1,0:T(1,128)S(1)}, f32[2,1,4096]{2,1,0:T(1,128)S(1)}, u32[]{:S(2)}, u32[]{:S(2)}) collective-permute-start(f32[2,1,4096]{2,1,0:T(1,128)S(1)} %get-tuple-element.916), channel_id=1, source_target_pairs={{0,1},{1,2},{2,3},{3,4},{4,5},{5,6},{6,7},{8,9},{9,10},{10,11},{11... | collective-permute-start | bytes 98312 | tf_op jit(solution)/shard_map/while/body/eval_jaxpr/ppermute | solution.py:24
  160.7 3.2 %collective-permute-start.5 = (f32[2,1,4096]{2,1,0:T(1,128)S(1)}, f32[2,1,4096]{2,1,0:T(1,128)S(1)}, u32[]{:S(2)}, u32[]{:S(2)}) collective-permute-start(f32[2,1,4096]{2,1,0:T(1,128)S(1)} %get-tuple-element.917), channel_id=1, source_target_pairs={{1,0},{2,1},{3,2},{4,3},{5,4},{6,5},{7,6},{9,8},{10,9},{11,10},{12... | collective-permute-start | bytes 98312 | tf_op jit(solution)/shard_map/while/body/eval_jaxpr/ppermute | solution.py:25
  167.3 7.3 %collective-permute-start.6 = (f32[2,1,4096]{2,1,0:T(1,128)S(1)}, f32[2,1,4096]{2,1,0:T(1,128)S(1)}, u32[]{:S(2)}, u32[]{:S(2)}) collective-permute-start(f32[2,1,4096]{2,1,0:T(1,128)S(1)} %get-tuple-element.924), channel_id=1, source_target_pairs={{0,1},{1,2},{2,3},{3,4},{4,5},{5,6},{6,7},{8,9},{9,10},{10,11},{11... | collective-permute-start | bytes 98312 | tf_op jit(solution)/shard_map/while/body/eval_jaxpr/ppermute | solution.py:24
  173.0 3.2 %collective-permute-start.7 = (f32[2,1,4096]{2,1,0:T(1,128)S(1)}, f32[2,1,4096]{2,1,0:T(1,128)S(1)}, u32[]{:S(2)}, u32[]{:S(2)}) collective-permute-start(f32[2,1,4096]{2,1,0:T(1,128)S(1)} %get-tuple-element.925), channel_id=1, source_target_pairs={{1,0},{2,1},{3,2},{4,3},{5,4},{6,5},{7,6},{9,8},{10,9},{11,10},{12... | collective-permute-start | bytes 98312 | tf_op jit(solution)/shard_map/while/body/eval_jaxpr/ppermute | solution.py:25
  177.0 14.6 %collective-permute-start.8 = (f32[2,16,4096]{2,1,0:T(8,128)S(1)}, f32[2,16,4096]{2,1,0:T(8,128)S(1)}, u32[]{:S(2)}, u32[]{:S(2)}) collective-permute-start(f32[2,16,4096]{2,1,0:T(8,128)S(1)} %get-tuple-element.929), channel_id=1, source_target_pairs={{8,0},{16,8},{24,16},{9,1},{17,9},{25,17},{10,2},{18,10},{26,18},{... | collective-permute-start | bytes 1572872 | tf_op jit(solution)/shard_map/while/body/eval_jaxpr/ppermute | solution.py:14
  178.8 12.8 %copy-start.2 = (f32[2,16,4096]{2,1,0:T(8,128)S(1)}, f32[2,16,4096]{2,1,0:T(8,128)}, u32[]{:S(2)}) copy-start(f32[2,16,4096]{2,1,0:T(8,128)} %get-tuple-element.1043) | copy-start | bytes 1572868 | tf_op jit(solution)/shard_map/while
  178.8 12.8 %copy-start.18 = (s32[2,512]{1,0:T(2,128)S(1)}, s32[2,512]{1,0:T(2,128)}, u32[]{:S(2)}) copy-start(s32[2,512]{1,0:T(2,128)} %copy-done.17) | copy-start | bytes 12292 | tf_op jit(solution)/shard_map/while
  191.8 10.1 %collective-permute-start = (f32[2,1,4096]{2,1,0:T(1,128)S(1)}, f32[2,1,4096]{2,1,0:T(1,128)}, u32[]{:S(2)}, u32[]{:S(2)}) collective-permute-start(f32[2,1,4096]{2,1,0:T(1,128)S(1)} %get-tuple-element.903), channel_id=1, source_target_pairs={{0,1},{1,2},{2,3},{3,4},{4,5},{5,6},{6,7},{8,9},{9,10},{10,11},{11... | collective-permute-start | bytes 98312 | tf_op jit(solution)/shard_map/while/body/eval_jaxpr/ppermute | solution.py:24
  196.2 5.6 %collective-permute-start.1 = (f32[2,1,4096]{2,1,0:T(1,128)S(1)}, f32[2,1,4096]{2,1,0:T(1,128)}, u32[]{:S(2)}, u32[]{:S(2)}) collective-permute-start(f32[2,1,4096]{2,1,0:T(1,128)S(1)} %get-tuple-element.904), channel_id=1, source_target_pairs={{1,0},{2,1},{3,2},{4,3},{5,4},{6,5},{7,6},{9,8},{10,9},{11,10},{12... | collective-permute-start | bytes 98312 | tf_op jit(solution)/shard_map/while/body/eval_jaxpr/ppermute | solution.py:25
  206.4 4.8 %collective-permute-start.2 = (f32[2,1,4096]{2,1,0:T(1,128)S(1)}, f32[2,1,4096]{2,1,0:T(1,128)S(1)}, u32[]{:S(2)}, u32[]{:S(2)}) collective-permute-start(f32[2,1,4096]{2,1,0:T(1,128)S(1)} %get-tuple-element.911), channel_id=1, source_target_pairs={{0,1},{1,2},{2,3},{3,4},{4,5},{5,6},{6,7},{8,9},{9,10},{10,11},{11... | collective-permute-start | bytes 98312 | tf_op jit(solution)/shard_map/while/body/eval_jaxpr/ppermute | solution.py:24
  209.7 4.3 %collective-permute-start.3 = (f32[2,1,4096]{2,1,0:T(1,128)S(1)}, f32[2,1,4096]{2,1,0:T(1,128)S(1)}, u32[]{:S(2)}, u32[]{:S(2)}) collective-permute-start(f32[2,1,4096]{2,1,0:T(1,128)S(1)} %get-tuple-element.912), channel_id=1, source_target_pairs={{1,0},{2,1},{3,2},{4,3},{5,4},{6,5},{7,6},{9,8},{10,9},{11,10},{12... | collective-permute-start | bytes 98312 | tf_op jit(solution)/shard_map/while/body/eval_jaxpr/ppermute | solution.py:25
  214.4 6.2 %collective-permute-start.4 = (f32[2,1,4096]{2,1,0:T(1,128)S(1)}, f32[2,1,4096]{2,1,0:T(1,128)S(1)}, u32[]{:S(2)}, u32[]{:S(2)}) collective-permute-start(f32[2,1,4096]{2,1,0:T(1,128)S(1)} %get-tuple-element.916), channel_id=1, source_target_pairs={{0,1},{1,2},{2,3},{3,4},{4,5},{5,6},{6,7},{8,9},{9,10},{10,11},{11... | collective-permute-start | bytes 98312 | tf_op jit(solution)/shard_map/while/body/eval_jaxpr/ppermute | solution.py:24
  219.0 3.2 %collective-permute-start.5 = (f32[2,1,4096]{2,1,0:T(1,128)S(1)}, f32[2,1,4096]{2,1,0:T(1,128)S(1)}, u32[]{:S(2)}, u32[]{:S(2)}) collective-permute-start(f32[2,1,4096]{2,1,0:T(1,128)S(1)} %get-tuple-element.917), channel_id=1, source_target_pairs={{1,0},{2,1},{3,2},{4,3},{5,4},{6,5},{7,6},{9,8},{10,9},{11,10},{12... | collective-permute-start | bytes 98312 | tf_op jit(solution)/shard_map/while/body/eval_jaxpr/ppermute | solution.py:25
  225.6 7.3 %collective-permute-start.6 = (f32[2,1,4096]{2,1,0:T(1,128)S(1)}, f32[2,1,4096]{2,1,0:T(1,128)S(1)}, u32[]{:S(2)}, u32[]{:S(2)}) collective-permute-start(f32[2,1,4096]{2,1,0:T(1,128)S(1)} %get-tuple-element.924), channel_id=1, source_target_pairs={{0,1},{1,2},{2,3},{3,4},{4,5},{5,6},{6,7},{8,9},{9,10},{10,11},{11... | collective-permute-start | bytes 98312 | tf_op jit(solution)/shard_map/while/body/eval_jaxpr/ppermute | solution.py:24
  231.3 3.2 %collective-permute-start.7 = (f32[2,1,4096]{2,1,0:T(1,128)S(1)}, f32[2,1,4096]{2,1,0:T(1,128)S(1)}, u32[]{:S(2)}, u32[]{:S(2)}) collective-permute-start(f32[2,1,4096]{2,1,0:T(1,128)S(1)} %get-tuple-element.925), channel_id=1, source_target_pairs={{1,0},{2,1},{3,2},{4,3},{5,4},{6,5},{7,6},{9,8},{10,9},{11,10},{12... | collective-permute-start | bytes 98312 | tf_op jit(solution)/shard_map/while/body/eval_jaxpr/ppermute | solution.py:25
  235.3 14.6 %collective-permute-start.8 = (f32[2,16,4096]{2,1,0:T(8,128)S(1)}, f32[2,16,4096]{2,1,0:T(8,128)S(1)}, u32[]{:S(2)}, u32[]{:S(2)}) collective-permute-start(f32[2,16,4096]{2,1,0:T(8,128)S(1)} %get-tuple-element.929), channel_id=1, source_target_pairs={{8,0},{16,8},{24,16},{9,1},{17,9},{25,17},{10,2},{18,10},{26,18},{... | collective-permute-start | bytes 1572872 | tf_op jit(solution)/shard_map/while/body/eval_jaxpr/ppermute | solution.py:14
  237.1 12.8 %copy-start.2 = (f32[2,16,4096]{2,1,0:T(8,128)S(1)}, f32[2,16,4096]{2,1,0:T(8,128)}, u32[]{:S(2)}) copy-start(f32[2,16,4096]{2,1,0:T(8,128)} %get-tuple-element.1043) | copy-start | bytes 1572868 | tf_op jit(solution)/shard_map/while
  237.1 12.8 %copy-start.18 = (s32[2,512]{1,0:T(2,128)S(1)}, s32[2,512]{1,0:T(2,128)}, u32[]{:S(2)}) copy-start(s32[2,512]{1,0:T(2,128)} %copy-done.17) | copy-start | bytes 12292 | tf_op jit(solution)/shard_map/while
  249.9 42.8 %copy-start = (f32[2,16,4096]{2,1,0:T(8,128)}, f32[2,16,4096]{2,1,0:T(8,128)S(1)}, u32[]{:S(2)}) copy-start(f32[2,16,4096]{2,1,0:T(8,128)S(1)} %get-tuple-element.1019) | copy-start | bytes 1572868
  (62 other events, 236.2 us)
Sparse Core Ops, SparseCore 0:
  250.1 21.9 reduce-scatter.1
where the time goes:
time: 301 us; the launch traced here: 300 us
  starting transfers between devices  103 us (34%)
  waiting for transfers between devices  72 us (24%)
  blocking collectives  42.7 us (14%)
  matrix products  30.7 us (10%)
  local copies, waits for them, and re-layouts  23 us (8%)
  between operations  14.1 us (5%)
  other arithmetic  12.8 us (4%)
    ppermute x16, starting transfers between devices, with_halo(): before = lax.ppermute(last, axis, up)  73 us
    ppermute x5, waiting for transfers between devices, shifted(): lax.ppermute(value, axis, [(source, source + steps) for source in range(l...  48.3 us
    psum x1, blocking collectives, shards(): storage = lax.psum(storage_part, ('tm', 'tile'))  42.7 us
    dot_general x8, matrix products, forcing(): jnp.einsum('gro,oc->grc', weighted_rows, col_hit, precision=lax.Precision...  30.7 us
    ppermute x16, waiting for transfers between devices, with_halo(): after = lax.ppermute(leading, axis, down)  23.7 us
    ppermute x16, starting transfers between devices, with_halo(): after = lax.ppermute(leading, axis, down)  22.2 us
    ppermute x5, starting transfers between devices, shifted(): lax.ppermute(value, axis, [(source, source + steps) for source in range(l...  7.53 us
  transfers between devices with their start and end apart: 38, of which 16 were waited for; matrix products, arithmetic and copies ran while one was open for 8% of the time, Pallas kernels for 0%

commit v1 on v0

v1 whole, which is shorter than its diff:
```python
import functools

import jax
import jax.numpy as jnp
from jax import lax
from jax.experimental import pallas as pl
from jax.experimental.pallas import tpu as pltpu
from jax.sharding import PartitionSpec as P

BLOCK = 128
STEPS = 2
SWEEPS = 2
LANES = 128
WIDE = 256
F32 = jnp.float32
BF16 = jnp.bfloat16
VMEM_LIMIT = 40 * 2**20


def peer(index, hop, count):
    if count & (count - 1) == 0:
        return index ^ hop
    return (index + hop) % count


def fetch(value, axis, hop):
    count = lax.axis_size(axis)
    return lax.ppermute(value, axis, [(peer(i, hop, count), i) for i in range(count)])


def gather(value, axis):
    count = lax.axis_size(axis)
    blocks, hop = (value[None], 1)
    while hop < count:
        blocks = jnp.concatenate([blocks, fetch(blocks[: count - hop], axis, hop)], axis=0)
        hop *= 2
    return blocks


def total(value, axes):
    for axis in axes:
        count = lax.axis_size(axis)
        if count & (count - 1):
            value = lax.psum(value, axis)
            continue
        hop = 1
        while hop < count:
            value = value + fetch(value, axis, hop)
            hop *= 2
    return value


def inner_pairs(value):
    count = lax.axis_size("tile")
    pairs = [(i, i ^ 1) for i in range(count) if i ^ 1 < count]
    return lax.ppermute(value, "tile", pairs)


def outer_pairs(value):
    count = lax.axis_size("tile")
    low = range(1, count - 1, 2)
    return lax.ppermute(value, "tile", [(i, i + 1) for i in low] + [(i + 1, i) for i in low])


class Plan:
    def __init__(self, rows, width, sections, members, observed):
        self.rows, self.width, self.sections = (rows, width, sections)
        self.members, self.observed = (members, observed)
        self.own = width // sections
        sweeps = sections * STEPS * SWEEPS
        halo = -(-sweeps // LANES) * LANES
        wide = -(-(self.own + 2 * halo) // WIDE) * WIDE
        self.window = min(width, wide)
        self.halo = halo
        self.ext = 3 * rows
        self.per_phase = max(1, rows // (STEPS * SWEEPS))
        self.head_window = min(width, self.own + LANES)

    def start(self, index):
        first = index * self.own - self.halo
        return pl.multiple_of(jnp.clip(first, 0, self.width - self.window), LANES)

    def head_start(self, index):
        return pl.multiple_of(jnp.minimum(index * self.own, self.width - self.head_window), LANES)


def pack_kernel(plan, heads, capacity, cond_row, cond_col, terminal, packed, *rest):
    head_outs, sems = (rest[:-1], rest[-1])
    me = lax.axis_index("tm")
    columns = pl.ds(plan.start(me), plan.window)
    copies = [
        (capacity.at[:, columns], packed.at[0]),
        (cond_row.at[:, columns], packed.at[1]),
        (cond_col.at[:, columns], packed.at[2]),
        (terminal.at[:, :, columns], packed.at[pl.ds(3, plan.members)]),
    ]
    for hop, out in enumerate(head_outs, 1):
        target = peer(me, hop, plan.sections)
        if plan.sections & (plan.sections - 1):
            target = (me - hop + plan.sections) % plan.sections
        copies.append((heads.at[0, :, :, pl.ds(plan.head_start(target), plan.head_window)], out))
    started = [pltpu.make_async_copy(a, b, sems.at[i]) for i, (a, b) in enumerate(copies)]
    for copy in started:
        copy.start()
    for copy in started:
        copy.wait()


def chain_kernel(plan, top, count, mask, packed, inner, outer, *rest):
    first = top == plan.sections - 1
    if first:
        obs, rest = (rest[0], rest[1:])
        field = None
    else:
        field, field_inner, field_outer, obs = rest[:4]
        rest = rest[4:]
    history_out = rest[0]
    last = top - count + 1 == 0
    single = first and last
    send_outs = rest[1 : 1 + plan.sections] if single else ()
    rest = rest[1 + len(send_outs) :]
    grid, east, west, south, north, act_rd, cap_rd, x0, x1, force, history, sems = rest
    me = lax.axis_index("tm")
    tile = lax.axis_index("tile")
    rows, ext, members = (plan.rows, plan.ext, plan.members)
    tiles = plan.window // LANES
    start = plan.start(me)
    inner_at = pl.multiple_of(jnp.where(tile % 2 == 0, 2 * rows, 0), rows)
    outer_at = pl.multiple_of(2 * rows - inner_at, rows)
    places = [(packed, rows), (inner, inner_at), (outer, outer_at)]
    copies = [(ref, grid.at[:, pl.ds(at, rows), :]) for ref, at in places]
    if not first:
        places = [(field, rows), (field_inner, inner_at), (field_outer, outer_at)]
        copies += [(ref, x0.at[:, pl.ds(at, rows), :]) for ref, at in places]
    started = [pltpu.make_async_copy(a, b, sems.at[i]) for i, (a, b) in enumerate(copies)]
    for copy in started:
        copy.start()
    for copy in started:
        copy.wait()

    lane = lax.broadcasted_iota(jnp.int32, (1, LANES), 1)
    ends = lane == LANES - 1
    begins = lane == 0
    tile_rows = lax.axis_size("tile") * rows

    def chunk_active(chunk, column):
        if column >= tiles:
            return jnp.float32(0.0)
        row = (tile + chunk - 1) * rows
        inside = (row >= 0) & (row < tile_rows)
        block = jnp.clip(row, 0, tile_rows - 1) // BLOCK
        value = mask[block, (start + column * LANES) // BLOCK]
        return jnp.where(inside, value, 0).astype(F32)

    def active(column):
        parts = [jnp.full((rows, LANES), chunk_active(chunk, column), F32) for chunk in range(3)]
        return jnp.concatenate(parts, axis=0)

    def cols(column):
        return pl.ds(column * LANES, LANES)

    row_id = lax.broadcasted_iota(jnp.int32, (ext, LANES), 0)
    act = active(0)
    previous = jnp.zeros((ext, LANES), F32)
    for c in range(tiles):
        act_next = active(c + 1)
        pair = act * jnp.where(ends, act_next, act)
        e = grid[1, :, cols(c)] * pair
        w = pltpu.roll(jnp.where(ends, previous, e), 1, axis=1)
        below = jnp.where(row_id == ext - 1, 0.0, pltpu.roll(act, ext - 1, axis=0))
        s = grid[2, :, cols(c)] * act * below
        n = jnp.where(row_id == 0, 0.0, pltpu.roll(s, 1, axis=0))
        cap = grid[0, :, cols(c)]
        diagonal = cap + e + w + s + n
        inverse = jnp.where(diagonal > 0.0, 1.0 / jnp.where(diagonal > 0.0, diagonal, 1.0), 0.0)
        east[:, cols(c)] = e * inverse
        west[:, cols(c)] = w * inverse
        south[:, cols(c)] = s * inverse
        north[:, cols(c)] = n * inverse
        act_rd[:, cols(c)] = act * inverse
        cap_rd[:, cols(c)] = act * cap * inverse
        if first:
            x0[:, :, cols(c)] = grid[pl.ds(3, members), :, cols(c)]
        previous = e
        act = act_next

    wides = plan.window // WIDE

    def observe(section, step, low, height):
        block = peer(section, me, plan.sections)
        if plan.sections & (plan.sections - 1):
            block = (section - me + plan.sections) % plan.sections
        lines = obs[block]
        row = lines[4 * step : 4 * step + 1] - ((tile - 1) * rows + low).astype(F32)
        col = lines[4 * step + 1 : 4 * step + 2] - start.astype(F32)
        inside = (row >= 0.0) & (row < height) & (col >= 0.0) & (col < plan.window)
        group = jnp.floor(col * (1.0 / WIDE))
        key = jnp.where(inside, group * height + row, -1.0).astype(jnp.int32)
        within = (col - group * WIDE).astype(jnp.int32)
        ids = lax.broadcasted_iota(jnp.int32, (wides * height, plan.observed), 0)
        hit = ids == key
        left = []
        for m in range(members):
            weight = lines[4 * step + 2 + m : 4 * step + 3 + m]
            parts = []
            for _ in range(3):
                piece = weight.astype(BF16).astype(F32)
                parts.append(jnp.where(hit, piece, 0.0).astype(BF16))
                weight = weight - piece
            left.append(jnp.concatenate(parts, axis=1))
        place = lax.broadcasted_iota(jnp.int32, (WIDE, plan.observed), 0)
        right = jnp.where(place == within, 1.0, 0.0).astype(BF16)
        right = jnp.concatenate([right] * 3, axis=1)
        found = lax.dot_general(
            jnp.concatenate(left, axis=0),
            right,
            (((1,), (1,)), ((), ())),
            preferred_element_type=F32,
        )
        for m in range(members):
            for g in range(wides):
                at = (m * wides + g) * height
                force[m, low : low + height, g * WIDE : (g + 1) * WIDE] = found[at : at + height]

    def sweep(source, target, low, height, initial):
        band = slice(low, low + height)
        for m in range(members):
            here = source[m, band, cols(0)]
            turned = pltpu.roll(here, LANES - 1, axis=1)
            left = jnp.zeros((height, LANES), F32)
            for c in range(tiles):
                if c + 1 < tiles:
                    after = source[m, band, cols(c + 1)]
                    after_turned = pltpu.roll(after, LANES - 1, axis=1)
                else:
                    after = after_turned = jnp.zeros((height, LANES), F32)
                back = pltpu.roll(here, 1, axis=1)
                x_east = jnp.where(ends, after_turned, turned)
                x_west = jnp.where(begins, left, back)
                x_south = pltpu.roll(here, height - 1, axis=0)
                x_north = pltpu.roll(here, 1, axis=0)
                if initial:
                    rhs = cap_rd[band, cols(c)] * here + act_rd[band, cols(c)] * force[m, band, cols(c)]
                    force[m, band, cols(c)] = rhs
                else:
                    rhs = force[m, band, cols(c)]
                target[m, band, cols(c)] = (
                    rhs
                    + east[band, cols(c)] * x_east
                    + west[band, cols(c)] * x_west
                    + south[band, cols(c)] * x_south
                    + north[band, cols(c)] * x_north
                )
                left, here, turned = (back, after, after_turned)

    def one_section(low, height, number):
        section = top - number
        for step in reversed(range(STEPS)):
            observe(section, step, low, height)
            refs = (x0, x1)
            for index in range(SWEEPS):
                sweep(refs[index % 2], refs[(index + 1) % 2], low, height, index == 0)
            if SWEEPS % 2:
                x0[:, low : low + height, :] = x1[:, low : low + height, :]
            history[section - (top - count + 1), step] = x0[:, rows : 2 * rows, :]

    done = 0
    while done < count:
        low = done * STEPS * SWEEPS // 8 * 8
        until = done + 1
        while until < count and until * STEPS * SWEEPS // 8 * 8 == low:
            until += 1
        lax.fori_loop(done, until, lambda i, _, low=low: one_section(low, ext - 2 * low, i), None)
        done = until

    copies = [(history, history_out)]
    own = pl.ds(pl.multiple_of(me * plan.own - start, LANES), plan.own)
    for hop, out in enumerate(send_outs):
        copies.append((history.at[target_of(plan, me, hop), 0, :, :, own], out))
    started = [pltpu.make_async_copy(a, b, sems.at[i]) for i, (a, b) in enumerate(copies)]
    for copy in started:
        copy.start()
    for copy in started:
        copy.wait()


def target_of(plan, me, hop):
    if plan.sections & (plan.sections - 1):
        return (me - hop + plan.sections) % plan.sections
    return peer(me, hop, plan.sections)


def split_kernel(plan, history, *rest):
    outs, sems = (rest[:-1], rest[-1])
    me = lax.axis_index("tm")
    own = pl.ds(pl.multiple_of(me * plan.own - plan.start(me), LANES), plan.own)
    started = [
        pltpu.make_async_copy(history.at[target_of(plan, me, hop), 0, :, :, own], out, sems.at[hop])
        for hop, out in enumerate(outs)
    ]
    for copy in started:
        copy.start()
    for copy in started:
        copy.wait()


def join_kernel(plan, *rest):
    blocks, out, sems = (rest[:-2], rest[-2], rest[-1])
    me = lax.axis_index("tm")
    started = []
    for hop, block in enumerate(blocks):
        at = pl.multiple_of(peer(me, hop, plan.sections) * plan.own, LANES)
        started.append(pltpu.make_async_copy(block, out.at[:, :, pl.ds(at, plan.own)], sems.at[hop]))
    for copy in started:
        copy.start()
    for copy in started:
        copy.wait()


def sens_kernel(plan, mask, packed, history_in, heads, *rest):
    received, rest = (rest[: plan.sections - 1], rest[plan.sections - 1 :])
    cond_out, storage_out, cap, adj, head, sems = rest
    me = lax.axis_index("tm")
    tile = lax.axis_index("tile")
    rows, members = (plan.rows, plan.members)
    start, head_start = (plan.start(me), plan.head_start(me))
    copies = [(packed.at[0], cap), (history_in, adj)]
    copies.append((heads.at[0, :, :, pl.ds(head_start, plan.head_window)], head.at[0]))
    for hop, ref in enumerate(received, 1):
        copies.append((ref, head.at[hop]))
    started = [pltpu.make_async_copy(a, b, sems.at[i]) for i, (a, b) in enumerate(copies)]
    for copy in started:
        copy.start()
    for copy in started:
        copy.wait()

    ends = lax.broadcasted_iota(jnp.int32, (1, LANES), 1) == LANES - 1
    tiles = plan.own // LANES

    def after(here, following):
        return jnp.where(ends, pltpu.roll(following, LANES - 1, axis=1), pltpu.roll(here, LANES - 1, axis=1))

    own = me * plan.own - start
    head_own = me * plan.own - head_start
    block_row = tile * rows // BLOCK
    columns = plan.width // LANES
    stored = [jnp.zeros((rows, LANES), F32) for _ in range(members)]
    for t in range(tiles):
        here = pl.ds(pl.multiple_of(own + t * LANES, LANES), LANES)
        there = pl.ds(pl.multiple_of(jnp.minimum(own + (t + 1) * LANES, plan.window - LANES), LANES), LANES)
        head_here = pl.ds(pl.multiple_of(head_own + t * LANES, LANES), LANES)
        head_next = jnp.minimum(head_own + (t + 1) * LANES, plan.head_window - LANES)
        head_there = pl.ds(pl.multiple_of(head_next, LANES), LANES)
        column = me * tiles + t
        act = mask[block_row, column].astype(F32)
        act_next = mask[block_row, jnp.minimum(column + 1, columns - 1)].astype(F32)
        act_next = jnp.where(column + 1 < columns, act_next, 0.0)
        pair = act * jnp.where(ends, act_next, act)
        capacity = cap[:, here]
        sens = jnp.zeros((rows, LANES), F32)
        for hop in range(plan.sections):
            section = peer(me, hop, plan.sections)
            levels = [head[hop, k, :, head_here] for k in range(STEPS + 1)]
            for step in range(STEPS):
                fields = [adj[section, step, m, :, here] for m in range(members)]
                rise = capacity * (levels[step + 1] - levels[step])
                for m in range(members):
                    stored[m] = stored[m] + fields[m] * rise
                both = functools.reduce(jnp.add, fields)
                both_next = functools.reduce(jnp.add, [adj[section, step, m, :, there] for m in range(members)])
                slope = after(levels[step + 1], head[hop, step + 1, :, head_there]) - levels[step + 1]
                sens = sens + (after(both, both_next) - both) * slope
        cond_out[:, t * LANES : (t + 1) * LANES] = sens * pair
    storage_out[...] = jnp.zeros((8, LANES), F32)
    for m in range(members):
        storage_out[m : m + 1, :] = jnp.full((1, LANES), jnp.sum(stored[m]), F32)


def shards(heads, capacity, cond_row, cond_col, terminal, obs_cell, obs_weight, block_mask):
    rows, width = capacity.shape
    members = terminal.shape[0]
    sections = lax.axis_size("tm")
    plan = Plan(rows, width, sections, members, obs_cell.shape[2])
    anywhere = pl.BlockSpec(memory_space=pl.ANY)
    in_vmem = pl.BlockSpec(memory_space=pltpu.VMEM)
    in_smem = pl.BlockSpec(memory_space=pltpu.SMEM)
    params = pltpu.CompilerParams(vmem_limit_bytes=VMEM_LIMIT)

    def shape(*dims):
        return jax.ShapeDtypeStruct(dims, F32)

    window = plan.window
    ext = plan.ext
    packed, *head_sends = pl.pallas_call(
        functools.partial(pack_kernel, plan),
        out_shape=[shape(3 + members, rows, window)]
        + [shape(STEPS + 1, rows, plan.head_window)] * (sections - 1),
        in_specs=[anywhere] * 5,
        out_specs=[in_vmem] * sections,
        scratch_shapes=[pltpu.SemaphoreType.DMA((3 + sections,))],
        name="pack",
    )(heads, capacity, cond_row, cond_col, terminal)
    outer = outer_pairs(packed)
    inner = inner_pairs(packed)

    cells = obs_cell[0]
    lines = []
    for step in range(STEPS):
        lines += [(cells[step] // width).astype(F32), (cells[step] % width).astype(F32)]
        lines += [obs_weight[0, step, m] for m in range(members)]
    obs = gather(jnp.stack(lines), "tm")
    received = [fetch(part, "tm", hop) for hop, part in enumerate(head_sends, 1)]

    block = (members, rows, plan.own)
    histories = []
    top = sections - 1
    field = []
    sends = None
    while top >= 0:
        count = min(plan.per_phase, top + 1)
        single = count == sections
        outs = [shape(count, STEPS, members, rows, window)]
        outs += [shape(*block)] * (sections if single else 0)
        plane = pltpu.VMEM((ext, window), F32)
        fields = pltpu.VMEM((members, ext, window), F32)
        results = pl.pallas_call(
            functools.partial(chain_kernel, plan, top, count),
            out_shape=outs,
            in_specs=[in_smem] + [anywhere] * (3 + len(field)) + [in_vmem],
            out_specs=[anywhere] * len(outs),
            scratch_shapes=[
                pltpu.VMEM((3 + members, ext, window), F32),
                *([plane] * 6),
                *([fields] * 3),
                pltpu.VMEM((count, STEPS, members, rows, window), F32),
                pltpu.SemaphoreType.DMA((max(6, 1 + sections),)),
            ],
            compiler_params=params,
            name="chain",
        )(block_mask, packed, inner, outer, *field, obs)
        histories.insert(0, results[0])
        if single:
            sends = results[1:]
        top -= count
        if top >= 0:
            reached = results[0][0, 0]
            field = [reached, inner_pairs(reached), outer_pairs(reached)]
    history = histories[0] if len(histories) == 1 else jnp.concatenate(histories, axis=0)
    if sends is None:
        sends = pl.pallas_call(
            functools.partial(split_kernel, plan),
            out_shape=[shape(*block)] * sections,
            in_specs=[anywhere],
            out_specs=[in_vmem] * sections,
            scratch_shapes=[pltpu.SemaphoreType.DMA((sections,))],
            name="split",
        )(history)

    cond, storage = pl.pallas_call(
        functools.partial(sens_kernel, plan),
        out_shape=[shape(rows, plan.own), shape(8, LANES)],
        in_specs=[in_smem] + [anywhere] * (2 + sections),
        out_specs=[in_vmem, in_vmem],
        scratch_shapes=[
            pltpu.VMEM((rows, window), F32),
            pltpu.VMEM((sections, STEPS, members, rows, window), F32),
            pltpu.VMEM((sections, STEPS + 1, rows, plan.head_window), F32),
            pltpu.SemaphoreType.DMA((2 + sections,)),
        ],
        compiler_params=params,
        name="sens",
    )(block_mask, packed, history, heads, *received)

    blocks = [sends[0]] + [fetch(part, "tm", hop) for hop, part in enumerate(sends[1:], 1)]
    adjoint = pl.pallas_call(
        functools.partial(join_kernel, plan),
        out_shape=shape(members, rows, width),
        in_specs=[anywhere] * sections,
        out_specs=in_vmem,
        scratch_shapes=[pltpu.SemaphoreType.DMA((sections,))],
        name="join",
    )(*blocks)
    storage = total(storage, ("tile", "tm"))
    return (adjoint[None], cond, storage[:members, 0])


def solution(mesh):
    placed = (
        P("tm", None, "tile", None),
        P("tile", None),
        P("tile", None),
        P("tile", None),
        P(None, "tile", None),
        P("tm", None, None),
        P("tm", None, None, None),
        P(),
    )
    return jax.shard_map(
        shards,
        mesh=mesh,
        in_specs=placed,
        out_specs=(P("tm", None, "tile", None), P("tile", "tm"), P()),
        check_vma=False,
    )
```

time: 301 us -> 62.4 us (0.21)
  starting transfers between devices: 103 us -> 27.1 us
  waiting for transfers between devices: 72 us -> 15.1 us
  blocking collectives: 42.7 us -> 0 us
  matrix products: 30.7 us -> 0 us
  local copies, waits for them, and re-layouts: 23 us -> 3.05 us
  Pallas kernels: 0 us -> 16 us
  between operations: 14.1 us -> 0.81 us
  other arithmetic: 12.8 us -> 0.07 us
    ppermute x37 -> x15, starting transfers between devices: 103 us -> 27.1 us  [the longest x13 22 us: fetch(): lax.ppermute(value, axis, [(peer(i, hop, count), i) for i in range(count)])]
    ppermute x37 -> x15, waiting for transfers between devices: 72 us -> 15.1 us  [the longest x13 15.1 us: fetch(): lax.ppermute(value, axis, [(peer(i, hop, count), i) for i in range(count)])]
    psum x1 -> x0, blocking collectives: 42.7 us -> none  [shards(): storage = lax.psum(storage_part, ('tm', 'tile'))]
    dot_general x8 -> x0, matrix products: 30.7 us -> none  [forcing(): jnp.einsum('gro,oc->grc', weighted_rows, col_hit, precision=lax.Precision...]
    pallas_call x0 -> x4, Pallas kernels: none -> 16 us  [the longest x1 8.68 us: shards(): pl.pallas_call(functools.partial(chain_kernel, plan, top, count), out_sha...]
    slice x39 -> x1, local copies, waits for them, and re-layouts: 8.69 us -> 0.63 us  [shards(): return (adjoint[None], cond, storage[:members, 0])]
    while x132 -> x0, local copies, waits for them, and re-layouts: 5.74 us -> none
    reduce_sum x8 -> x0, other arithmetic: 4.29 us -> none  [the longest x4 2.49 us: one_round(): jnp.sum(field * capacity * (later - earlier), axis=(1, 2))]
  transfers between devices with their start and end apart: 38 -> 15, of which waited for: 16 -> 7; matrix products, arithmetic and copies ran while one was open for 8% -> 1% of each run, Pallas kernels for 0% -> 14%
where the time goes in v1:
time: 62.4 us; the launch traced here: 62.2 us
  starting transfers between devices  27.1 us (43%)
  Pallas kernels  16 us (26%)
  waiting for transfers between devices  15.1 us (24%)
  local copies, waits for them, and re-layouts  3.05 us (5%)
  between operations  0.81 us (1%)
    ppermute x13, starting transfers between devices, fetch(): lax.ppermute(value, axis, [(peer(i, hop, count), i) for i in range(count)])  22 us
    ppermute x13, waiting for transfers between devices, fetch(): lax.ppermute(value, axis, [(peer(i, hop, count), i) for i in range(count)])  15.1 us
    pallas_call x1, Pallas kernels, shards(): pl.pallas_call(functools.partial(chain_kernel, plan, top, count), out_sha...  8.68 us
    ppermute x1, starting transfers between devices, inner_pairs(): return lax.ppermute(value, 'tile', pairs)  4.34 us
    pallas_call x1, Pallas kernels, shards(): pl.pallas_call(functools.partial(sens_kernel, plan), out_shape=[shape(row...  3.04 us
    unnamed x18, local copies, waits for them, and re-layouts  2.38 us
    pallas_call x1, Pallas kernels, shards(): pl.pallas_call(functools.partial(pack_kernel, plan), out_shape=[shape(3 +...  2.37 us
    pallas_call x1, Pallas kernels, shards(): pl.pallas_call(functools.partial(join_kernel, plan), out_shape=shape(memb...  1.92 us
  transfers between devices with their start and end apart: 15, of which 7 were waited for; matrix products, arithmetic and copies ran while one was open for 1% of the time, Pallas kernels for 14%

profile of v1, /device:TPU:0, one launch (start us, length us, event | category | flops | bytes accessed | tf_op | source)
XLA Modules:
  0.0 62.2 jit_solution(4871286815374323151)
XLA Ops:
  0.6 0.0 copy-start.8
  0.6 0.0 copy-start.7
  0.7 0.0 copy-start.3
  0.7 2.4 %pack.1 = (f32[5,16,1280]{2,1,0:T(8,128)}, f32[3,16,1152]{2,1,0:T(8,128)}, f32[3,16,1152]{2,1,0:T(8,128)}, f32[3,16,1152]{2,1,0:T(8,128)}) custom-call(f32[1,3,16,4096]{3,2,1,0:T(8,128)} %heads.3, f32[16,4096]{1,0:T(8,128)} %capacity.1, f32[16,4096]{1,0:T(8,128)} %cond_row.1, f32[16,4096]{1,0:T(8,128)} %cond_col.1, f32[2,16,4096]{2,1,0:T(8,128)} %terminal.1), custom_call_target="tpu_custom_call" | custom-call | tf_op jit(solution)/shard_map/pack/pallas_call | solution.py:394
  3.0 0.0 copy-start
  3.1 0.8 %collective-permute-start.1 = (f32[5,16,1280]{2,1,0:T(8,128)}, f32[5,16,1280]{2,1,0:T(8,128)S(1)}, u32[]{:S(2)}, u32[]{:S(2)}) collective-permute-start(f32[5,16,1280]{2,1,0:T(8,128)} %get-tuple-element.14.packed), channel_id=1, source_target_pairs={{1,2},{3,4},{5,6},{2,1},{4,3},{6,5},{9,10},{11,12},{13,14},{10,9},... | collective-permute-start | bytes 1228808 | tf_op jit(solution)/shard_map/ppermute | solution.py:62
  3.9 4.3 %collective-permute-start = (f32[5,16,1280]{2,1,0:T(8,128)}, f32[5,16,1280]{2,1,0:T(8,128)S(1)}, u32[]{:S(2)}, u32[]{:S(2)}) collective-permute-start(f32[5,16,1280]{2,1,0:T(8,128)} %get-tuple-element.14.packed), channel_id=1, source_target_pairs={{0,1},{1,0},{2,3},{3,2},{4,5},{5,4},{6,7},{7,6},{8,9},{9,8},{10,11... | collective-permute-start | bytes 1228808 | tf_op jit(solution)/shard_map/ppermute | solution.py:56
  8.2 0.0 copy-done.8
  8.2 0.0 copy-done.7
  8.3 1.6 %collective-permute-start.2 = (f32[1,8,512]{2,1,0:T(8,128)S(1)}, f32[1,8,512]{2,1,0:T(8,128)S(1)}, u32[]{:S(2)}, u32[]{:S(2)}) collective-permute-start(f32[1,8,512]{2,1,0:T(8,128)S(1)} %bitcast.39), channel_id=1, source_target_pairs={{8,0},{0,8},{24,16},{16,24},{9,1},{1,9},{25,17},{17,25},{10,2},{2,... | collective-permute-start | bytes 49160 | tf_op jit(solution)/shard_map/ppermute | solution.py:28
  10.0 2.2 %collective-permute-done.2 = f32[1,8,512]{2,1,0:T(8,128)S(1)} collective-permute-done((f32[1,8,512]{2,1,0:T(8,128)S(1)}, f32[1,8,512]{2,1,0:T(8,128)S(1)}, u32[]{:S(2)}, u32[]{:S(2)}) %collective-permute-start.2) | collective-permute-done | bytes 16416 | tf_op jit(solution)/shard_map/ppermute | solution.py:28
  12.2 2.6 %collective-permute-start.3 = (f32[2,8,512]{2,1,0:T(8,128)S(1)}, f32[2,8,512]{2,1,0:T(8,128)S(1)}, u32[]{:S(2)}, u32[]{:S(2)}) collective-permute-start(f32[2,8,512]{2,1,0:T(8,128)S(1)} %pad_maximum_fusion.1), channel_id=1, source_target_pairs={{16,0},{24,8},{0,16},{8,24},{17,1},{25,9},{1,17},{9,25},{18,2},{26... | collective-permute-start | bytes 98312 | tf_op jit(solution)/shard_map/ppermute | solution.py:28
  14.7 1.6 %collective-permute-start.7 = (f32[3,16,1152]{2,1,0:T(8,128)}, f32[3,16,1152]{2,1,0:T(8,128)S(1)}, u32[]{:S(2)}, u32[]{:S(2)}) collective-permute-start(f32[3,16,1152]{2,1,0:T(8,128)} %get-tuple-element.20), channel_id=1, source_target_pairs={{8,0},{0,8},{24,16},{16,24},{9,1},{1,9},{25,17},{17,25},{10,2},{2,... | collective-permute-start | bytes 663560 | tf_op jit(solution)/shard_map/ppermute | solution.py:28
  16.3 0.3 collective-permute-start.8
  16.7 0.4 collective-permute-done.3
  17.1 4.3 %collective-permute-start.9 = (f32[3,16,1152]{2,1,0:T(8,128)}, f32[3,16,1152]{2,1,0:T(8,128)S(1)}, u32[]{:S(2)}, u32[]{:S(2)}) collective-permute-start(f32[3,16,1152]{2,1,0:T(8,128)} %get-tuple-element.22), channel_id=1, source_target_pairs={{24,0},{16,8},{8,16},{0,24},{25,1},{17,9},{9,17},{1,25},{26,2},{18... | collective-permute-start | bytes 663560 | tf_op jit(solution)/shard_map/ppermute | solution.py:28
  21.4 0.0 collective-permute-done.1.outer
  21.4 0.0 collective-permute-done.inner
  21.4 0.0 copy-done.3
  21.4 0.0 copy-start.1
  21.4 1.0 %copy-done.1 = f32[5,16,1280]{2,1,0:T(8,128)S(1)} copy-done((f32[5,16,1280]{2,1,0:T(8,128)S(1)}, f32[5,16,1280]{2,1,0:T(8,128)}, u32[]{:S(2)}) %copy-start.1) | copy-done | bytes 409624
  22.4 8.7 %chain.1 = (f32[4,2,2,16,1280]{4,3,2,1,0:T(8,128)S(1)}, f32[2,16,1024]{2,1,0:T(8,128)S(1)}, f32[2,16,1024]{2,1,0:T(8,128)S(1)}, f32[2,16,1024]{2,1,0:T(8,128)S(1)}, f32[2,16,1024]{2,1,0:T(8,128)S(1)}) custom-call(s32[1,32]{1,0:T(1,128)S(1)} %copy-done.3, f32[5,16,1280]{2,1,0:T(8,128)S(1)} %copy-done.1, f32[5,16,1280]{2,1,0:T(8,128)S(1)} %collective-permute-done.inner, ...), custom_call_target="tpu_custom_call" | custom-call | tf_op jit(solution)/shard_map/chain/pallas_call | solution.py:426
  31.1 0.6 %copy-done.2 = f32[2,16,1024]{2,1,0:T(8,128)} copy-done((f32[2,16,1024]{2,1,0:T(8,128)}, f32[2,16,1024]{2,1,0:T(8,128)S(1)}, u32[]{:S(2)}) %copy-start.2) | copy-done | bytes 131096
  31.7 0.0 collective-permute-done.7.rest_0_
  31.7 2.5 %collective-permute-done.8.rest_1_ = f32[3,16,1152]{2,1,0:T(8,128)S(1)} collective-permute-done((f32[3,16,1152]{2,1,0:T(8,128)}, f32[3,16,1152]{2,1,0:T(8,128)S(1)}, u32[]{:S(2)}, u32[]{:S(2)}) %collective-permute-start.8) | collective-permute-done | bytes 221216 | tf_op jit(solution)/shard_map/ppermute | solution.py:28
  34.2 0.0 collective-permute-done.9.rest_2_
  34.2 3.0 %sens.1 = (f32[16,1024]{1,0:T(8,128)}, f32[8,128]{1,0:T(8,128)S(1)}) custom-call(s32[1,32]{1,0:T(1,128)S(1)} %copy-done.3, f32[5,16,1280]{2,1,0:T(8,128)S(1)} %copy-done.1, f32[4,2,2,16,1280]{4,3,2,1,0:T(8,128)S(1)} %get-tuple-element.19.history_in, f32[1,3,16,4096]{3,2,1,0:T(8,128)S(1)} %copy-done, f32[3,16,1152]{2,1,0:T(8,128)S(1)} %collective-permute-done.7.rest_0_, ...), custom_call_target="tpu_custom_call" | custom-call | tf_op jit(solution)/shard_map/sens/pallas_call | solution.py:459
  37.3 0.1 collective-permute-start.10
  37.4 3.7 %collective-permute-start.4 = (f32[2,16,1024]{2,1,0:T(8,128)S(1)}, f32[2,16,1024]{2,1,0:T(8,128)S(1)}, u32[]{:S(2)}, u32[]{:S(2)}) collective-permute-start(f32[2,16,1024]{2,1,0:T(8,128)S(1)} %get-tuple-element.16), channel_id=1, source_target_pairs={{8,0},{0,8},{24,16},{16,24},{9,1},{1,9},{25,17},{17,25},{10,2},{2,... | collective-permute-start | bytes 393224 | tf_op jit(solution)/shard_map/ppermute | solution.py:28
  41.1 0.0 collective-permute-start.5
  41.1 2.4 %collective-permute-start.6 = (f32[2,16,1024]{2,1,0:T(8,128)S(1)}, f32[2,16,1024]{2,1,0:T(8,128)S(1)}, u32[]{:S(2)}, u32[]{:S(2)}) collective-permute-start(f32[2,16,1024]{2,1,0:T(8,128)S(1)} %get-tuple-element.18), channel_id=1, source_target_pairs={{24,0},{16,8},{8,16},{0,24},{25,1},{17,9},{9,17},{1,25},{26,2},{18... | collective-permute-start | bytes 393224 | tf_op jit(solution)/shard_map/ppermute | solution.py:28
  43.5 0.0 collective-permute-done.10
  43.5 1.8 %collective-permute-start.11 = (f32[8,128]{1,0:T(8,128)S(1)}, f32[8,128]{1,0:T(8,128)S(1)}, u32[]{:S(2)}, u32[]{:S(2)}) collective-permute-start(f32[8,128]{1,0:T(8,128)S(1)} %add.57), channel_id=1, source_target_pairs={{2,0},{3,1},{0,2},{1,3},{6,4},{7,5},{4,6},{5,7},{10,8},{11,9},{8,1... | collective-permute-start | bytes 12296 | tf_op jit(solution)/shard_map/ppermute | solution.py:28
  45.3 1.8 %collective-permute-done.11 = f32[8,128]{1,0:T(8,128)S(1)} collective-permute-done((f32[8,128]{1,0:T(8,128)S(1)}, f32[8,128]{1,0:T(8,128)S(1)}, u32[]{:S(2)}, u32[]{:S(2)}) %collective-permute-start.11) | collective-permute-done | bytes 4128 | tf_op jit(solution)/shard_map/ppermute | solution.py:28
  47.2 1.8 %collective-permute-start.12 = (f32[8,128]{1,0:T(8,128)S(1)}, f32[8,128]{1,0:T(8,128)S(1)}, u32[]{:S(2)}, u32[]{:S(2)}) collective-permute-start(f32[8,128]{1,0:T(8,128)S(1)} %add.58), channel_id=1, source_target_pairs={{4,0},{5,1},{6,2},{7,3},{0,4},{1,5},{2,6},{3,7},{12,8},{13,9},{14,... | collective-permute-start | bytes 12296 | tf_op jit(solution)/shard_map/ppermute | solution.py:28
  48.9 1.8 %collective-permute-done.12 = f32[8,128]{1,0:T(8,128)S(1)} collective-permute-done((f32[8,128]{1,0:T(8,128)S(1)}, f32[8,128]{1,0:T(8,128)S(1)}, u32[]{:S(2)}, u32[]{:S(2)}) %collective-permute-start.12) | collective-permute-done | bytes 4128 | tf_op jit(solution)/shard_map/ppermute | solution.py:28
  50.8 1.0 %collective-permute-start.13 = (f32[8,128]{1,0:T(8,128)S(1)}, f32[8,128]{1,0:T(8,128)S(1)}, u32[]{:S(2)}, u32[]{:S(2)}) collective-permute-start(f32[8,128]{1,0:T(8,128)S(1)} %add.59), channel_id=1, source_target_pairs={{8,0},{0,8},{24,16},{16,24},{9,1},{1,9},{25,17},{17,25},{10,2},{2,... | collective-permute-start | bytes 12296 | tf_op jit(solution)/shard_map/ppermute | solution.py:28
  51.8 2.6 %collective-permute-done.13 = f32[8,128]{1,0:T(8,128)S(1)} collective-permute-done((f32[8,128]{1,0:T(8,128)S(1)}, f32[8,128]{1,0:T(8,128)S(1)}, u32[]{:S(2)}, u32[]{:S(2)}) %collective-permute-start.13) | collective-permute-done | bytes 4128 | tf_op jit(solution)/shard_map/ppermute | solution.py:28
  54.4 0.7 %collective-permute-start.14 = (f32[8,128]{1,0:T(8,128)S(1)}, f32[8,128]{1,0:T(8,128)S(1)}, u32[]{:S(2)}, u32[]{:S(2)}) collective-permute-start(f32[8,128]{1,0:T(8,128)S(1)} %add.60), channel_id=1, source_target_pairs={{16,0},{24,8},{0,16},{8,24},{17,1},{25,9},{1,17},{9,25},{18,2},{26... | collective-permute-start | bytes 12296 | tf_op jit(solution)/shard_map/ppermute | solution.py:28
  55.1 3.8 %collective-permute-done.14 = f32[8,128]{1,0:T(8,128)S(1)} collective-permute-done((f32[8,128]{1,0:T(8,128)S(1)}, f32[8,128]{1,0:T(8,128)S(1)}, u32[]{:S(2)}, u32[]{:S(2)}) %collective-permute-start.14) | collective-permute-done | bytes 4128 | tf_op jit(solution)/shard_map/ppermute | solution.py:28
  58.9 0.6 %slice_reduce_fusion = f32[2]{0:T(128)} fusion(f32[8,128]{1,0:T(8,128)S(1)} %add.61), kind=kLoop, calls=%fused_computation.22 | loop fusion | bytes 16 | tf_op jit(solution)/shard_map/slice | solution.py:484
  59.5 0.0 collective-permute-done.4.rest_1_
  59.5 0.0 collective-permute-done.5.rest_2_
  59.5 0.0 collective-permute-done.6.rest_3_
  59.6 0.6 copy-done.4
  60.2 0.1 copy-done.5
  60.2 0.1 copy-done.6
  60.3 1.9 %join.1 = f32[2,16,4096]{2,1,0:T(8,128)} custom-call(f32[2,16,1024]{2,1,0:T(8,128)} %copy-done.2, f32[2,16,1024]{2,1,0:T(8,128)} %copy-done.4, f32[2,16,1024]{2,1,0:T(8,128)} %copy-done.5, f32[2,16,1024]{2,1,0:T(8,128)} %copy-done.6), custom_call_target="tpu_custom_call" | custom-call | tf_op jit(solution)/shard_map/join/pallas_call | solution.py:475
  (16 shorter events, 0.1 us)
Async XLA Ops:
  0.6 7.6 %copy-start.8 = (f32[1,2,2,512]{3,2,1,0:T(2,128)S(1)}, f32[1,2,2,512]{3,2,1,0:T(2,128)}, u32[]{:S(2)}) copy-start(f32[1,2,2,512]{3,2,1,0:T(2,128)} %param.14) | copy-start | bytes 24580
  0.6 7.6 %copy-start.7 = (s32[1,2,512]{2,1,0:T(2,128)S(1)}, s32[1,2,512]{2,1,0:T(2,128)}, u32[]{:S(2)}) copy-start(s32[1,2,512]{2,1,0:T(2,128)} %param.13) | copy-start | bytes 12292
  0.7 20.7 %copy-start.3 = (s32[1,32]{1,0:T(1,128)S(1)}, s32[1,32]{1,0:T(1,128)}, u32[]{:S(2)}) copy-start(s32[1,32]{1,0:T(1,128)} %mask.3) | copy-start | bytes 388
  3.0 31.2 %copy-start = (f32[1,3,16,4096]{3,2,1,0:T(8,128)S(1)}, f32[1,3,16,4096]{3,2,1,0:T(8,128)}, u32[]{:S(2)}) copy-start(f32[1,3,16,4096]{3,2,1,0:T(8,128)} %heads.3) | copy-start | bytes 2359300
  3.1 18.3 %collective-permute-start.1 = (f32[5,16,1280]{2,1,0:T(8,128)}, f32[5,16,1280]{2,1,0:T(8,128)S(1)}, u32[]{:S(2)}, u32[]{:S(2)}) collective-permute-start(f32[5,16,1280]{2,1,0:T(8,128)} %get-tuple-element.14.packed), channel_id=1, source_target_pairs={{1,2},{3,4},{5,6},{2,1},{4,3},{6,5},{9,10},{11,12},{13,14},{10,9},... | collective-permute-start | bytes 1228808 | tf_op jit(solution)/shard_map/ppermute | solution.py:62
  3.9 17.5 %collective-permute-start = (f32[5,16,1280]{2,1,0:T(8,128)}, f32[5,16,1280]{2,1,0:T(8,128)S(1)}, u32[]{:S(2)}, u32[]{:S(2)}) collective-permute-start(f32[5,16,1280]{2,1,0:T(8,128)} %get-tuple-element.14.packed), channel_id=1, source_target_pairs={{0,1},{1,0},{2,3},{3,2},{4,5},{5,4},{6,7},{7,6},{8,9},{9,8},{10,11... | collective-permute-start | bytes 1228808 | tf_op jit(solution)/shard_map/ppermute | solution.py:56
  8.3 3.8 %collective-permute-start.2 = (f32[1,8,512]{2,1,0:T(8,128)S(1)}, f32[1,8,512]{2,1,0:T(8,128)S(1)}, u32[]{:S(2)}, u32[]{:S(2)}) collective-permute-start(f32[1,8,512]{2,1,0:T(8,128)S(1)} %bitcast.39), channel_id=1, source_target_pairs={{8,0},{0,8},{24,16},{16,24},{9,1},{1,9},{25,17},{17,25},{10,2},{2,... | collective-permute-start | bytes 49160 | tf_op jit(solution)/shard_map/ppermute | solution.py:28
  12.2 4.9 %collective-permute-start.3 = (f32[2,8,512]{2,1,0:T(8,128)S(1)}, f32[2,8,512]{2,1,0:T(8,128)S(1)}, u32[]{:S(2)}, u32[]{:S(2)}) collective-permute-start(f32[2,8,512]{2,1,0:T(8,128)S(1)} %pad_maximum_fusion.1), channel_id=1, source_target_pairs={{16,0},{24,8},{0,16},{8,24},{17,1},{25,9},{1,17},{9,25},{18,2},{26... | collective-permute-start | bytes 98312 | tf_op jit(solution)/shard_map/ppermute | solution.py:28
  14.7 17.0 %collective-permute-start.7 = (f32[3,16,1152]{2,1,0:T(8,128)}, f32[3,16,1152]{2,1,0:T(8,128)S(1)}, u32[]{:S(2)}, u32[]{:S(2)}) collective-permute-start(f32[3,16,1152]{2,1,0:T(8,128)} %get-tuple-element.20), channel_id=1, source_target_pairs={{8,0},{0,8},{24,16},{16,24},{9,1},{1,9},{25,17},{17,25},{10,2},{2,... | collective-permute-start | bytes 663560 | tf_op jit(solution)/shard_map/ppermute | solution.py:28
  16.3 17.9 %collective-permute-start.8 = (f32[3,16,1152]{2,1,0:T(8,128)}, f32[3,16,1152]{2,1,0:T(8,128)S(1)}, u32[]{:S(2)}, u32[]{:S(2)}) collective-permute-start(f32[3,16,1152]{2,1,0:T(8,128)} %get-tuple-element.21), channel_id=1, source_target_pairs={{16,0},{24,8},{0,16},{8,24},{17,1},{25,9},{1,17},{9,25},{18,2},{26... | collective-permute-start | bytes 663560 | tf_op jit(solution)/shard_map/ppermute | solution.py:28
  17.1 17.1 %collective-permute-start.9 = (f32[3,16,1152]{2,1,0:T(8,128)}, f32[3,16,1152]{2,1,0:T(8,128)S(1)}, u32[]{:S(2)}, u32[]{:S(2)}) collective-permute-start(f32[3,16,1152]{2,1,0:T(8,128)} %get-tuple-element.22), channel_id=1, source_target_pairs={{24,0},{16,8},{8,16},{0,24},{25,1},{17,9},{9,17},{1,25},{26,2},{18... | collective-permute-start | bytes 663560 | tf_op jit(solution)/shard_map/ppermute | solution.py:28
  21.4 1.0 %copy-start.1 = (f32[5,16,1280]{2,1,0:T(8,128)S(1)}, f32[5,16,1280]{2,1,0:T(8,128)}, u32[]{:S(2)}) copy-start(f32[5,16,1280]{2,1,0:T(8,128)} %get-tuple-element.14.packed) | copy-start | bytes 1228804
  31.1 0.6 %copy-start.2 = (f32[2,16,1024]{2,1,0:T(8,128)}, f32[2,16,1024]{2,1,0:T(8,128)S(1)}, u32[]{:S(2)}) copy-start(f32[2,16,1024]{2,1,0:T(8,128)S(1)} %get-tuple-element.15.rest_0_) | copy-start | bytes 393220
  37.3 6.3 %collective-permute-start.10 = (f32[8,128]{1,0:T(8,128)S(1)}, f32[8,128]{1,0:T(8,128)S(1)}, u32[]{:S(2)}, u32[]{:S(2)}) collective-permute-start(f32[8,128]{1,0:T(8,128)S(1)} %get-tuple-element.24), channel_id=1, source_target_pairs={{1,0},{0,1},{3,2},{2,3},{5,4},{4,5},{7,6},{6,7},{9,8},{8,9},{11,10... | collective-permute-start | bytes 12296 | tf_op jit(solution)/shard_map/ppermute | solution.py:28
  37.4 22.2 %collective-permute-start.4 = (f32[2,16,1024]{2,1,0:T(8,128)S(1)}, f32[2,16,1024]{2,1,0:T(8,128)S(1)}, u32[]{:S(2)}, u32[]{:S(2)}) collective-permute-start(f32[2,16,1024]{2,1,0:T(8,128)S(1)} %get-tuple-element.16), channel_id=1, source_target_pairs={{8,0},{0,8},{24,16},{16,24},{9,1},{1,9},{25,17},{17,25},{10,2},{2,... | collective-permute-start | bytes 393224 | tf_op jit(solution)/shard_map/ppermute | solution.py:28
  41.1 18.4 %collective-permute-start.5 = (f32[2,16,1024]{2,1,0:T(8,128)S(1)}, f32[2,16,1024]{2,1,0:T(8,128)S(1)}, u32[]{:S(2)}, u32[]{:S(2)}) collective-permute-start(f32[2,16,1024]{2,1,0:T(8,128)S(1)} %get-tuple-element.17), channel_id=1, source_target_pairs={{16,0},{24,8},{0,16},{8,24},{17,1},{25,9},{1,17},{9,25},{18,2},{26... | collective-permute-start | bytes 393224 | tf_op jit(solution)/shard_map/ppermute | solution.py:28
  41.1 18.4 %collective-permute-start.6 = (f32[2,16,1024]{2,1,0:T(8,128)S(1)}, f32[2,16,1024]{2,1,0:T(8,128)S(1)}, u32[]{:S(2)}, u32[]{:S(2)}) collective-permute-start(f32[2,16,1024]{2,1,0:T(8,128)S(1)} %get-tuple-element.18), channel_id=1, source_target_pairs={{24,0},{16,8},{8,16},{0,24},{25,1},{17,9},{9,17},{1,25},{26,2},{18... | collective-permute-start | bytes 393224 | tf_op jit(solution)/shard_map/ppermute | solution.py:28
  43.5 3.6 %collective-permute-start.11 = (f32[8,128]{1,0:T(8,128)S(1)}, f32[8,128]{1,0:T(8,128)S(1)}, u32[]{:S(2)}, u32[]{:S(2)}) collective-permute-start(f32[8,128]{1,0:T(8,128)S(1)} %add.57), channel_id=1, source_target_pairs={{2,0},{3,1},{0,2},{1,3},{6,4},{7,5},{4,6},{5,7},{10,8},{11,9},{8,1... | collective-permute-start | bytes 12296 | tf_op jit(solution)/shard_map/ppermute | solution.py:28
  47.2 3.6 %collective-permute-start.12 = (f32[8,128]{1,0:T(8,128)S(1)}, f32[8,128]{1,0:T(8,128)S(1)}, u32[]{:S(2)}, u32[]{:S(2)}) collective-permute-start(f32[8,128]{1,0:T(8,128)S(1)} %add.58), channel_id=1, source_target_pairs={{4,0},{5,1},{6,2},{7,3},{0,4},{1,5},{2,6},{3,7},{12,8},{13,9},{14,... | collective-permute-start | bytes 12296 | tf_op jit(solution)/shard_map/ppermute | solution.py:28
  50.8 3.6 %collective-permute-start.13 = (f32[8,128]{1,0:T(8,128)S(1)}, f32[8,128]{1,0:T(8,128)S(1)}, u32[]{:S(2)}, u32[]{:S(2)}) collective-permute-start(f32[8,128]{1,0:T(8,128)S(1)} %add.59), channel_id=1, source_target_pairs={{8,0},{0,8},{24,16},{16,24},{9,1},{1,9},{25,17},{17,25},{10,2},{2,... | collective-permute-start | bytes 12296 | tf_op jit(solution)/shard_map/ppermute | solution.py:28
  54.4 4.5 %collective-permute-start.14 = (f32[8,128]{1,0:T(8,128)S(1)}, f32[8,128]{1,0:T(8,128)S(1)}, u32[]{:S(2)}, u32[]{:S(2)}) collective-permute-start(f32[8,128]{1,0:T(8,128)S(1)} %add.60), channel_id=1, source_target_pairs={{16,0},{24,8},{0,16},{8,24},{17,1},{25,9},{1,17},{9,25},{18,2},{26... | collective-permute-start | bytes 12296 | tf_op jit(solution)/shard_map/ppermute | solution.py:28
  59.5 0.6 %copy-start.4 = (f32[2,16,1024]{2,1,0:T(8,128)}, f32[2,16,1024]{2,1,0:T(8,128)S(1)}, u32[]{:S(2)}) copy-start(f32[2,16,1024]{2,1,0:T(8,128)S(1)} %collective-permute-done.4.rest_1_) | copy-start | bytes 393220
  59.5 0.7 %copy-start.5 = (f32[2,16,1024]{2,1,0:T(8,128)}, f32[2,16,1024]{2,1,0:T(8,128)S(1)}, u32[]{:S(2)}) copy-start(f32[2,16,1024]{2,1,0:T(8,128)S(1)} %collective-permute-done.5.rest_2_) | copy-start | bytes 393220
  59.5 0.7 %copy-start.6 = (f32[2,16,1024]{2,1,0:T(8,128)}, f32[2,16,1024]{2,1,0:T(8,128)S(1)}, u32[]{:S(2)}) copy-start(f32[2,16,1024]{2,1,0:T(8,128)S(1)} %collective-permute-done.6.rest_3_) | copy-start | bytes 393220

commit v2 on v0

v2 whole, which is shorter than its diff:
```python
import functools

import jax
import jax.numpy as jnp
from jax import lax
from jax.experimental import pallas as pl
from jax.experimental.pallas import tpu as pltpu
from jax.sharding import PartitionSpec as P

BLOCK = 128
STEPS = 2
SWEEPS = 2
LANES = 128
WIDE = 256
PIECES = 3
F32 = jnp.float32
BF16 = jnp.bfloat16
VMEM_LIMIT = 24 * 2**20


def fetch(value, axis, hop):
    count = lax.axis_size(axis)
    return lax.ppermute(value, axis, [(i ^ hop, i) for i in range(count)])


def gather(value, axis):
    blocks, hop = (value[None], 1)
    while hop < lax.axis_size(axis):
        blocks = jnp.concatenate([blocks, fetch(blocks, axis, hop)], axis=0)
        hop *= 2
    return blocks


def total(value, axis, hop=1, until=None):
    while hop < (until or lax.axis_size(axis)):
        value = value + fetch(value, axis, hop)
        hop *= 2
    return value


def inner_pairs(value):
    count = lax.axis_size("tile")
    pairs = [(i, i ^ 1) for i in range(count) if i ^ 1 < count]
    return lax.ppermute(value, "tile", pairs)


def outer_pairs(value):
    count = lax.axis_size("tile")
    low = range(1, count - 1, 2)
    return lax.ppermute(value, "tile", [(i, i + 1) for i in low] + [(i + 1, i) for i in low])


class Plan:
    def __init__(self, rows, width, sections, members, observed):
        self.rows, self.width, self.sections = (rows, width, sections)
        self.members, self.observed = (members, observed)
        self.half = width // 2
        sweeps = sections * STEPS * SWEEPS
        self.halo = -(-sweeps // LANES) * LANES
        self.window = self.half + self.halo
        self.tiles = self.window // LANES
        self.ext = 3 * rows
        self.per_phase = max(1, rows // (STEPS * SWEEPS))
        self.groups = sections // 2
        self.out_columns = width // sections

    def start(self, index):
        return pl.multiple_of((index % 2) * (self.half - self.halo), LANES)

    def own(self, index):
        return pl.multiple_of((index % 2) * self.halo, LANES)

    def bands(self, top, count):
        done = 0
        while done < count:
            low = done * STEPS * SWEEPS // 8 * 8
            until = done + 1
            while until < count and until * STEPS * SWEEPS // 8 * 8 == low:
                until += 1
            yield done, until, low
            done = until


def run_copies(copies, sems):
    started = [pltpu.make_async_copy(a, b, sems.at[i]) for i, (a, b) in enumerate(copies)]
    for copy in started:
        copy.start()
    for copy in started:
        copy.wait()


def pack_kernel(plan, capacity, cond_row, cond_col, terminal, packed, sems):
    columns = pl.ds(plan.start(lax.axis_index("tm")), plan.window)
    copies = [
        (capacity.at[:, columns], packed.at[0]),
        (cond_row.at[:, columns], packed.at[1]),
        (cond_col.at[:, columns], packed.at[2]),
        (terminal.at[:, :, columns], packed.at[pl.ds(3, plan.members)]),
    ]
    run_copies(copies, sems)


def heads_kernel(plan, heads, out, sems):
    others = pl.ds(plan.start(lax.axis_index("tm") + 1), plan.window)
    run_copies([(heads.at[0, :, :, others], out)], sems)


def lines_kernel(plan, cells, weights, lines):
    at = 0
    for step in range(STEPS):
        place = cells[0, step : step + 1].astype(F32)
        row = jnp.floor((place + 0.5) * (1.0 / plan.width))
        lines[at : at + 1] = row
        lines[at + 1 : at + 2] = place - row * plan.width
        lines[at + 2 : at + 2 + plan.members] = weights[0, step]
        at += 2 + plan.members


def force_kernel(plan, top, count, obs, force):
    me = lax.axis_index("tm")
    tile = lax.axis_index("tile")
    start = plan.start(me)
    members, observed = (plan.members, plan.observed)
    wides = -(-plan.window // WIDE)

    def observe(number, step, low, height):
        lines = obs[(top - number) ^ me]
        first = (2 + members) * step
        row = lines[first : first + 1] - ((tile - 1) * plan.rows + low).astype(F32)
        col = lines[first + 1 : first + 2] - start.astype(F32)
        inside = (row >= 0.0) & (row < height) & (col >= 0.0) & (col < plan.window)
        group = jnp.floor(col * (1.0 / WIDE))
        key = jnp.where(inside, group * height + row, -1.0).astype(jnp.int32)
        within = (col - group * WIDE).astype(jnp.int32)
        hit = lax.broadcasted_iota(jnp.int32, (wides * height, observed), 0) == key
        left = []
        for m in range(members):
            weight = lines[first + 2 + m : first + 3 + m]
            parts = []
            for _ in range(PIECES):
                piece = weight.astype(BF16).astype(F32)
                parts.append(jnp.where(hit, piece, 0.0).astype(BF16))
                weight = weight - piece
            left.append(jnp.concatenate(parts, axis=1))
        place = lax.broadcasted_iota(jnp.int32, (WIDE, observed), 0)
        right = jnp.where(place == within, 1.0, 0.0).astype(BF16)
        found = lax.dot_general(
            jnp.concatenate(left, axis=0),
            jnp.concatenate([right] * PIECES, axis=1),
            (((1,), (1,)), ((), ())),
            preferred_element_type=F32,
        )
        for m in range(members):
            for g in range(wides):
                at = (m * wides + g) * height
                end = min(plan.window, (g + 1) * WIDE)
                value = found[at : at + height, : end - g * WIDE]
                force[number, step, m, low : low + height, g * WIDE : end] = value

    for first, end, low in plan.bands(top, count):

        def body(number, _, low=low):
            for step in range(STEPS):
                observe(number, step, low, plan.ext - 2 * low)

        lax.fori_loop(first, end, body, None)


def chain_kernel(plan, top, count, mask, packed_in, inner, outer, force, *rest):
    first = top == plan.sections - 1
    if not first:
        field, field_inner, field_outer = rest[:3]
        rest = rest[3:]
    history, mine, send, east, west, south, north, act_rd, cap_rd, x0, x1, rhs, packed, sem = rest
    copy = pltpu.make_async_copy(packed_in, packed, sem)
    copy.start()
    me = lax.axis_index("tm")
    tile = lax.axis_index("tile")
    rows, ext, members, tiles = (plan.rows, plan.ext, plan.members, plan.tiles)
    start = plan.start(me)
    even = tile % 2 == 0

    def stacked(own, core, chip, index, columns):
        a, b = (core[index, :, columns], chip[index, :, columns])
        parts = [jnp.where(even, b, a), own[index, :, columns], jnp.where(even, a, b)]
        return jnp.concatenate(parts, axis=0)

    lane = lax.broadcasted_iota(jnp.int32, (1, LANES), 1)
    ends = lane == LANES - 1
    begins = lane == 0
    tile_rows = lax.axis_size("tile") * rows

    def chunk_active(chunk, column):
        if column >= tiles:
            return jnp.float32(0.0)
        row = (tile + chunk - 1) * rows
        inside = (row >= 0) & (row < tile_rows)
        block = jnp.clip(row, 0, tile_rows - 1) // BLOCK
        value = mask[block, (start + column * LANES) // BLOCK]
        return jnp.where(inside, value, 0).astype(F32)

    def active(column):
        parts = [jnp.full((rows, LANES), chunk_active(chunk, column), F32) for chunk in range(3)]
        return jnp.concatenate(parts, axis=0)

    def cols(column):
        return pl.ds(column * LANES, LANES)

    row_id = lax.broadcasted_iota(jnp.int32, (ext, LANES), 0)
    act = active(0)
    previous = jnp.zeros((ext, LANES), F32)
    copy.wait()
    for c in range(tiles):
        act_next = active(c + 1)
        pair = act * jnp.where(ends, act_next, act)
        e = stacked(packed, inner, outer, 1, cols(c)) * pair
        w = pltpu.roll(jnp.where(ends, previous, e), 1, axis=1)
        below = jnp.where(row_id == ext - 1, 0.0, pltpu.roll(act, ext - 1, axis=0))
        s = stacked(packed, inner, outer, 2, cols(c)) * act * below
        n = jnp.where(row_id == 0, 0.0, pltpu.roll(s, 1, axis=0))
        cap = stacked(packed, inner, outer, 0, cols(c))
        diagonal = cap + e + w + s + n
        inverse = jnp.where(diagonal > 0.0, 1.0 / jnp.where(diagonal > 0.0, diagonal, 1.0), 0.0)
        east[:, cols(c)] = e * inverse
        west[:, cols(c)] = w * inverse
        south[:, cols(c)] = s * inverse
        north[:, cols(c)] = n * inverse
        act_rd[:, cols(c)] = act * inverse
        cap_rd[:, cols(c)] = act * cap * inverse
        for m in range(members):
            if first:
                x0[m, :, cols(c)] = stacked(packed, inner, outer, 3 + m, cols(c))
            else:
                x0[m, :, cols(c)] = stacked(field, field_inner, field_outer, m, cols(c))
        previous = e
        act = act_next

    def sweep(source, target, low, height, number, step, initial):
        band = slice(low, low + height)
        zero = jnp.zeros((height, LANES), F32)
        here = [source[m, band, cols(0)] for m in range(members)]
        turned = [pltpu.roll(h, LANES - 1, axis=1) for h in here]
        left = [zero] * members
        for c in range(tiles):
            e, w, s, n = (ref[band, cols(c)] for ref in (east, west, south, north))
            for m in range(members):
                if c + 1 < tiles:
                    after = source[m, band, cols(c + 1)]
                    after_turned = pltpu.roll(after, LANES - 1, axis=1)
                else:
                    after = after_turned = zero
                back = pltpu.roll(here[m], 1, axis=1)
                x_east = jnp.where(ends, after_turned, turned[m])
                x_west = jnp.where(begins, left[m], back)
                x_south = pltpu.roll(here[m], height - 1, axis=0)
                x_north = pltpu.roll(here[m], 1, axis=0)
                if initial:
                    value = cap_rd[band, cols(c)] * here[m] + act_rd[band, cols(c)] * force[number, step, m, band, cols(c)]
                    rhs[m, band, cols(c)] = value
                else:
                    value = rhs[m, band, cols(c)]
                target[m, band, cols(c)] = value + e * x_east + w * x_west + s * x_south + n * x_north
                left[m], here[m], turned[m] = (back, after, after_turned)

    lowest = me - me % 2

    def one_section(number, low):
        slot = jnp.clip(top - number - lowest, 0, 1)
        height = ext - 2 * low
        for step in reversed(range(STEPS)):
            refs = (x0, x1)
            for index in range(SWEEPS):
                sweep(refs[index % 2], refs[(index + 1) % 2], low, height, number, step, index == 0)
            if SWEEPS % 2:
                x0[:, low : low + height, :] = x1[:, low : low + height, :]
            history[slot, step] = x0[:, rows : 2 * rows, :]

    wanted = top - lowest + 1
    for begin, end, low in plan.bands(top, count):
        lax.fori_loop(begin, jnp.clip(wanted, begin, end), lambda i, _, low=low: one_section(i, low), None)

    own = pl.ds(plan.own(me), plan.half)
    mine[...] = history[me % 2, 0, :, :, own]
    send[...] = history[1 - me % 2, 0, :, :, own]


def sens_kernel(plan, mask, packed, history, heads, other_heads, *rest):
    cond_outs, storage_out = (rest[:-1], rest[-1])
    me = lax.axis_index("tm")
    tile = lax.axis_index("tile")
    rows, members = (plan.rows, plan.members)
    start, own = (plan.start(me), plan.own(me))
    side, group = (me % 2, me // 2)
    ends = lax.broadcasted_iota(jnp.int32, (1, LANES), 1) == LANES - 1
    block_row = tile * rows // BLOCK
    columns = plan.width // LANES

    def after(here, following):
        return jnp.where(ends, pltpu.roll(following, LANES - 1, axis=1), pltpu.roll(here, LANES - 1, axis=1))

    def lanes(offset):
        return pl.ds(pl.multiple_of(offset, LANES), LANES)

    stored = [jnp.zeros((rows, LANES), F32) for _ in range(members)]
    for slot, out in enumerate(cond_outs):
        for t in range(plan.out_columns // LANES):
            here = own + (group ^ slot) * plan.out_columns + t * LANES
            there = jnp.minimum(here + LANES, plan.window - LANES)
            column = (start + here) // LANES
            act = mask[block_row, column].astype(F32)
            act_next = mask[block_row, jnp.minimum(column + 1, columns - 1)].astype(F32)
            act_next = jnp.where(column + 1 < columns, act_next, 0.0)
            pair = act * jnp.where(ends, act_next, act)
            capacity = packed[0, :, lanes(here)]
            sens = jnp.zeros((rows, LANES), F32)
            for which in range(2):
                section = side if which == 0 else 1 - side
                if which == 0:
                    levels = [heads[0, k, :, lanes(start + here)] for k in range(STEPS + 1)]
                    nexts = [heads[0, k, :, lanes(start + there)] for k in range(STEPS + 1)]
                else:
                    levels = [other_heads[k, :, lanes(here)] for k in range(STEPS + 1)]
                    nexts = [other_heads[k, :, lanes(there)] for k in range(STEPS + 1)]
                for step in range(STEPS):
                    fields = [history[section, step, m, :, lanes(here)] for m in range(members)]
                    rise = capacity * (levels[step + 1] - levels[step])
                    for m in range(members):
                        stored[m] = stored[m] + fields[m] * rise
                    both = functools.reduce(jnp.add, fields)
                    follow = [history[section, step, m, :, lanes(there)] for m in range(members)]
                    both_next = functools.reduce(jnp.add, follow)
                    slope = after(levels[step + 1], nexts[step + 1]) - levels[step + 1]
                    sens = sens + (after(both, both_next) - both) * slope
            out[:, t * LANES : (t + 1) * LANES] = sens * pair
    storage_out[...] = jnp.zeros((8, LANES), F32)
    for m in range(members):
        storage_out[m : m + 1, :] = jnp.full((1, LANES), jnp.sum(stored[m]), F32)


def shards(heads, capacity, cond_row, cond_col, terminal, obs_cell, obs_weight, block_mask):
    rows, width = capacity.shape
    members = terminal.shape[0]
    sections = lax.axis_size("tm")
    plan = Plan(rows, width, sections, members, obs_cell.shape[2])
    window, ext, half = (plan.window, plan.ext, plan.half)
    me = lax.axis_index("tm")
    anywhere = pl.BlockSpec(memory_space=pl.ANY)
    in_vmem = pl.BlockSpec(memory_space=pltpu.VMEM)
    in_smem = pl.BlockSpec(memory_space=pltpu.SMEM)
    params = pltpu.CompilerParams(vmem_limit_bytes=VMEM_LIMIT)

    def shape(*dims):
        return jax.ShapeDtypeStruct(dims, F32)

    packed = pl.pallas_call(
        functools.partial(pack_kernel, plan),
        out_shape=shape(3 + members, rows, window),
        in_specs=[anywhere] * 4,
        out_specs=in_vmem,
        scratch_shapes=[pltpu.SemaphoreType.DMA((4,))],
        name="pack",
    )(capacity, cond_row, cond_col, terminal)
    head_send = pl.pallas_call(
        functools.partial(heads_kernel, plan),
        out_shape=shape(STEPS + 1, rows, window),
        in_specs=[anywhere],
        out_specs=in_vmem,
        scratch_shapes=[pltpu.SemaphoreType.DMA((1,))],
        name="heads",
    )(heads)
    lines = pl.pallas_call(
        functools.partial(lines_kernel, plan),
        out_shape=shape(STEPS * (2 + members), plan.observed),
        in_specs=[in_vmem] * 2,
        out_specs=in_vmem,
        name="lines",
    )(obs_cell, obs_weight)
    outer = outer_pairs(packed)
    inner = inner_pairs(packed)

    obs = gather(lines, "tm")
    obs, head_send = lax.optimization_barrier((obs, head_send))
    other_heads = fetch(head_send, "tm", 1)

    part = (members, rows, half)
    top = sections - 1
    field = []
    results = None
    while top >= 0:
        count = min(plan.per_phase, top + 1)
        force = pl.pallas_call(
            functools.partial(force_kernel, plan, top, count),
            out_shape=shape(count, STEPS, members, ext, window),
            in_specs=[in_vmem],
            out_specs=in_vmem,
            compiler_params=params,
            name="force",
        )(obs)
        plane = pltpu.VMEM((ext, window), F32)
        fields = pltpu.VMEM((members, ext, window), F32)
        now = pl.pallas_call(
            functools.partial(chain_kernel, plan, top, count),
            out_shape=[shape(2, STEPS, members, rows, window), shape(*part), shape(*part)],
            in_specs=[in_smem, anywhere] + [in_vmem] * (3 + len(field)),
            out_specs=[in_vmem] * 3,
            scratch_shapes=[
                *([plane] * 6),
                *([fields] * 3),
                pltpu.VMEM((3 + members, rows, window), F32),
                pltpu.SemaphoreType.DMA,
            ],
            compiler_params=params,
            name="chain",
        )(block_mask, packed, inner, outer, force, *field)
        if results is None:
            results = now
        else:
            results = [jnp.where(me - me % 2 > top, a, b) for a, b in zip(results, now)]
        top -= count
        if top >= 0:
            reached = now[0][0, 0]
            field = [reached, inner_pairs(reached), outer_pairs(reached)]
    history, mine, send = results

    other = fetch(send, "tm", 1)
    *cond, storage = pl.pallas_call(
        functools.partial(sens_kernel, plan),
        out_shape=[shape(rows, plan.out_columns)] * plan.groups + [shape(8, LANES)],
        in_specs=[in_smem] + [in_vmem] * 4,
        out_specs=[in_vmem] * (plan.groups + 1),
        compiler_params=params,
        name="sens",
    )(block_mask, packed, history, heads, other_heads)

    groups = plan.groups
    parts = []
    for slot in range(groups):
        moves = [(i, (i % 2) * groups + (i // 2 ^ slot)) for i in range(sections)]
        parts.append(lax.ppermute(cond[slot], "tm", moves))
    cond = functools.reduce(jnp.add, parts)
    storage = total(storage, "tile")
    side = me % 2
    halves = [jnp.where(side == 0, mine, other), jnp.where(side == 0, other, mine)]
    adjoint = jnp.concatenate(halves, axis=2)
    storage, adjoint = lax.optimization_barrier((storage, adjoint))
    storage = total(storage, "tm")
    return (adjoint[None], cond, storage[:members, 0])


def solution(mesh):
    placed = (
        P("tm", None, "tile", None),
        P("tile", None),
        P("tile", None),
        P("tile", None),
        P(None, "tile", None),
        P("tm", None, None),
        P("tm", None, None, None),
        P(),
    )
    return jax.shard_map(
        shards,
        mesh=mesh,
        in_specs=placed,
        out_specs=(P("tm", None, "tile", None), P("tile", "tm"), P()),
        check_vma=False,
    )
```

time: 301 us -> 56.4 us (0.19)
  starting transfers between devices: 103 us -> 20.9 us
  waiting for transfers between devices: 72 us -> 10.5 us
  blocking collectives: 42.7 us -> 0 us
  matrix products: 30.7 us -> 0 us
  local copies, waits for them, and re-layouts: 23 us -> 0.64 us
  Pallas kernels: 0 us -> 20.1 us
  between operations: 14.1 us -> 0.76 us
  other arithmetic: 12.8 us -> 2.97 us
    ppermute x37 -> x13, starting transfers between devices: 103 us -> 20.9 us  [the longest x9 16.2 us: fetch(): return lax.ppermute(value, axis, [(i ^ hop, i) for i in range(count)])]
    ppermute x37 -> x13, waiting for transfers between devices: 72 us -> 10.5 us  [the longest x9 10.5 us: fetch(): return lax.ppermute(value, axis, [(i ^ hop, i) for i in range(count)])]
    psum x1 -> x0, blocking collectives: 42.7 us -> none  [shards(): storage = lax.psum(storage_part, ('tm', 'tile'))]
    dot_general x8 -> x0, matrix products: 30.7 us -> none  [forcing(): jnp.einsum('gro,oc->grc', weighted_rows, col_hit, precision=lax.Precision...]
    pallas_call x0 -> x6, Pallas kernels: none -> 20.1 us  [the longest x1 8.22 us: shards(): pl.pallas_call(functools.partial(chain_kernel, plan, top, count), out_sha...]
    slice x39 -> x1, local copies, waits for them, and re-layouts: 8.69 us -> 0.63 us  [shards(): return (adjoint[None], cond, storage[:members, 0])]
    while x132 -> x0, local copies, waits for them, and re-layouts: 5.74 us -> none
    reduce_sum x8 -> x0, other arithmetic: 4.29 us -> none  [the longest x4 2.49 us: one_round(): jnp.sum(field * capacity * (later - earlier), axis=(1, 2))]
  transfers between devices with their start and end apart: 38 -> 13, of which waited for: 16 -> 6; matrix products, arithmetic and copies ran while one was open for 8% -> 5% of each run, Pallas kernels for 0% -> 32%
where the time goes in v2:
time: 56.4 us; the launch traced here: 55.9 us
  starting transfers between devices  20.9 us (37%)
  Pallas kernels  20.1 us (36%)
  waiting for transfers between devices  10.5 us (19%)
  other arithmetic  2.97 us (5%)
  between operations  0.76 us (1%)
  local copies, waits for them, and re-layouts  0.64 us (1%)
    ppermute x9, starting transfers between devices, fetch(): return lax.ppermute(value, axis, [(i ^ hop, i) for i in range(count)])  16.2 us
    ppermute x9, waiting for transfers between devices, fetch(): return lax.ppermute(value, axis, [(i ^ hop, i) for i in range(count)])  10.5 us
    pallas_call x1, Pallas kernels, shards(): pl.pallas_call(functools.partial(chain_kernel, plan, top, count), out_sha...  8.22 us
    pallas_call x1, Pallas kernels, shards(): pl.pallas_call(functools.partial(force_kernel, plan, top, count), out_sha...  5.49 us
    ppermute x2, starting transfers between devices, shards(): parts.append(lax.ppermute(cond[slot], 'tm', moves))  3.52 us
    pallas_call x1, Pallas kernels, shards(): pl.pallas_call(functools.partial(pack_kernel, plan), out_shape=shape(3 +...  2.08 us
    pallas_call x1, Pallas kernels, shards(): pl.pallas_call(functools.partial(heads_kernel, plan), out_shape=shape(STE...  1.76 us
    concatenate x2, other arithmetic, gather(): blocks = jnp.concatenate([blocks, fetch(blocks, axis, hop)], axis=0)  1.44 us
  transfers between devices with their start and end apart: 13, of which 6 were waited for; matrix products, arithmetic and copies ran while one was open for 5% of the time, Pallas kernels for 32%

profile of v2, /device:TPU:0, one launch (start us, length us, event | category | flops | bytes accessed | tf_op | source)
XLA Modules:
  0.0 55.9 jit_solution(11426682682706281232)
XLA Ops:
  0.6 0.0 copy-start.2
  0.6 2.1 %pack.1.packed_in.packed = f32[5,16,2176]{2,1,0:T(8,128)} custom-call(f32[16,4096]{1,0:T(8,128)} %capacity.1, f32[16,4096]{1,0:T(8,128)} %cond_row.1, f32[16,4096]{1,0:T(8,128)} %cond_col.1, f32[2,16,4096]{2,1,0:T(8,128)} %terminal.1), custom_call_target="tpu_custom_call" | custom-call | tf_op jit(solution)/shard_map/pack/pallas_call | solution.py:355
  2.7 0.0 copy-start
  2.7 0.5 collective-permute-start
  3.3 0.7 %collective-permute-start.1 = (f32[5,16,2176]{2,1,0:T(8,128)}, f32[5,16,2176]{2,1,0:T(8,128)S(1)}, u32[]{:S(2)}, u32[]{:S(2)}) collective-permute-start(f32[5,16,2176]{2,1,0:T(8,128)} %pack.1.packed_in.packed), channel_id=1, source_target_pairs={{1,2},{3,4},{5,6},{2,1},{4,3},{6,5},{9,10},{11,12},{13,14},{10,9},... | collective-permute-start | bytes 2088968 | tf_op jit(solution)/shard_map/ppermute | solution.py:50
  4.0 1.3 %lines.1 = f32[8,512]{1,0:T(8,128)} custom-call(s32[1,2,512]{2,1,0:T(2,128)} %cells.1, f32[1,2,2,512]{3,2,1,0:T(2,128)} %weights.1), custom_call_target="tpu_custom_call" | custom-call | tf_op jit(solution)/shard_map/lines/pallas_call | solution.py:371
  5.3 2.7 %collective-permute-start.2 = (f32[1,8,512]{2,1,0:T(8,128)}, f32[1,8,512]{2,1,0:T(8,128)S(1)}, u32[]{:S(2)}, u32[]{:S(2)}) collective-permute-start(f32[1,8,512]{2,1,0:T(8,128)} %bitcast.3), channel_id=1, source_target_pairs={{8,0},{0,8},{24,16},{16,24},{9,1},{1,9},{25,17},{17,25},{10,2},{2,... | collective-permute-start | bytes 49160 | tf_op jit(solution)/shard_map/ppermute | solution.py:23
  8.0 1.9 %collective-permute-done.2 = f32[1,8,512]{2,1,0:T(8,128)S(1)} collective-permute-done((f32[1,8,512]{2,1,0:T(8,128)}, f32[1,8,512]{2,1,0:T(8,128)S(1)}, u32[]{:S(2)}, u32[]{:S(2)}) %collective-permute-start.2) | collective-permute-done | bytes 16416 | tf_op jit(solution)/shard_map/ppermute | solution.py:23
  9.9 0.7 %pad_maximum_fusion.2 = f32[2,8,512]{2,1,0:T(8,128)S(1)} fusion(f32[1,8,512]{2,1,0:T(8,128)S(1)} %collective-permute-done.2, f32[1,8,512]{2,1,0:T(8,128)} %bitcast.4), kind=kLoop, calls=%fused_computation.4 | loop fusion | flops 8192 | bytes 65536 | tf_op jit(solution)/shard_map/concatenate | solution.py:29
  10.7 3.0 %collective-permute-start.3 = (f32[2,8,512]{2,1,0:T(8,128)S(1)}, f32[2,8,512]{2,1,0:T(8,128)S(1)}, u32[]{:S(2)}, u32[]{:S(2)}) collective-permute-start(f32[2,8,512]{2,1,0:T(8,128)S(1)} %pad_maximum_fusion.2), channel_id=1, source_target_pairs={{16,0},{24,8},{0,16},{8,24},{17,1},{25,9},{1,17},{9,25},{18,2},{26... | collective-permute-start | bytes 98312 | tf_op jit(solution)/shard_map/ppermute | solution.py:23
  13.7 1.8 %heads.3 = f32[3,16,2176]{2,1,0:T(8,128)} custom-call(f32[1,3,16,4096]{3,2,1,0:T(8,128)} %heads.5), custom_call_target="tpu_custom_call" | custom-call | tf_op jit(solution)/shard_map/heads/pallas_call | solution.py:363
  15.5 0.1 collective-permute-done.3
  15.6 0.7 %pad_maximum_fusion.1.obs = f32[4,8,512]{2,1,0:T(8,128)S(1)} fusion(f32[2,8,512]{2,1,0:T(8,128)S(1)} %collective-permute-done.3, f32[1,8,512]{2,1,0:T(8,128)S(1)} %collective-permute-done.2, f32[1,8,512]{2,1,0:T(8,128)} %bitcast.5), kind=kLoop, calls=%fused_computation.3 | loop fusion | flops 32768 | bytes 131072 | tf_op jit(solution)/shard_map/concatenate | solution.py:29
  16.3 0.0 copy-start.1
  16.3 1.9 %collective-permute-start.4 = (f32[3,16,2176]{2,1,0:T(8,128)}, f32[3,16,2176]{2,1,0:T(8,128)S(1)}, u32[]{:S(2)}, u32[]{:S(2)}) collective-permute-start(f32[3,16,2176]{2,1,0:T(8,128)} %heads.3), channel_id=1, source_target_pairs={{8,0},{0,8},{24,16},{16,24},{9,1},{1,9},{25,17},{17,25},{10,2},{2,... | collective-permute-start | bytes 1253384 | tf_op jit(solution)/shard_map/ppermute | solution.py:23
  18.3 5.5 %force.1 = f32[4,2,2,48,2176]{4,3,2,1,0:T(8,128)S(1)} custom-call(f32[4,8,512]{2,1,0:T(8,128)S(1)} %pad_maximum_fusion.1.obs), custom_call_target="tpu_custom_call" | custom-call | tf_op jit(solution)/shard_map/force/pallas_call | solution.py:391
  23.8 0.0 collective-permute-done.inner
  23.8 0.0 collective-permute-done.1.outer
  23.8 0.0 copy-done.2
  23.8 0.0 copy-done
  23.8 8.2 %chain.1 = (f32[2,2,2,16,2176]{4,3,2,1,0:T(8,128)S(1)}, f32[2,16,2048]{2,1,0:T(8,128)S(1)}, f32[2,16,2048]{2,1,0:T(8,128)S(1)}) custom-call(s32[1,32]{1,0:T(1,128)S(1)} %copy-done.2, f32[5,16,2176]{2,1,0:T(8,128)S(1)} %copy-done, f32[5,16,2176]{2,1,0:T(8,128)S(1)} %collective-permute-done.inner, f32[5,16,2176]{2,1,0:T(8,128)S(1)} %collective-permute-done.1.outer, ...), custom_call_target="tpu_custom_call" | custom-call | tf_op jit(solution)/shard_map/chain/pallas_call | solution.py:401
  32.0 0.2 collective-permute-start.8
  32.2 0.0 collective-permute-done.4.other_heads
  32.2 0.0 copy-done.1
  32.2 1.3 %sens.1 = (f32[16,1024]{1,0:T(8,128)S(1)}, f32[16,1024]{1,0:T(8,128)S(1)}, f32[8,128]{1,0:T(8,128)S(1)}) custom-call(s32[1,32]{1,0:T(1,128)S(1)} %copy-done.2, f32[5,16,2176]{2,1,0:T(8,128)S(1)} %copy-done, f32[2,2,2,16,2176]{4,3,2,1,0:T(8,128)S(1)} %get-tuple-element.14.history, f32[1,3,16,4096]{3,2,1,0:T(8,128)S(1)} %copy-done.1, ...), custom_call_target="tpu_custom_call" | custom-call | tf_op jit(solution)/shard_map/sens/pallas_call | solution.py:426
  33.4 2.2 %collective-permute-start.5 = (f32[8,128]{1,0:T(8,128)S(1)}, f32[8,128]{1,0:T(8,128)S(1)}, u32[]{:S(2)}, u32[]{:S(2)}) collective-permute-start(f32[8,128]{1,0:T(8,128)S(1)} %get-tuple-element.16), channel_id=1, source_target_pairs={{1,0},{0,1},{3,2},{2,3},{5,4},{4,5},{7,6},{6,7},{9,8},{8,9},{11,10... | collective-permute-start | bytes 12296 | tf_op jit(solution)/shard_map/ppermute | solution.py:23
  35.6 0.8 %collective-permute-done.5 = f32[8,128]{1,0:T(8,128)S(1)} collective-permute-done((f32[8,128]{1,0:T(8,128)S(1)}, f32[8,128]{1,0:T(8,128)S(1)}, u32[]{:S(2)}, u32[]{:S(2)}) %collective-permute-start.5) | collective-permute-done | bytes 4128 | tf_op jit(solution)/shard_map/ppermute | solution.py:23
  36.5 2.0 %collective-permute-start.6 = (f32[8,128]{1,0:T(8,128)S(1)}, f32[8,128]{1,0:T(8,128)S(1)}, u32[]{:S(2)}, u32[]{:S(2)}) collective-permute-start(f32[8,128]{1,0:T(8,128)S(1)} %add.22), channel_id=1, source_target_pairs={{2,0},{3,1},{0,2},{1,3},{6,4},{7,5},{4,6},{5,7},{10,8},{11,9},{8,1... | collective-permute-start | bytes 12296 | tf_op jit(solution)/shard_map/ppermute | solution.py:23
  38.4 1.6 %collective-permute-done.6 = f32[8,128]{1,0:T(8,128)S(1)} collective-permute-done((f32[8,128]{1,0:T(8,128)S(1)}, f32[8,128]{1,0:T(8,128)S(1)}, u32[]{:S(2)}, u32[]{:S(2)}) %collective-permute-start.6) | collective-permute-done | bytes 4128 | tf_op jit(solution)/shard_map/ppermute | solution.py:23
  40.1 2.7 %collective-permute-start.7 = (f32[8,128]{1,0:T(8,128)S(1)}, f32[8,128]{1,0:T(8,128)S(1)}, u32[]{:S(2)}, u32[]{:S(2)}) collective-permute-start(f32[8,128]{1,0:T(8,128)S(1)} %add.23), channel_id=1, source_target_pairs={{4,0},{5,1},{6,2},{7,3},{0,4},{1,5},{2,6},{3,7},{12,8},{13,9},{14,... | collective-permute-start | bytes 12296 | tf_op jit(solution)/shard_map/ppermute | solution.py:23
  42.7 0.7 %collective-permute-start.9 = (f32[16,1024]{1,0:T(8,128)S(1)}, f32[16,1024]{1,0:T(8,128)S(1)}, u32[]{:S(2)}, u32[]{:S(2)}) collective-permute-start(f32[16,1024]{1,0:T(8,128)S(1)} %get-tuple-element.20), channel_id=1, source_target_pairs={{0,0},{8,16},{16,8},{24,24},{1,1},{9,17},{17,9},{25,25},{2,2},{10,... | collective-permute-start | bytes 196616 | tf_op jit(solution)/shard_map/ppermute | solution.py:439
  43.4 2.9 %collective-permute-start.10 = (f32[16,1024]{1,0:T(8,128)S(1)}, f32[16,1024]{1,0:T(8,128)S(1)}, u32[]{:S(2)}, u32[]{:S(2)}) collective-permute-start(f32[16,1024]{1,0:T(8,128)S(1)} %get-tuple-element.21), channel_id=1, source_target_pairs={{0,8},{8,24},{16,0},{24,16},{1,9},{9,25},{17,1},{25,17},{2,10},{10... | collective-permute-start | bytes 196616 | tf_op jit(solution)/shard_map/ppermute | solution.py:439
  46.3 0.0 collective-permute-done.7
  46.3 0.0 collective-permute-done.8
  46.3 0.8 %pad_maximum_fusion = f32[2,16,4096]{2,1,0:T(8,128)} fusion(f32[2,16,2048]{2,1,0:T(8,128)S(1)} %get-tuple-element.24, f32[2,16,2048]{2,1,0:T(8,128)S(1)} %get-tuple-element.23), kind=kLoop, calls=%fused_computation | loop fusion | flops 131072 | bytes 1048576 | tf_op jit(solution)/shard_map/concatenate | solution.py:444
  47.2 0.0 collective-permute-start.11
  47.2 3.6 %collective-permute-done.11 = f32[8,128]{1,0:T(8,128)S(1)} collective-permute-done((f32[8,128]{1,0:T(8,128)S(1)}, f32[8,128]{1,0:T(8,128)S(1)}, u32[]{:S(2)}, u32[]{:S(2)}) %collective-permute-start.11) | collective-permute-done | bytes 4128 | tf_op jit(solution)/shard_map/ppermute | solution.py:23
  50.8 1.5 %collective-permute-start.12 = (f32[8,128]{1,0:T(8,128)S(1)}, f32[8,128]{1,0:T(8,128)S(1)}, u32[]{:S(2)}, u32[]{:S(2)}) collective-permute-start(f32[8,128]{1,0:T(8,128)S(1)} %add.27), channel_id=1, source_target_pairs={{16,0},{24,8},{0,16},{8,24},{17,1},{25,9},{1,17},{9,25},{18,2},{26... | collective-permute-start | bytes 12296 | tf_op jit(solution)/shard_map/ppermute | solution.py:23
  52.3 0.0 collective-permute-done.9
  52.3 0.0 collective-permute-done.10
  52.3 0.6 %add.26 = f32[16,1024]{1,0:T(8,128)} add(f32[16,1024]{1,0:T(8,128)S(1)} %collective-permute-done.9, f32[16,1024]{1,0:T(8,128)S(1)} %collective-permute-done.10) | non-fusion elementwise | flops 16384 | bytes 196608 | tf_op jit(solution)/shard_map/add | solution.py:440
  52.9 2.4 %collective-permute-done.12 = f32[8,128]{1,0:T(8,128)S(1)} collective-permute-done((f32[8,128]{1,0:T(8,128)S(1)}, f32[8,128]{1,0:T(8,128)S(1)}, u32[]{:S(2)}, u32[]{:S(2)}) %collective-permute-start.12) | collective-permute-done | bytes 4128 | tf_op jit(solution)/shard_map/ppermute | solution.py:23
  55.3 0.6 %slice_reduce_fusion = f32[2]{0:T(128)} fusion(f32[8,128]{1,0:T(8,128)S(1)} %add.28), kind=kLoop, calls=%fused_computation.5 | loop fusion | bytes 16 | tf_op jit(solution)/shard_map/slice | solution.py:447
  (6 shorter events, 0.1 us)
Async XLA Ops:
  0.6 23.1 %copy-start.2 = (s32[1,32]{1,0:T(1,128)S(1)}, s32[1,32]{1,0:T(1,128)}, u32[]{:S(2)}) copy-start(s32[1,32]{1,0:T(1,128)} %mask.3) | copy-start | bytes 388
  2.7 21.1 %copy-start = (f32[5,16,2176]{2,1,0:T(8,128)S(1)}, f32[5,16,2176]{2,1,0:T(8,128)}, u32[]{:S(2)}) copy-start(f32[5,16,2176]{2,1,0:T(8,128)} %pack.1.packed_in.packed) | copy-start | bytes 2088964
  2.7 21.0 %collective-permute-start = (f32[5,16,2176]{2,1,0:T(8,128)}, f32[5,16,2176]{2,1,0:T(8,128)S(1)}, u32[]{:S(2)}, u32[]{:S(2)}) collective-permute-start(f32[5,16,2176]{2,1,0:T(8,128)} %pack.1.packed_in.packed), channel_id=1, source_target_pairs={{0,1},{1,0},{2,3},{3,2},{4,5},{5,4},{6,7},{7,6},{8,9},{9,8},{10,11... | collective-permute-start | bytes 2088968 | tf_op jit(solution)/shard_map/ppermute | solution.py:44
  3.3 20.5 %collective-permute-start.1 = (f32[5,16,2176]{2,1,0:T(8,128)}, f32[5,16,2176]{2,1,0:T(8,128)S(1)}, u32[]{:S(2)}, u32[]{:S(2)}) collective-permute-start(f32[5,16,2176]{2,1,0:T(8,128)} %pack.1.packed_in.packed), channel_id=1, source_target_pairs={{1,2},{3,4},{5,6},{2,1},{4,3},{6,5},{9,10},{11,12},{13,14},{10,9},... | collective-permute-start | bytes 2088968 | tf_op jit(solution)/shard_map/ppermute | solution.py:50
  5.3 4.7 %collective-permute-start.2 = (f32[1,8,512]{2,1,0:T(8,128)}, f32[1,8,512]{2,1,0:T(8,128)S(1)}, u32[]{:S(2)}, u32[]{:S(2)}) collective-permute-start(f32[1,8,512]{2,1,0:T(8,128)} %bitcast.3), channel_id=1, source_target_pairs={{8,0},{0,8},{24,16},{16,24},{9,1},{1,9},{25,17},{17,25},{10,2},{2,... | collective-permute-start | bytes 49160 | tf_op jit(solution)/shard_map/ppermute | solution.py:23
  10.7 4.9 %collective-permute-start.3 = (f32[2,8,512]{2,1,0:T(8,128)S(1)}, f32[2,8,512]{2,1,0:T(8,128)S(1)}, u32[]{:S(2)}, u32[]{:S(2)}) collective-permute-start(f32[2,8,512]{2,1,0:T(8,128)S(1)} %pad_maximum_fusion.2), channel_id=1, source_target_pairs={{16,0},{24,8},{0,16},{8,24},{17,1},{25,9},{1,17},{9,25},{18,2},{26... | collective-permute-start | bytes 98312 | tf_op jit(solution)/shard_map/ppermute | solution.py:23
  16.3 15.9 %copy-start.1 = (f32[1,3,16,4096]{3,2,1,0:T(8,128)S(1)}, f32[1,3,16,4096]{3,2,1,0:T(8,128)}, u32[]{:S(2)}) copy-start(f32[1,3,16,4096]{3,2,1,0:T(8,128)} %heads.5) | copy-start | bytes 2359300
  16.3 15.9 %collective-permute-start.4 = (f32[3,16,2176]{2,1,0:T(8,128)}, f32[3,16,2176]{2,1,0:T(8,128)S(1)}, u32[]{:S(2)}, u32[]{:S(2)}) collective-permute-start(f32[3,16,2176]{2,1,0:T(8,128)} %heads.3), channel_id=1, source_target_pairs={{8,0},{0,8},{24,16},{16,24},{9,1},{1,9},{25,17},{17,25},{10,2},{2,... | collective-permute-start | bytes 1253384 | tf_op jit(solution)/shard_map/ppermute | solution.py:23
  32.0 14.3 %collective-permute-start.8 = (f32[2,16,2048]{2,1,0:T(8,128)S(1)}, f32[2,16,2048]{2,1,0:T(8,128)S(1)}, u32[]{:S(2)}, u32[]{:S(2)}) collective-permute-start(f32[2,16,2048]{2,1,0:T(8,128)S(1)} %get-tuple-element.18), channel_id=1, source_target_pairs={{8,0},{0,8},{24,16},{16,24},{9,1},{1,9},{25,17},{17,25},{10,2},{2,... | collective-permute-start | bytes 786440 | tf_op jit(solution)/shard_map/ppermute | solution.py:23
  33.4 3.0 %collective-permute-start.5 = (f32[8,128]{1,0:T(8,128)S(1)}, f32[8,128]{1,0:T(8,128)S(1)}, u32[]{:S(2)}, u32[]{:S(2)}) collective-permute-start(f32[8,128]{1,0:T(8,128)S(1)} %get-tuple-element.16), channel_id=1, source_target_pairs={{1,0},{0,1},{3,2},{2,3},{5,4},{4,5},{7,6},{6,7},{9,8},{8,9},{11,10... | collective-permute-start | bytes 12296 | tf_op jit(solution)/shard_map/ppermute | solution.py:23
  36.5 3.6 %collective-permute-start.6 = (f32[8,128]{1,0:T(8,128)S(1)}, f32[8,128]{1,0:T(8,128)S(1)}, u32[]{:S(2)}, u32[]{:S(2)}) collective-permute-start(f32[8,128]{1,0:T(8,128)S(1)} %add.22), channel_id=1, source_target_pairs={{2,0},{3,1},{0,2},{1,3},{6,4},{7,5},{4,6},{5,7},{10,8},{11,9},{8,1... | collective-permute-start | bytes 12296 | tf_op jit(solution)/shard_map/ppermute | solution.py:23
  40.1 6.2 %collective-permute-start.7 = (f32[8,128]{1,0:T(8,128)S(1)}, f32[8,128]{1,0:T(8,128)S(1)}, u32[]{:S(2)}, u32[]{:S(2)}) collective-permute-start(f32[8,128]{1,0:T(8,128)S(1)} %add.23), channel_id=1, source_target_pairs={{4,0},{5,1},{6,2},{7,3},{0,4},{1,5},{2,6},{3,7},{12,8},{13,9},{14,... | collective-permute-start | bytes 12296 | tf_op jit(solution)/shard_map/ppermute | solution.py:23
  42.7 9.5 %collective-permute-start.9 = (f32[16,1024]{1,0:T(8,128)S(1)}, f32[16,1024]{1,0:T(8,128)S(1)}, u32[]{:S(2)}, u32[]{:S(2)}) collective-permute-start(f32[16,1024]{1,0:T(8,128)S(1)} %get-tuple-element.20), channel_id=1, source_target_pairs={{0,0},{8,16},{16,8},{24,24},{1,1},{9,17},{17,9},{25,25},{2,2},{10,... | collective-permute-start | bytes 196616 | tf_op jit(solution)/shard_map/ppermute | solution.py:439
  43.4 8.9 %collective-permute-start.10 = (f32[16,1024]{1,0:T(8,128)S(1)}, f32[16,1024]{1,0:T(8,128)S(1)}, u32[]{:S(2)}, u32[]{:S(2)}) collective-permute-start(f32[16,1024]{1,0:T(8,128)S(1)} %get-tuple-element.21), channel_id=1, source_target_pairs={{0,8},{8,24},{16,0},{24,16},{1,9},{9,25},{17,1},{25,17},{2,10},{10... | collective-permute-start | bytes 196616 | tf_op jit(solution)/shard_map/ppermute | solution.py:439
  47.2 3.6 %collective-permute-start.11 = (f32[8,128]{1,0:T(8,128)S(1)}, f32[8,128]{1,0:T(8,128)S(1)}, u32[]{:S(2)}, u32[]{:S(2)}) collective-permute-start(f32[8,128]{1,0:T(8,128)S(1)} %add.24), channel_id=1, source_target_pairs={{8,0},{0,8},{24,16},{16,24},{9,1},{1,9},{25,17},{17,25},{10,2},{2,... | collective-permute-start | bytes 12296 | tf_op jit(solution)/shard_map/ppermute | solution.py:23
  50.8 4.5 %collective-permute-start.12 = (f32[8,128]{1,0:T(8,128)S(1)}, f32[8,128]{1,0:T(8,128)S(1)}, u32[]{:S(2)}, u32[]{:S(2)}) collective-permute-start(f32[8,128]{1,0:T(8,128)S(1)} %add.27), channel_id=1, source_target_pairs={{16,0},{24,8},{0,16},{8,24},{17,1},{25,9},{1,17},{9,25},{18,2},{26... | collective-permute-start | bytes 12296 | tf_op jit(solution)/shard_map/ppermute | solution.py:23

commit v3 on v2

v3 whole, which is shorter than its diff:
```python
import functools

import jax
import jax.numpy as jnp
from jax import lax
from jax.experimental import pallas as pl
from jax.experimental.pallas import tpu as pltpu
from jax.sharding import PartitionSpec as P

BLOCK = 128
STEPS = 2
SWEEPS = 2
LANES = 128
WIDE = 256
PIECES = 3
UNROLL = 32
F32 = jnp.float32
BF16 = jnp.bfloat16
VMEM_LIMIT = 24 * 2**20


def fetch(value, axis, hop):
    count = lax.axis_size(axis)
    return lax.ppermute(value, axis, [(i ^ hop, i) for i in range(count)])


def gather(value, axis):
    blocks, hop = (value[None], 1)
    while 2 * hop < lax.axis_size(axis):
        blocks = jnp.concatenate([blocks, fetch(blocks, axis, hop)], axis=0)
        hop *= 2
    return blocks, fetch(blocks, axis, hop)


def total(value, axis, hop=1, until=None):
    while hop < (until or lax.axis_size(axis)):
        value = value + fetch(value, axis, hop)
        hop *= 2
    return value


def inner_pairs(value):
    count = lax.axis_size("tile")
    pairs = [(i, i ^ 1) for i in range(count) if i ^ 1 < count]
    return lax.ppermute(value, "tile", pairs)


def outer_pairs(value):
    count = lax.axis_size("tile")
    low = range(1, count - 1, 2)
    return lax.ppermute(value, "tile", [(i, i + 1) for i in low] + [(i + 1, i) for i in low])


class Plan:
    def __init__(self, rows, width, sections, members, observed):
        self.rows, self.width, self.sections = (rows, width, sections)
        self.members, self.observed = (members, observed)
        self.half = width // 2
        sweeps = sections * STEPS * SWEEPS
        self.halo = -(-sweeps // LANES) * LANES
        self.window = self.half + self.halo
        self.tiles = self.window // LANES
        self.ext = 3 * rows
        self.per_phase = max(1, rows // (STEPS * SWEEPS))
        self.groups = sections // 2
        self.out_columns = width // sections

    def start(self, index):
        return pl.multiple_of((index % 2) * (self.half - self.halo), LANES)

    def own(self, index):
        return pl.multiple_of((index % 2) * self.halo, LANES)

    def bands(self, count):
        return [(number, number * STEPS * SWEEPS // 4 * 4) for number in range(count)]


def run_copies(copies, sems):
    started = [pltpu.make_async_copy(a, b, sems.at[i]) for i, (a, b) in enumerate(copies)]
    for copy in started:
        copy.start()
    for copy in started:
        copy.wait()


def pack_kernel(plan, capacity, cond_row, cond_col, terminal, packed, room, into, out):
    columns = pl.ds(plan.start(lax.axis_index("tm")), plan.window)
    fields = pl.ds(3, plan.members)
    parts = [(ref.at[:, columns], i) for i, ref in enumerate((capacity, cond_row, cond_col))]
    parts.append((terminal.at[:, :, columns], fields))
    loads = [pltpu.make_async_copy(ref, room.at[i], into.at[k]) for k, (ref, i) in enumerate(parts)]
    stores = [pltpu.make_async_copy(room.at[i], packed.at[i], out.at[k]) for k, (_, i) in enumerate(parts)]
    for load in loads:
        load.start()
    for load, store in zip(loads, stores):
        load.wait()
        store.start()
    for store in stores:
        store.wait()


def lines_kernel(plan, cells, weights, lines):
    at = 0
    for step in range(STEPS):
        place = cells[0, step : step + 1].astype(F32)
        row = jnp.floor((place + 0.5) * (1.0 / plan.width))
        lines[at : at + 1] = row
        lines[at + 1 : at + 2] = place - row * plan.width
        lines[at + 2 : at + 2 + plan.members] = weights[0, step]
        at += 2 + plan.members


def heads_kernel(plan, heads, out, sems):
    others = pl.ds(plan.start(lax.axis_index("tm") + 1), plan.window)
    run_copies([(heads.at[0, :, :, others], out)], sems)


def force_kernel(plan, top, count, obs_near, obs_far, force):
    me = lax.axis_index("tm")
    tile = lax.axis_index("tile")
    start = plan.start(me)
    members, observed = (plan.members, plan.observed)
    wides = -(-plan.window // WIDE)

    def observe(number, step, low, height):
        block = (top - number) ^ me
        split = plan.sections // 2
        near = obs_near[jnp.minimum(block, split - 1)]
        lines = jnp.where(block < split, near, obs_far[jnp.maximum(block - split, 0)])
        first = (2 + members) * step
        row = lines[first : first + 1] - ((tile - 1) * plan.rows + low).astype(F32)
        col = lines[first + 1 : first + 2] - start.astype(F32)
        inside = (row >= 0.0) & (row < height) & (col >= 0.0) & (col < plan.window)
        group = jnp.floor(col * (1.0 / WIDE))
        key = jnp.where(inside, group * height + row, -1.0).astype(jnp.int32)
        within = (col - group * WIDE).astype(jnp.int32)
        hit = lax.broadcasted_iota(jnp.int32, (wides * height, observed), 0) == key
        left = []
        for m in range(members):
            weight = lines[first + 2 + m : first + 3 + m]
            parts = []
            for _ in range(PIECES):
                piece = weight.astype(BF16).astype(F32)
                parts.append(jnp.where(hit, piece, 0.0).astype(BF16))
                weight = weight - piece
            left.append(jnp.concatenate(parts, axis=1))
        place = lax.broadcasted_iota(jnp.int32, (WIDE, observed), 0)
        right = jnp.where(place == within, 1.0, 0.0).astype(BF16)
        found = lax.dot_general(
            jnp.concatenate(left, axis=0),
            jnp.concatenate([right] * PIECES, axis=1),
            (((1,), (1,)), ((), ())),
            preferred_element_type=F32,
        )
        for m in range(members):
            for t in range(plan.tiles):
                at = (m * wides + t * LANES // WIDE) * height
                lane = t * LANES % WIDE
                force[number, step, m, t, :height, :] = found[at : at + height, lane : lane + LANES]

    for number, low in plan.bands(count):
        for step in range(STEPS):
            observe(number, step, low, plan.ext - 2 * low)


def chain_kernel(plan, top, count, mask, packed_in, inner, outer, force, *rest):
    first = top == plan.sections - 1
    if not first:
        field, field_inner, field_outer = rest[:3]
        rest = rest[3:]
    history, mine, send, own_capacity, east, west, south, north, act_rd, cap_rd, x0, x1, rhs, packed, sem = rest
    copy = pltpu.make_async_copy(packed_in, packed, sem)
    copy.start()
    me = lax.axis_index("tm")
    tile = lax.axis_index("tile")
    rows, ext, members, tiles = (plan.rows, plan.ext, plan.members, plan.tiles)
    start = plan.start(me)
    even = tile % 2 == 0

    def stacked(own, core, chip, index, columns):
        a, b = (core[index, :, columns], chip[index, :, columns])
        parts = [jnp.where(even, b, a), own[index, :, columns], jnp.where(even, a, b)]
        return jnp.concatenate(parts, axis=0)

    lane = lax.broadcasted_iota(jnp.int32, (1, LANES), 1)
    ends = lane == LANES - 1
    begins = lane == 0
    tile_rows = lax.axis_size("tile") * rows

    def chunk_active(chunk, column):
        if column >= tiles:
            return jnp.float32(0.0)
        row = (tile + chunk - 1) * rows
        inside = (row >= 0) & (row < tile_rows)
        block = jnp.clip(row, 0, tile_rows - 1) // BLOCK
        value = mask[block, (start + column * LANES) // BLOCK]
        return jnp.where(inside, value, 0).astype(F32)

    def active(column):
        parts = [jnp.full((rows, LANES), chunk_active(chunk, column), F32) for chunk in range(3)]
        return jnp.concatenate(parts, axis=0)

    def cols(column):
        return pl.ds(column * LANES, LANES)

    row_id = lax.broadcasted_iota(jnp.int32, (ext, LANES), 0)
    act = active(0)
    previous = jnp.zeros((ext, LANES), F32)
    copy.wait()
    own_capacity[...] = packed[0]
    for c in range(tiles):
        act_next = active(c + 1)
        pair = act * jnp.where(ends, act_next, act)
        e = stacked(packed, inner, outer, 1, cols(c)) * pair
        w = pltpu.roll(jnp.where(ends, previous, e), 1, axis=1)
        below = jnp.where(row_id == ext - 1, 0.0, pltpu.roll(act, ext - 1, axis=0))
        s = stacked(packed, inner, outer, 2, cols(c)) * act * below
        n = jnp.where(row_id == 0, 0.0, pltpu.roll(s, 1, axis=0))
        cap = stacked(packed, inner, outer, 0, cols(c))
        diagonal = cap + e + w + s + n
        inverse = jnp.where(diagonal > 0.0, 1.0 / jnp.where(diagonal > 0.0, diagonal, 1.0), 0.0)
        east[c] = e * inverse
        west[c] = w * inverse
        south[c] = s * inverse
        north[c] = n * inverse
        act_rd[c] = act * inverse
        cap_rd[c] = act * cap * inverse
        for m in range(members):
            if first:
                x0[m, c] = stacked(packed, inner, outer, 3 + m, cols(c))
            else:
                x0[m, c] = stacked(field, field_inner, field_outer, m, cols(c))
        previous = e
        act = act_next

    def sweep(source, target, low, number, step, initial):
        depth = (ext - 2 * low) // 8
        every = range(depth)
        pairs = [(m, v) for m in range(members) for v in every]

        def rows_of(v, first=low):
            return pl.ds(first + v, 8, stride=depth)

        def load(c):
            return [source[m, c, rows_of(v), :] for m, v in pairs]

        def group(first, length):
            before = load(first - 1) if not isinstance(first, int) or first else None
            here = load(first)
            for c in [first + i for i in range(length)]:
                after = load(c + 1) if not isinstance(c, int) or c + 1 < tiles else here
                before = before or here
                for v in every:
                    e, w, s, n = (ref[c, rows_of(v), :] for ref in (east, west, south, north))
                    if initial:
                        a, k = (act_rd[c, rows_of(v), :], cap_rd[c, rows_of(v), :])
                    for m in range(members):
                        at = m * depth + v
                        x = here[m * depth : (m + 1) * depth]
                        x_east = pltpu.roll(jnp.where(begins, after[at], x[v]), LANES - 1, axis=1)
                        x_west = pltpu.roll(jnp.where(ends, before[at], x[v]), 1, axis=1)
                        x_south = x[v + 1] if v + 1 < depth else pltpu.roll(x[0], 7, axis=0)
                        x_north = x[v - 1] if v else pltpu.roll(x[depth - 1], 1, axis=0)
                        if initial:
                            value = k * x[v] + a * force[number, step, m, c, rows_of(v, 0), :]
                            rhs[m, c, rows_of(v), :] = value
                        else:
                            value = rhs[m, c, rows_of(v), :]
                        value = value + e * x_east + w * x_west + s * x_south + n * x_north
                        target[m, c, rows_of(v), :] = value
                before, here = (here, after)

        if UNROLL >= tiles:
            group(0, tiles)
        else:
            group(0, 1)
            turns = (tiles - 2) // UNROLL
            lax.fori_loop(0, turns, lambda i, _: group(i * UNROLL + 1, UNROLL), None)
            group(1 + turns * UNROLL, tiles - 1 - turns * UNROLL)

    lowest = me - me % 2

    def one_section(number, low):
        slot = jnp.clip(top - number - lowest, 0, 1)
        for step in reversed(range(STEPS)):
            refs = (x0, x1)
            for index in range(SWEEPS):
                sweep(refs[index % 2], refs[(index + 1) % 2], low, number, step, index == 0)
            if SWEEPS % 2:
                x0[...] = x1[...]

            @pl.when(top - number - lowest < 2)
            def _():
                for c in range(tiles):
                    history[slot, step, :, :, cols(c)] = x0[:, c, rows : 2 * rows, :]

    for number, low in plan.bands(count):
        pl.when(top - number >= lowest)(functools.partial(one_section, number, low))

    own = pl.ds(plan.own(me), plan.half)
    mine[...] = history[me % 2, 0, :, :, own]
    send[...] = history[1 - me % 2, 0, :, :, own]


def window_of_heads(plan, heads, other_heads, step, columns, which):
    if which:
        return other_heads[step, :, columns]
    start = plan.start(lax.axis_index("tm"))
    return heads[0, step, :, pl.ds(pl.multiple_of(start + columns.start, LANES), columns.size)]


def storage_kernel(plan, own_capacity, history, heads, other_heads, out):
    me = lax.axis_index("tm")
    members = plan.members
    stored = [jnp.zeros((plan.rows, LANES), F32) for _ in range(members)]
    for t in range(plan.half // LANES):
        here = pl.ds(pl.multiple_of(plan.own(me) + t * LANES, LANES), LANES)
        capacity = own_capacity[:, here]
        for which in range(2):
            section = me % 2 if which == 0 else 1 - me % 2
            levels = [window_of_heads(plan, heads, other_heads, k, here, which) for k in range(STEPS + 1)]
            for step in range(STEPS):
                rise = capacity * (levels[step + 1] - levels[step])
                for m in range(members):
                    stored[m] = stored[m] + history[section, step, m, :, here] * rise
    out[...] = jnp.zeros((8, LANES), F32)
    for m in range(members):
        out[m : m + 1, :] = jnp.full((1, LANES), jnp.sum(stored[m]), F32)


def cond_kernel(plan, mask, history, heads, other_heads, *outs):
    me = lax.axis_index("tm")
    tile = lax.axis_index("tile")
    rows, members = (plan.rows, plan.members)
    start, own = (plan.start(me), plan.own(me))
    side, group = (me % 2, me // 2)
    ends = lax.broadcasted_iota(jnp.int32, (1, LANES), 1) == LANES - 1
    block_row = tile * rows // BLOCK
    columns = plan.width // LANES

    def after(here, following):
        return jnp.where(ends, pltpu.roll(following, LANES - 1, axis=1), pltpu.roll(here, LANES - 1, axis=1))

    def lanes(offset):
        return pl.ds(pl.multiple_of(offset, LANES), LANES)

    for slot, out in enumerate(outs):
        for t in range(plan.out_columns // LANES):
            here = own + (group ^ slot) * plan.out_columns + t * LANES
            there = jnp.minimum(here + LANES, plan.window - LANES)
            column = (start + here) // LANES
            act = mask[block_row, column].astype(F32)
            act_next = mask[block_row, jnp.minimum(column + 1, columns - 1)].astype(F32)
            act_next = jnp.where(column + 1 < columns, act_next, 0.0)
            pair = act * jnp.where(ends, act_next, act)
            sens = jnp.zeros((rows, LANES), F32)
            for which in range(2):
                section = side if which == 0 else 1 - side
                for step in range(STEPS):
                    level = window_of_heads(plan, heads, other_heads, step + 1, lanes(here), which)
                    level_next = window_of_heads(plan, heads, other_heads, step + 1, lanes(there), which)
                    both = functools.reduce(jnp.add, [history[section, step, m, :, lanes(here)] for m in range(members)])
                    follow = [history[section, step, m, :, lanes(there)] for m in range(members)]
                    both_next = functools.reduce(jnp.add, follow)
                    sens = sens + (after(both, both_next) - both) * (after(level, level_next) - level)
            out[:, t * LANES : (t + 1) * LANES] = sens * pair


def shards(heads, capacity, cond_row, cond_col, terminal, obs_cell, obs_weight, block_mask):
    rows, width = capacity.shape
    members = terminal.shape[0]
    sections = lax.axis_size("tm")
    plan = Plan(rows, width, sections, members, obs_cell.shape[2])
    window, ext, half = (plan.window, plan.ext, plan.half)
    me = lax.axis_index("tm")
    anywhere = pl.BlockSpec(memory_space=pl.ANY)
    in_vmem = pl.BlockSpec(memory_space=pltpu.VMEM)
    in_smem = pl.BlockSpec(memory_space=pltpu.SMEM)
    params = pltpu.CompilerParams(vmem_limit_bytes=VMEM_LIMIT)

    def shape(*dims):
        return jax.ShapeDtypeStruct(dims, F32)

    packed = pl.pallas_call(
        functools.partial(pack_kernel, plan),
        out_shape=shape(3 + members, rows, window),
        in_specs=[anywhere] * 4,
        out_specs=anywhere,
        scratch_shapes=[
            pltpu.VMEM((3 + members, rows, window), F32),
            pltpu.SemaphoreType.DMA((4,)),
            pltpu.SemaphoreType.DMA((4,)),
        ],
        name="pack",
    )(capacity, cond_row, cond_col, terminal)
    later_weight, _ = lax.optimization_barrier((obs_weight, packed))
    lines = pl.pallas_call(
        functools.partial(lines_kernel, plan),
        out_shape=shape(STEPS * (2 + members), plan.observed),
        in_specs=[in_vmem] * 2,
        out_specs=in_vmem,
        name="lines",
    )(obs_cell, later_weight)
    head_send = pl.pallas_call(
        functools.partial(heads_kernel, plan),
        out_shape=shape(STEPS + 1, rows, window),
        in_specs=[anywhere],
        out_specs=in_vmem,
        scratch_shapes=[pltpu.SemaphoreType.DMA((1,))],
        name="heads",
    )(heads)
    outer = outer_pairs(packed)
    inner = inner_pairs(packed)
    lines, inner = lax.optimization_barrier((lines, inner))
    obs = gather(lines, "tm")
    *obs, head_send = lax.optimization_barrier((*obs, head_send))
    other_heads = fetch(head_send, "tm", 1)

    part = (members, rows, half)
    top = sections - 1
    field = []
    results = None
    while top >= 0:
        count = min(plan.per_phase, top + 1)
        force = pl.pallas_call(
            functools.partial(force_kernel, plan, top, count),
            out_shape=shape(count, STEPS, members, plan.tiles, ext, LANES),
            in_specs=[in_vmem] * 2,
            out_specs=in_vmem,
            compiler_params=params,
            name="force",
        )(*obs)
        plane = pltpu.VMEM((plan.tiles, ext, LANES), F32)
        fields = pltpu.VMEM((members, plan.tiles, ext, LANES), F32)
        now = pl.pallas_call(
            functools.partial(chain_kernel, plan, top, count),
            out_shape=[shape(2, STEPS, members, rows, window), shape(*part), shape(*part), shape(rows, window)],
            in_specs=[in_smem, anywhere] + [in_vmem] * (3 + len(field)),
            out_specs=[in_vmem] * 4,
            scratch_shapes=[
                *([plane] * 6),
                *([fields] * 3),
                pltpu.VMEM((3 + members, rows, window), F32),
                pltpu.SemaphoreType.DMA,
            ],
            compiler_params=params,
            name="chain",
        )(block_mask, packed, inner, outer, force, *field)
        if results is None:
            results = now
        else:
            results = [jnp.where(me - me % 2 > top, a, b) for a, b in zip(results, now)]
        top -= count
        if top >= 0:
            reached = now[0][0, 0]
            field = [reached, inner_pairs(reached), outer_pairs(reached)]
    history, mine, send, own_capacity = results

    storage = pl.pallas_call(
        functools.partial(storage_kernel, plan),
        out_shape=shape(8, LANES),
        in_specs=[in_vmem] * 4,
        out_specs=in_vmem,
        compiler_params=params,
        name="storage",
    )(own_capacity, history, heads, other_heads)
    storage, send = lax.optimization_barrier((storage, send))
    other = fetch(send, "tm", 1)
    cond = pl.pallas_call(
        functools.partial(cond_kernel, plan),
        out_shape=[shape(rows, plan.out_columns)] * plan.groups,
        in_specs=[in_smem] + [in_vmem] * 3,
        out_specs=[in_vmem] * plan.groups,
        compiler_params=params,
        name="cond",
    )(block_mask, history, heads, other_heads)

    storage = total(storage, "tile", until=4)
    storage, *cond = lax.optimization_barrier((storage, *cond))
    groups = plan.groups
    parts = []
    for slot in range(groups):
        moves = [(i, (i % 2) * groups + (i // 2 ^ slot)) for i in range(sections)]
        parts.append(lax.ppermute(cond[slot], "tm", moves))
    storage = total(storage, "tile", hop=4)
    storage = total(storage, "tm", until=2)
    side = me % 2
    halves = [jnp.where(side == 0, mine, other), jnp.where(side == 0, other, mine)]
    adjoint = jnp.concatenate(halves, axis=2)
    storage, adjoint = lax.optimization_barrier((storage, adjoint))
    storage = total(storage, "tm", hop=2)
    cond = functools.reduce(jnp.add, parts)
    return (adjoint[None], cond, storage[:members, 0])


def solution(mesh):
    placed = (
        P("tm", None, "tile", None),
        P("tile", None),
        P("tile", None),
        P("tile", None),
        P(None, "tile", None),
        P("tm", None, None),
        P("tm", None, None, None),
        P(),
    )
    return jax.shard_map(
        shards,
        mesh=mesh,
        in_specs=placed,
        out_specs=(P("tm", None, "tile", None), P("tile", "tm"), P()),
        check_vma=False,
    )
```

time: 56.4 us -> 52.4 us (0.929)
  waiting for transfers between devices: 10.5 us -> 7.32 us
  Pallas kernels: 20.1 us -> 18.5 us
  starting transfers between devices: 20.9 us -> 22.5 us
  other arithmetic: 2.97 us -> 2.24 us
    ppermute x9, waiting for transfers between devices: 10.5 us -> 5.37 us  [fetch(): return lax.ppermute(value, axis, [(i ^ hop, i) for i in range(count)])]
    ppermute x2, waiting for transfers between devices: 0.01 us -> 1.94 us  [shards(): parts.append(lax.ppermute(cond[slot], 'tm', moves))]
    ppermute x9, starting transfers between devices: 16.2 us -> 17.7 us  [fetch(): return lax.ppermute(value, axis, [(i ^ hop, i) for i in range(count)])]
    pallas_call x1, Pallas kernels: 8.22 us -> 7.33 us  [shards(): pl.pallas_call(functools.partial(chain_kernel, plan, top, count), out_sha...]
    pallas_call x1, Pallas kernels: 5.49 us -> 4.62 us  [shards(): pl.pallas_call(functools.partial(force_kernel, plan, top, count), out_sha...]
    concatenate x2 -> x1, other arithmetic: 1.44 us -> 0.72 us  [gather(): blocks = jnp.concatenate([blocks, fetch(blocks, axis, hop)], axis=0)]
    pallas_call x1 -> x2, Pallas kernels: 1.26 us -> 1.53 us  [the longest x1 1.19 us: shards(): pl.pallas_call(functools.partial(cond_kernel, plan), out_shape=[shape(row...]
  transfers between devices with their start and end apart: 13 -> 13, of which waited for: 6 -> 7; matrix products, arithmetic and copies ran while one was open for 5% -> 4% of each run, Pallas kernels for 32% -> 31%
where the time goes in v3:
time: 52.4 us; the launch traced here: 52.1 us
  starting transfers between devices  22.5 us (43%)
  Pallas kernels  18.5 us (35%)
  waiting for transfers between devices  7.32 us (14%)
  other arithmetic  2.24 us (4%)
  between operations  0.78 us (1%)
  local copies, waits for them, and re-layouts  0.64 us (1%)
    ppermute x9, starting transfers between devices, fetch(): return lax.ppermute(value, axis, [(i ^ hop, i) for i in range(count)])  17.7 us
    pallas_call x1, Pallas kernels, shards(): pl.pallas_call(functools.partial(chain_kernel, plan, top, count), out_sha...  7.33 us
    ppermute x9, waiting for transfers between devices, fetch(): return lax.ppermute(value, axis, [(i ^ hop, i) for i in range(count)])  5.37 us
    pallas_call x1, Pallas kernels, shards(): pl.pallas_call(functools.partial(force_kernel, plan, top, count), out_sha...  4.62 us
    ppermute x2, starting transfers between devices, shards(): parts.append(lax.ppermute(cond[slot], 'tm', moves))  3.67 us
    pallas_call x1, Pallas kernels, shards(): pl.pallas_call(functools.partial(pack_kernel, plan), out_shape=shape(3 +...  1.96 us
    ppermute x2, waiting for transfers between devices, shards(): parts.append(lax.ppermute(cond[slot], 'tm', moves))  1.94 us
    pallas_call x1, Pallas kernels, shards(): pl.pallas_call(functools.partial(heads_kernel, plan), out_shape=shape(STE...  1.76 us
  transfers between devices with their start and end apart: 13, of which 7 were waited for; matrix products, arithmetic and copies ran while one was open for 4% of the time, Pallas kernels for 31%

profile of v3, /device:TPU:0, one launch (start us, length us, event | category | flops | bytes accessed | tf_op | source)
XLA Modules:
  0.0 52.1 jit_solution(12897161457751663603)
XLA Ops:
  0.6 0.0 copy-start.2
  0.6 2.0 %pack.1.packed_in = f32[5,16,2176]{2,1,0:T(8,128)} custom-call(f32[16,4096]{1,0:T(8,128)} %capacity.1, f32[16,4096]{1,0:T(8,128)} %cond_row.1, f32[16,4096]{1,0:T(8,128)} %cond_col.1, f32[2,16,4096]{2,1,0:T(8,128)} %terminal.1), custom_call_target="tpu_custom_call" | custom-call | tf_op jit(solution)/shard_map/pack/pallas_call | solution.py:384
  2.6 0.0 copy-start.1
  2.6 0.5 collective-permute-start
  3.1 0.7 %collective-permute-start.1 = (f32[5,16,2176]{2,1,0:T(8,128)}, f32[5,16,2176]{2,1,0:T(8,128)S(1)}, u32[]{:S(2)}, u32[]{:S(2)}) collective-permute-start(f32[5,16,2176]{2,1,0:T(8,128)} %pack.1.packed_in), channel_id=1, source_target_pairs={{1,2},{3,4},{5,6},{2,1},{4,3},{6,5},{9,10},{11,12},{13,14},{10,9},... | collective-permute-start | bytes 2088968 | tf_op jit(solution)/shard_map/ppermute | solution.py:51
  3.8 1.3 %lines.1 = f32[8,512]{1,0:T(8,128)} custom-call(s32[1,2,512]{2,1,0:T(2,128)} %cells.1, f32[1,2,2,512]{3,2,1,0:T(2,128)} %weights), custom_call_target="tpu_custom_call" | custom-call | tf_op jit(solution)/shard_map/lines/pallas_call | solution.py:397
  5.2 0.0 collective-permute-done.inner
  5.2 2.9 %collective-permute-start.2 = (f32[1,8,512]{2,1,0:T(8,128)}, f32[1,8,512]{2,1,0:T(8,128)S(1)}, u32[]{:S(2)}, u32[]{:S(2)}) collective-permute-start(f32[1,8,512]{2,1,0:T(8,128)} %bitcast.3), channel_id=1, source_target_pairs={{8,0},{0,8},{24,16},{16,24},{9,1},{1,9},{25,17},{17,25},{10,2},{2,... | collective-permute-start | bytes 49160 | tf_op jit(solution)/shard_map/ppermute | solution.py:24
  8.1 1.9 %collective-permute-done.2 = f32[1,8,512]{2,1,0:T(8,128)S(1)} collective-permute-done((f32[1,8,512]{2,1,0:T(8,128)}, f32[1,8,512]{2,1,0:T(8,128)S(1)}, u32[]{:S(2)}, u32[]{:S(2)}) %collective-permute-start.2) | collective-permute-done | bytes 16416 | tf_op jit(solution)/shard_map/ppermute | solution.py:24
  10.0 0.7 %pad_maximum_fusion.1.obs_near = f32[2,8,512]{2,1,0:T(8,128)S(1)} fusion(f32[1,8,512]{2,1,0:T(8,128)S(1)} %collective-permute-done.2, f32[1,8,512]{2,1,0:T(8,128)} %bitcast.4), kind=kLoop, calls=%fused_computation.3 | loop fusion | flops 8192 | bytes 65536 | tf_op jit(solution)/shard_map/concatenate | solution.py:30
  10.7 3.0 %collective-permute-start.3 = (f32[2,8,512]{2,1,0:T(8,128)S(1)}, f32[2,8,512]{2,1,0:T(8,128)S(1)}, u32[]{:S(2)}, u32[]{:S(2)}) collective-permute-start(f32[2,8,512]{2,1,0:T(8,128)S(1)} %pad_maximum_fusion.1.obs_near), channel_id=1, source_target_pairs={{16,0},{24,8},{0,16},{8,24},{17,1},{25,9},{1,17},{9,25},{18,2},{26... | collective-permute-start | bytes 98312 | tf_op jit(solution)/shard_map/ppermute | solution.py:24
  13.8 1.8 %heads.4 = f32[3,16,2176]{2,1,0:T(8,128)} custom-call(f32[1,3,16,4096]{3,2,1,0:T(8,128)} %heads.7), custom_call_target="tpu_custom_call" | custom-call | tf_op jit(solution)/shard_map/heads/pallas_call | solution.py:404
  15.5 0.0 copy-start
  15.5 0.1 collective-permute-done.3.obs_far
  15.7 1.9 %collective-permute-start.4 = (f32[3,16,2176]{2,1,0:T(8,128)}, f32[3,16,2176]{2,1,0:T(8,128)S(1)}, u32[]{:S(2)}, u32[]{:S(2)}) collective-permute-start(f32[3,16,2176]{2,1,0:T(8,128)} %heads.4), channel_id=1, source_target_pairs={{8,0},{0,8},{24,16},{16,24},{9,1},{1,9},{25,17},{17,25},{10,2},{2,... | collective-permute-start | bytes 1253384 | tf_op jit(solution)/shard_map/ppermute | solution.py:24
  17.6 4.6 %force.1 = f32[4,2,2,17,48,128]{5,4,3,2,1,0:T(8,128)S(1)} custom-call(f32[2,8,512]{2,1,0:T(8,128)S(1)} %pad_maximum_fusion.1.obs_near, f32[2,8,512]{2,1,0:T(8,128)S(1)} %collective-permute-done.3.obs_far), custom_call_target="tpu_custom_call" | custom-call | tf_op jit(solution)/shard_map/force/pallas_call | solution.py:425
  22.2 0.0 collective-permute-done.1.outer
  22.2 0.0 copy-done.2
  22.2 0.0 copy-done.1
  22.2 7.3 %chain.1 = (f32[2,2,2,16,2176]{4,3,2,1,0:T(8,128)S(1)}, f32[2,16,2048]{2,1,0:T(8,128)S(1)}, f32[2,16,2048]{2,1,0:T(8,128)S(1)}, f32[16,2176]{1,0:T(8,128)S(1)}) custom-call(s32[1,32]{1,0:T(1,128)S(1)} %copy-done.2, f32[5,16,2176]{2,1,0:T(8,128)S(1)} %copy-done.1, f32[5,16,2176]{2,1,0:T(8,128)S(1)} %collective-permute-done.inner, ...), custom_call_target="tpu_custom_call" | custom-call | tf_op jit(solution)/shard_map/chain/pallas_call | solution.py:435
  29.6 0.0 collective-permute-done.4.other_heads
  29.6 0.0 copy-done
  29.6 0.3 storage.1
  29.9 0.6 %collective-permute-start.9 = (f32[2,16,2048]{2,1,0:T(8,128)S(1)}, f32[2,16,2048]{2,1,0:T(8,128)S(1)}, u32[]{:S(2)}, u32[]{:S(2)}) collective-permute-start(f32[2,16,2048]{2,1,0:T(8,128)S(1)} %get-tuple-element.36), channel_id=1, source_target_pairs={{8,0},{0,8},{24,16},{16,24},{9,1},{1,9},{25,17},{17,25},{10,2},{2,... | collective-permute-start | bytes 786440 | tf_op jit(solution)/shard_map/ppermute | solution.py:24
  30.6 3.1 %collective-permute-start.5 = (f32[8,128]{1,0:T(8,128)S(1)}, f32[8,128]{1,0:T(8,128)S(1)}, u32[]{:S(2)}, u32[]{:S(2)}) collective-permute-start(f32[8,128]{1,0:T(8,128)S(1)} %storage.1), channel_id=1, source_target_pairs={{1,0},{0,1},{3,2},{2,3},{5,4},{4,5},{7,6},{6,7},{9,8},{8,9},{11,10... | collective-permute-start | bytes 12296 | tf_op jit(solution)/shard_map/ppermute | solution.py:24
  33.7 0.8 %collective-permute-done.5 = f32[8,128]{1,0:T(8,128)S(1)} collective-permute-done((f32[8,128]{1,0:T(8,128)S(1)}, f32[8,128]{1,0:T(8,128)S(1)}, u32[]{:S(2)}, u32[]{:S(2)}) %collective-permute-start.5) | collective-permute-done | bytes 4128 | tf_op jit(solution)/shard_map/ppermute | solution.py:24
  34.5 2.0 %collective-permute-start.6 = (f32[8,128]{1,0:T(8,128)S(1)}, f32[8,128]{1,0:T(8,128)S(1)}, u32[]{:S(2)}, u32[]{:S(2)}) collective-permute-start(f32[8,128]{1,0:T(8,128)S(1)} %add.22), channel_id=1, source_target_pairs={{2,0},{3,1},{0,2},{1,3},{6,4},{7,5},{4,6},{5,7},{10,8},{11,9},{8,1... | collective-permute-start | bytes 12296 | tf_op jit(solution)/shard_map/ppermute | solution.py:24
  36.5 1.2 %cond.1 = (f32[16,1024]{1,0:T(8,128)S(1)}, f32[16,1024]{1,0:T(8,128)S(1)}) custom-call(s32[1,32]{1,0:T(1,128)S(1)} %copy-done.2, f32[2,2,2,16,2176]{4,3,2,1,0:T(8,128)S(1)} %get-tuple-element.28.history, f32[1,3,16,4096]{3,2,1,0:T(8,128)S(1)} %copy-done, f32[3,16,2176]{2,1,0:T(8,128)S(1)} %collective-permute-done.4.other_heads), custom_call_target="tpu_custom_call" | custom-call | tf_op jit(solution)/shard_map/cond/pallas_call | solution.py:469
  37.7 0.4 collective-permute-done.6
  38.1 2.3 %collective-permute-start.7 = (f32[8,128]{1,0:T(8,128)S(1)}, f32[8,128]{1,0:T(8,128)S(1)}, u32[]{:S(2)}, u32[]{:S(2)}) collective-permute-start(f32[8,128]{1,0:T(8,128)S(1)} %add.23), channel_id=1, source_target_pairs={{4,0},{5,1},{6,2},{7,3},{0,4},{1,5},{2,6},{3,7},{12,8},{13,9},{14,... | collective-permute-start | bytes 12296 | tf_op jit(solution)/shard_map/ppermute | solution.py:24
  40.4 1.6 %collective-permute-done.7 = f32[8,128]{1,0:T(8,128)S(1)} collective-permute-done((f32[8,128]{1,0:T(8,128)S(1)}, f32[8,128]{1,0:T(8,128)S(1)}, u32[]{:S(2)}, u32[]{:S(2)}) %collective-permute-start.7) | collective-permute-done | bytes 4128 | tf_op jit(solution)/shard_map/ppermute | solution.py:24
  42.0 0.3 collective-permute-start.8
  42.3 0.7 %collective-permute-start.10 = (f32[16,1024]{1,0:T(8,128)S(1)}, f32[16,1024]{1,0:T(8,128)S(1)}, u32[]{:S(2)}, u32[]{:S(2)}) collective-permute-start(f32[16,1024]{1,0:T(8,128)S(1)} %get-tuple-element.38), channel_id=1, source_target_pairs={{0,0},{8,16},{16,8},{24,24},{1,1},{9,17},{17,9},{25,25},{2,2},{10,... | collective-permute-start | bytes 196616 | tf_op jit(solution)/shard_map/ppermute | solution.py:484
  43.0 3.0 %collective-permute-start.11 = (f32[16,1024]{1,0:T(8,128)S(1)}, f32[16,1024]{1,0:T(8,128)S(1)}, u32[]{:S(2)}, u32[]{:S(2)}) collective-permute-start(f32[16,1024]{1,0:T(8,128)S(1)} %get-tuple-element.39), channel_id=1, source_target_pairs={{0,8},{8,24},{16,0},{24,16},{1,9},{9,25},{17,1},{25,17},{2,10},{10... | collective-permute-start | bytes 196616 | tf_op jit(solution)/shard_map/ppermute | solution.py:484
  46.0 0.0 collective-permute-done.8
  46.0 0.0 collective-permute-done.9
  46.1 0.8 %pad_maximum_fusion = f32[2,16,4096]{2,1,0:T(8,128)} fusion(f32[2,16,2048]{2,1,0:T(8,128)S(1)} %get-tuple-element.42, f32[2,16,2048]{2,1,0:T(8,128)S(1)} %get-tuple-element.41), kind=kLoop, calls=%fused_computation | loop fusion | flops 131072 | bytes 1048576 | tf_op jit(solution)/shard_map/concatenate | solution.py:489
  46.9 1.5 %collective-permute-start.12 = (f32[8,128]{1,0:T(8,128)S(1)}, f32[8,128]{1,0:T(8,128)S(1)}, u32[]{:S(2)}, u32[]{:S(2)}) collective-permute-start(f32[8,128]{1,0:T(8,128)S(1)} %add.25), channel_id=1, source_target_pairs={{16,0},{24,8},{0,16},{8,24},{17,1},{25,9},{1,17},{9,25},{18,2},{26... | collective-permute-start | bytes 12296 | tf_op jit(solution)/shard_map/ppermute | solution.py:24
  48.4 0.0 collective-permute-done.10
  48.4 1.9 %collective-permute-done.11 = f32[16,1024]{1,0:T(8,128)S(1)} collective-permute-done((f32[16,1024]{1,0:T(8,128)S(1)}, f32[16,1024]{1,0:T(8,128)S(1)}, u32[]{:S(2)}, u32[]{:S(2)}) %collective-permute-start.11) | collective-permute-done | bytes 65568 | tf_op jit(solution)/shard_map/ppermute | solution.py:484
  50.3 0.6 %add.27 = f32[16,1024]{1,0:T(8,128)} add(f32[16,1024]{1,0:T(8,128)S(1)} %collective-permute-done.10, f32[16,1024]{1,0:T(8,128)S(1)} %collective-permute-done.11) | non-fusion elementwise | flops 16384 | bytes 196608 | tf_op jit(solution)/shard_map/add | solution.py:492
  51.0 0.5 collective-permute-done.12
  51.4 0.6 %slice_reduce_fusion = f32[2]{0:T(128)} fusion(f32[8,128]{1,0:T(8,128)S(1)} %add.28), kind=kLoop, calls=%fused_computation.4 | loop fusion | bytes 16 | tf_op jit(solution)/shard_map/slice | solution.py:493
  (6 shorter events, 0.1 us)
Async XLA Ops:
  0.6 21.6 %copy-start.2 = (s32[1,32]{1,0:T(1,128)S(1)}, s32[1,32]{1,0:T(1,128)}, u32[]{:S(2)}) copy-start(s32[1,32]{1,0:T(1,128)} %mask.3) | copy-start | bytes 388
  2.6 19.6 %copy-start.1 = (f32[5,16,2176]{2,1,0:T(8,128)S(1)}, f32[5,16,2176]{2,1,0:T(8,128)}, u32[]{:S(2)}) copy-start(f32[5,16,2176]{2,1,0:T(8,128)} %pack.1.packed_in) | copy-start | bytes 2088964
  2.6 2.6 %collective-permute-start = (f32[5,16,2176]{2,1,0:T(8,128)}, f32[5,16,2176]{2,1,0:T(8,128)S(1)}, u32[]{:S(2)}, u32[]{:S(2)}) collective-permute-start(f32[5,16,2176]{2,1,0:T(8,128)} %pack.1.packed_in), channel_id=1, source_target_pairs={{0,1},{1,0},{2,3},{3,2},{4,5},{5,4},{6,7},{7,6},{8,9},{9,8},{10,11... | collective-permute-start | bytes 2088968 | tf_op jit(solution)/shard_map/ppermute | solution.py:45
  3.1 19.1 %collective-permute-start.1 = (f32[5,16,2176]{2,1,0:T(8,128)}, f32[5,16,2176]{2,1,0:T(8,128)S(1)}, u32[]{:S(2)}, u32[]{:S(2)}) collective-permute-start(f32[5,16,2176]{2,1,0:T(8,128)} %pack.1.packed_in), channel_id=1, source_target_pairs={{1,2},{3,4},{5,6},{2,1},{4,3},{6,5},{9,10},{11,12},{13,14},{10,9},... | collective-permute-start | bytes 2088968 | tf_op jit(solution)/shard_map/ppermute | solution.py:51
  5.2 4.8 %collective-permute-start.2 = (f32[1,8,512]{2,1,0:T(8,128)}, f32[1,8,512]{2,1,0:T(8,128)S(1)}, u32[]{:S(2)}, u32[]{:S(2)}) collective-permute-start(f32[1,8,512]{2,1,0:T(8,128)} %bitcast.3), channel_id=1, source_target_pairs={{8,0},{0,8},{24,16},{16,24},{9,1},{1,9},{25,17},{17,25},{10,2},{2,... | collective-permute-start | bytes 49160 | tf_op jit(solution)/shard_map/ppermute | solution.py:24
  10.7 4.9 %collective-permute-start.3 = (f32[2,8,512]{2,1,0:T(8,128)S(1)}, f32[2,8,512]{2,1,0:T(8,128)S(1)}, u32[]{:S(2)}, u32[]{:S(2)}) collective-permute-start(f32[2,8,512]{2,1,0:T(8,128)S(1)} %pad_maximum_fusion.1.obs_near), channel_id=1, source_target_pairs={{16,0},{24,8},{0,16},{8,24},{17,1},{25,9},{1,17},{9,25},{18,2},{26... | collective-permute-start | bytes 98312 | tf_op jit(solution)/shard_map/ppermute | solution.py:24
  15.5 14.0 %copy-start = (f32[1,3,16,4096]{3,2,1,0:T(8,128)S(1)}, f32[1,3,16,4096]{3,2,1,0:T(8,128)}, u32[]{:S(2)}) copy-start(f32[1,3,16,4096]{3,2,1,0:T(8,128)} %heads.7) | copy-start | bytes 2359300
  15.7 13.9 %collective-permute-start.4 = (f32[3,16,2176]{2,1,0:T(8,128)}, f32[3,16,2176]{2,1,0:T(8,128)S(1)}, u32[]{:S(2)}, u32[]{:S(2)}) collective-permute-start(f32[3,16,2176]{2,1,0:T(8,128)} %heads.4), channel_id=1, source_target_pairs={{8,0},{0,8},{24,16},{16,24},{9,1},{1,9},{25,17},{17,25},{10,2},{2,... | collective-permute-start | bytes 1253384 | tf_op jit(solution)/shard_map/ppermute | solution.py:24
  29.9 16.1 %collective-permute-start.9 = (f32[2,16,2048]{2,1,0:T(8,128)S(1)}, f32[2,16,2048]{2,1,0:T(8,128)S(1)}, u32[]{:S(2)}, u32[]{:S(2)}) collective-permute-start(f32[2,16,2048]{2,1,0:T(8,128)S(1)} %get-tuple-element.36), channel_id=1, source_target_pairs={{8,0},{0,8},{24,16},{16,24},{9,1},{1,9},{25,17},{17,25},{10,2},{2,... | collective-permute-start | bytes 786440 | tf_op jit(solution)/shard_map/ppermute | solution.py:24
  30.6 3.9 %collective-permute-start.5 = (f32[8,128]{1,0:T(8,128)S(1)}, f32[8,128]{1,0:T(8,128)S(1)}, u32[]{:S(2)}, u32[]{:S(2)}) collective-permute-start(f32[8,128]{1,0:T(8,128)S(1)} %storage.1), channel_id=1, source_target_pairs={{1,0},{0,1},{3,2},{2,3},{5,4},{4,5},{7,6},{6,7},{9,8},{8,9},{11,10... | collective-permute-start | bytes 12296 | tf_op jit(solution)/shard_map/ppermute | solution.py:24
  34.5 3.6 %collective-permute-start.6 = (f32[8,128]{1,0:T(8,128)S(1)}, f32[8,128]{1,0:T(8,128)S(1)}, u32[]{:S(2)}, u32[]{:S(2)}) collective-permute-start(f32[8,128]{1,0:T(8,128)S(1)} %add.22), channel_id=1, source_target_pairs={{2,0},{3,1},{0,2},{1,3},{6,4},{7,5},{4,6},{5,7},{10,8},{11,9},{8,1... | collective-permute-start | bytes 12296 | tf_op jit(solution)/shard_map/ppermute | solution.py:24
  38.1 3.9 %collective-permute-start.7 = (f32[8,128]{1,0:T(8,128)S(1)}, f32[8,128]{1,0:T(8,128)S(1)}, u32[]{:S(2)}, u32[]{:S(2)}) collective-permute-start(f32[8,128]{1,0:T(8,128)S(1)} %add.23), channel_id=1, source_target_pairs={{4,0},{5,1},{6,2},{7,3},{0,4},{1,5},{2,6},{3,7},{12,8},{13,9},{14,... | collective-permute-start | bytes 12296 | tf_op jit(solution)/shard_map/ppermute | solution.py:24
  42.0 4.0 %collective-permute-start.8 = (f32[8,128]{1,0:T(8,128)S(1)}, f32[8,128]{1,0:T(8,128)S(1)}, u32[]{:S(2)}, u32[]{:S(2)}) collective-permute-start(f32[8,128]{1,0:T(8,128)S(1)} %add.24), channel_id=1, source_target_pairs={{8,0},{0,8},{24,16},{16,24},{9,1},{1,9},{25,17},{17,25},{10,2},{2,... | collective-permute-start | bytes 12296 | tf_op jit(solution)/shard_map/ppermute | solution.py:24
  42.3 6.1 %collective-permute-start.10 = (f32[16,1024]{1,0:T(8,128)S(1)}, f32[16,1024]{1,0:T(8,128)S(1)}, u32[]{:S(2)}, u32[]{:S(2)}) collective-permute-start(f32[16,1024]{1,0:T(8,128)S(1)} %get-tuple-element.38), channel_id=1, source_target_pairs={{0,0},{8,16},{16,8},{24,24},{1,1},{9,17},{17,9},{25,25},{2,2},{10,... | collective-permute-start | bytes 196616 | tf_op jit(solution)/shard_map/ppermute | solution.py:484
  43.0 7.3 %collective-permute-start.11 = (f32[16,1024]{1,0:T(8,128)S(1)}, f32[16,1024]{1,0:T(8,128)S(1)}, u32[]{:S(2)}, u32[]{:S(2)}) collective-permute-start(f32[16,1024]{1,0:T(8,128)S(1)} %get-tuple-element.39), channel_id=1, source_target_pairs={{0,8},{8,24},{16,0},{24,16},{1,9},{9,25},{17,1},{25,17},{2,10},{10... | collective-permute-start | bytes 196616 | tf_op jit(solution)/shard_map/ppermute | solution.py:484
  46.9 4.5 %collective-permute-start.12 = (f32[8,128]{1,0:T(8,128)S(1)}, f32[8,128]{1,0:T(8,128)S(1)}, u32[]{:S(2)}, u32[]{:S(2)}) collective-permute-start(f32[8,128]{1,0:T(8,128)S(1)} %add.25), channel_id=1, source_target_pairs={{16,0},{24,8},{0,16},{8,24},{17,1},{25,9},{1,17},{9,25},{18,2},{26... | collective-permute-start | bytes 12296 | tf_op jit(solution)/shard_map/ppermute | solution.py:24

commit v4 on v3

--- a/solution.py
+++ b/solution.py
@@ -484,11 +484,12 @@
         parts.append(lax.ppermute(cond[slot], "tm", moves))
     storage = total(storage, "tile", hop=4)
     storage = total(storage, "tm", until=2)
+    storage, other = lax.optimization_barrier((storage, other))
+    storage = total(storage, "tm", hop=2)
+    mine, other, parts[0] = lax.optimization_barrier((mine, other, parts[0]))
     side = me % 2
     halves = [jnp.where(side == 0, mine, other), jnp.where(side == 0, other, mine)]
     adjoint = jnp.concatenate(halves, axis=2)
-    storage, adjoint = lax.optimization_barrier((storage, adjoint))
-    storage = total(storage, "tm", hop=2)
     cond = functools.reduce(jnp.add, parts)
     return (adjoint[None], cond, storage[:members, 0])
 

time: 52.4 us -> 52.3 us (level)
    ppermute x2, starting transfers between devices: 3.67 us -> 0.69 us  [shards(): parts.append(lax.ppermute(cond[slot], 'tm', moves))]
    ppermute x9, starting transfers between devices: 17.7 us -> 20.6 us  [fetch(): return lax.ppermute(value, axis, [(i ^ hop, i) for i in range(count)])]
    ppermute x2, waiting for transfers between devices: 1.94 us -> 0.01 us  [shards(): parts.append(lax.ppermute(cond[slot], 'tm', moves))]
    ppermute x9, waiting for transfers between devices: 5.37 us -> 7.24 us  [fetch(): return lax.ppermute(value, axis, [(i ^ hop, i) for i in range(count)])]
    broadcast_in_dim x0 -> x1, other arithmetic: none -> 0.83 us  [shards(): return (adjoint[None], cond, storage[:members, 0])]
    concatenate x1 -> x0, other arithmetic: 0.83 us -> none  [shards(): adjoint = jnp.concatenate(halves, axis=2)]
where the time goes in v4:
time: 52.3 us; the launch traced here: 51.9 us
  starting transfers between devices  22.5 us (43%)
  Pallas kernels  18.5 us (35%)
  waiting for transfers between devices  7.25 us (14%)
  other arithmetic  2.24 us (4%)
  between operations  0.78 us (1%)
  local copies, waits for them, and re-layouts  0.64 us (1%)
    ppermute x9, starting transfers between devices, fetch(): return lax.ppermute(value, axis, [(i ^ hop, i) for i in range(count)])  20.6 us
    pallas_call x1, Pallas kernels, shards(): pl.pallas_call(functools.partial(chain_kernel, plan, top, count), out_sha...  7.33 us
    ppermute x9, waiting for transfers between devices, fetch(): return lax.ppermute(value, axis, [(i ^ hop, i) for i in range(count)])  7.24 us
    pallas_call x1, Pallas kernels, shards(): pl.pallas_call(functools.partial(force_kernel, plan, top, count), out_sha...  4.62 us
    pallas_call x1, Pallas kernels, shards(): pl.pallas_call(functools.partial(pack_kernel, plan), out_shape=shape(3 +...  1.96 us
    pallas_call x1, Pallas kernels, shards(): pl.pallas_call(functools.partial(heads_kernel, plan), out_shape=shape(STE...  1.76 us
    pallas_call x1, Pallas kernels, shards(): pl.pallas_call(functools.partial(lines_kernel, plan), out_shape=shape(STE...  1.33 us
    pallas_call x1, Pallas kernels, shards(): pl.pallas_call(functools.partial(cond_kernel, plan), out_shape=[shape(row...  1.19 us
  transfers between devices with their start and end apart: 13, of which 7 were waited for; matrix products, arithmetic and copies ran while one was open for 4% of the time, Pallas kernels for 31%

profile of v4, /device:TPU:0, one launch (start us, length us, event | category | flops | bytes accessed | tf_op | source)
XLA Modules:
  0.0 51.9 jit_solution(13364287189300291457)
XLA Ops:
  0.6 0.0 copy-start.2
  0.6 2.0 %pack.1.packed_in = f32[5,16,2176]{2,1,0:T(8,128)} custom-call(f32[16,4096]{1,0:T(8,128)} %capacity.1, f32[16,4096]{1,0:T(8,128)} %cond_row.1, f32[16,4096]{1,0:T(8,128)} %cond_col.1, f32[2,16,4096]{2,1,0:T(8,128)} %terminal.1), custom_call_target="tpu_custom_call" | custom-call | tf_op jit(solution)/shard_map/pack/pallas_call | solution.py:384
  2.6 0.0 copy-start.1
  2.6 0.5 collective-permute-start
  3.1 0.7 %collective-permute-start.1 = (f32[5,16,2176]{2,1,0:T(8,128)}, f32[5,16,2176]{2,1,0:T(8,128)S(1)}, u32[]{:S(2)}, u32[]{:S(2)}) collective-permute-start(f32[5,16,2176]{2,1,0:T(8,128)} %pack.1.packed_in), channel_id=1, source_target_pairs={{1,2},{3,4},{5,6},{2,1},{4,3},{6,5},{9,10},{11,12},{13,14},{10,9},... | collective-permute-start | bytes 2088968 | tf_op jit(solution)/shard_map/ppermute | solution.py:51
  3.8 1.3 %lines.1 = f32[8,512]{1,0:T(8,128)} custom-call(s32[1,2,512]{2,1,0:T(2,128)} %cells.1, f32[1,2,2,512]{3,2,1,0:T(2,128)} %weights), custom_call_target="tpu_custom_call" | custom-call | tf_op jit(solution)/shard_map/lines/pallas_call | solution.py:397
  5.2 0.0 collective-permute-done.inner
  5.2 2.9 %collective-permute-start.2 = (f32[1,8,512]{2,1,0:T(8,128)}, f32[1,8,512]{2,1,0:T(8,128)S(1)}, u32[]{:S(2)}, u32[]{:S(2)}) collective-permute-start(f32[1,8,512]{2,1,0:T(8,128)} %bitcast.3), channel_id=1, source_target_pairs={{8,0},{0,8},{24,16},{16,24},{9,1},{1,9},{25,17},{17,25},{10,2},{2,... | collective-permute-start | bytes 49160 | tf_op jit(solution)/shard_map/ppermute | solution.py:24
  8.1 1.9 %collective-permute-done.2 = f32[1,8,512]{2,1,0:T(8,128)S(1)} collective-permute-done((f32[1,8,512]{2,1,0:T(8,128)}, f32[1,8,512]{2,1,0:T(8,128)S(1)}, u32[]{:S(2)}, u32[]{:S(2)}) %collective-permute-start.2) | collective-permute-done | bytes 16416 | tf_op jit(solution)/shard_map/ppermute | solution.py:24
  10.0 0.7 %pad_maximum_fusion.obs_near = f32[2,8,512]{2,1,0:T(8,128)S(1)} fusion(f32[1,8,512]{2,1,0:T(8,128)S(1)} %collective-permute-done.2, f32[1,8,512]{2,1,0:T(8,128)} %bitcast.4), kind=kLoop, calls=%fused_computation.3 | loop fusion | flops 8192 | bytes 65536 | tf_op jit(solution)/shard_map/concatenate | solution.py:30
  10.7 3.0 %collective-permute-start.3 = (f32[2,8,512]{2,1,0:T(8,128)S(1)}, f32[2,8,512]{2,1,0:T(8,128)S(1)}, u32[]{:S(2)}, u32[]{:S(2)}) collective-permute-start(f32[2,8,512]{2,1,0:T(8,128)S(1)} %pad_maximum_fusion.obs_near), channel_id=1, source_target_pairs={{16,0},{24,8},{0,16},{8,24},{17,1},{25,9},{1,17},{9,25},{18,2},{26... | collective-permute-start | bytes 98312 | tf_op jit(solution)/shard_map/ppermute | solution.py:24
  13.8 1.8 %heads.4 = f32[3,16,2176]{2,1,0:T(8,128)} custom-call(f32[1,3,16,4096]{3,2,1,0:T(8,128)} %heads.7), custom_call_target="tpu_custom_call" | custom-call | tf_op jit(solution)/shard_map/heads/pallas_call | solution.py:404
  15.5 0.0 copy-start
  15.5 0.1 collective-permute-done.3.obs_far
  15.7 1.9 %collective-permute-start.4 = (f32[3,16,2176]{2,1,0:T(8,128)}, f32[3,16,2176]{2,1,0:T(8,128)S(1)}, u32[]{:S(2)}, u32[]{:S(2)}) collective-permute-start(f32[3,16,2176]{2,1,0:T(8,128)} %heads.4), channel_id=1, source_target_pairs={{8,0},{0,8},{24,16},{16,24},{9,1},{1,9},{25,17},{17,25},{10,2},{2,... | collective-permute-start | bytes 1253384 | tf_op jit(solution)/shard_map/ppermute | solution.py:24
  17.6 4.6 %force.1 = f32[4,2,2,17,48,128]{5,4,3,2,1,0:T(8,128)S(1)} custom-call(f32[2,8,512]{2,1,0:T(8,128)S(1)} %pad_maximum_fusion.obs_near, f32[2,8,512]{2,1,0:T(8,128)S(1)} %collective-permute-done.3.obs_far), custom_call_target="tpu_custom_call" | custom-call | tf_op jit(solution)/shard_map/force/pallas_call | solution.py:425
  22.2 0.0 collective-permute-done.1.outer
  22.2 0.0 copy-done.2
  22.2 0.0 copy-done.1
  22.2 7.3 %chain.1 = (f32[2,2,2,16,2176]{4,3,2,1,0:T(8,128)S(1)}, f32[2,16,2048]{2,1,0:T(8,128)S(1)}, f32[2,16,2048]{2,1,0:T(8,128)S(1)}, f32[16,2176]{1,0:T(8,128)S(1)}) custom-call(s32[1,32]{1,0:T(1,128)S(1)} %copy-done.2, f32[5,16,2176]{2,1,0:T(8,128)S(1)} %copy-done.1, f32[5,16,2176]{2,1,0:T(8,128)S(1)} %collective-permute-done.inner, ...), custom_call_target="tpu_custom_call" | custom-call | tf_op jit(solution)/shard_map/chain/pallas_call | solution.py:435
  29.6 0.0 collective-permute-done.4.other_heads
  29.6 0.0 copy-done
  29.6 0.3 storage.1
  29.9 0.6 %collective-permute-start.9 = (f32[2,16,2048]{2,1,0:T(8,128)S(1)}, f32[2,16,2048]{2,1,0:T(8,128)S(1)}, u32[]{:S(2)}, u32[]{:S(2)}) collective-permute-start(f32[2,16,2048]{2,1,0:T(8,128)S(1)} %get-tuple-element.39), channel_id=1, source_target_pairs={{8,0},{0,8},{24,16},{16,24},{9,1},{1,9},{25,17},{17,25},{10,2},{2,... | collective-permute-start | bytes 786440 | tf_op jit(solution)/shard_map/ppermute | solution.py:24
  30.6 3.1 %collective-permute-start.5 = (f32[8,128]{1,0:T(8,128)S(1)}, f32[8,128]{1,0:T(8,128)S(1)}, u32[]{:S(2)}, u32[]{:S(2)}) collective-permute-start(f32[8,128]{1,0:T(8,128)S(1)} %storage.1), channel_id=1, source_target_pairs={{1,0},{0,1},{3,2},{2,3},{5,4},{4,5},{7,6},{6,7},{9,8},{8,9},{11,10... | collective-permute-start | bytes 12296 | tf_op jit(solution)/shard_map/ppermute | solution.py:24
  33.7 0.8 %collective-permute-done.5 = f32[8,128]{1,0:T(8,128)S(1)} collective-permute-done((f32[8,128]{1,0:T(8,128)S(1)}, f32[8,128]{1,0:T(8,128)S(1)}, u32[]{:S(2)}, u32[]{:S(2)}) %collective-permute-start.5) | collective-permute-done | bytes 4128 | tf_op jit(solution)/shard_map/ppermute | solution.py:24
  34.5 2.0 %collective-permute-start.6 = (f32[8,128]{1,0:T(8,128)S(1)}, f32[8,128]{1,0:T(8,128)S(1)}, u32[]{:S(2)}, u32[]{:S(2)}) collective-permute-start(f32[8,128]{1,0:T(8,128)S(1)} %add.23), channel_id=1, source_target_pairs={{2,0},{3,1},{0,2},{1,3},{6,4},{7,5},{4,6},{5,7},{10,8},{11,9},{8,1... | collective-permute-start | bytes 12296 | tf_op jit(solution)/shard_map/ppermute | solution.py:24
  36.5 1.2 %cond.1 = (f32[16,1024]{1,0:T(8,128)S(1)}, f32[16,1024]{1,0:T(8,128)S(1)}) custom-call(s32[1,32]{1,0:T(1,128)S(1)} %copy-done.2, f32[2,2,2,16,2176]{4,3,2,1,0:T(8,128)S(1)} %get-tuple-element.32.history, f32[1,3,16,4096]{3,2,1,0:T(8,128)S(1)} %copy-done, f32[3,16,2176]{2,1,0:T(8,128)S(1)} %collective-permute-done.4.other_heads), custom_call_target="tpu_custom_call" | custom-call | tf_op jit(solution)/shard_map/cond/pallas_call | solution.py:469
  37.7 0.4 collective-permute-done.6
  38.1 0.7 %collective-permute-start.10 = (f32[16,1024]{1,0:T(8,128)S(1)}, f32[16,1024]{1,0:T(8,128)S(1)}, u32[]{:S(2)}, u32[]{:S(2)}) collective-permute-start(f32[16,1024]{1,0:T(8,128)S(1)} %get-tuple-element.41), channel_id=1, source_target_pairs={{0,0},{8,16},{16,8},{24,24},{1,1},{9,17},{17,9},{25,25},{2,2},{10,... | collective-permute-start | bytes 196616 | tf_op jit(solution)/shard_map/ppermute | solution.py:484
  38.8 2.4 %collective-permute-start.7 = (f32[8,128]{1,0:T(8,128)S(1)}, f32[8,128]{1,0:T(8,128)S(1)}, u32[]{:S(2)}, u32[]{:S(2)}) collective-permute-start(f32[8,128]{1,0:T(8,128)S(1)} %add.24), channel_id=1, source_target_pairs={{4,0},{5,1},{6,2},{7,3},{0,4},{1,5},{2,6},{3,7},{12,8},{13,9},{14,... | collective-permute-start | bytes 12296 | tf_op jit(solution)/shard_map/ppermute | solution.py:24
  41.1 1.6 %collective-permute-done.7 = f32[8,128]{1,0:T(8,128)S(1)} collective-permute-done((f32[8,128]{1,0:T(8,128)S(1)}, f32[8,128]{1,0:T(8,128)S(1)}, u32[]{:S(2)}, u32[]{:S(2)}) %collective-permute-start.7) | collective-permute-done | bytes 4128 | tf_op jit(solution)/shard_map/ppermute | solution.py:24
  42.7 2.0 %collective-permute-start.8 = (f32[8,128]{1,0:T(8,128)S(1)}, f32[8,128]{1,0:T(8,128)S(1)}, u32[]{:S(2)}, u32[]{:S(2)}) collective-permute-start(f32[8,128]{1,0:T(8,128)S(1)} %add.25), channel_id=1, source_target_pairs={{8,0},{0,8},{24,16},{16,24},{9,1},{1,9},{25,17},{17,25},{10,2},{2,... | collective-permute-start | bytes 12296 | tf_op jit(solution)/shard_map/ppermute | solution.py:24
  44.7 0.0 collective-permute-start.11
  44.8 2.0 %collective-permute-done.8 = f32[8,128]{1,0:T(8,128)S(1)} collective-permute-done((f32[8,128]{1,0:T(8,128)S(1)}, f32[8,128]{1,0:T(8,128)S(1)}, u32[]{:S(2)}, u32[]{:S(2)}) %collective-permute-start.8) | collective-permute-done | bytes 4128 | tf_op jit(solution)/shard_map/ppermute | solution.py:24
  46.8 0.0 collective-permute-done.9
  46.8 2.6 %collective-permute-start.12 = (f32[8,128]{1,0:T(8,128)S(1)}, f32[8,128]{1,0:T(8,128)S(1)}, u32[]{:S(2)}, u32[]{:S(2)}) collective-permute-start(f32[8,128]{1,0:T(8,128)S(1)} %add.26), channel_id=1, source_target_pairs={{16,0},{24,8},{0,16},{8,24},{17,1},{25,9},{1,17},{9,25},{18,2},{26... | collective-permute-start | bytes 12296 | tf_op jit(solution)/shard_map/ppermute | solution.py:24
  49.4 0.0 collective-permute-done.10
  49.4 0.8 %maximum_bitcast_fusion = f32[1,2,16,4096]{3,2,1,0:T(8,128)} fusion(f32[2,16,2048]{2,1,0:T(8,128)S(1)} %get-tuple-element.48, f32[2,16,2048]{2,1,0:T(8,128)S(1)} %get-tuple-element.47), kind=kLoop, calls=%fused_computation | loop fusion | flops 131072 | bytes 1048576 | tf_op jit(solution)/shard_map/broadcast_in_dim | solution.py:494
  50.3 0.0 collective-permute-done.11
  50.3 0.6 %add.27 = f32[16,1024]{1,0:T(8,128)} add(f32[16,1024]{1,0:T(8,128)S(1)} %collective-permute-done.10, f32[16,1024]{1,0:T(8,128)S(1)} %collective-permute-done.11) | non-fusion elementwise | flops 16384 | bytes 196608 | tf_op jit(solution)/shard_map/add | solution.py:493
  50.9 0.4 collective-permute-done.12
  51.3 0.6 %slice_reduce_fusion = f32[2]{0:T(128)} fusion(f32[8,128]{1,0:T(8,128)S(1)} %add.28), kind=kLoop, calls=%fused_computation.4 | loop fusion | bytes 16 | tf_op jit(solution)/shard_map/slice | solution.py:494
  (6 shorter events, 0.1 us)
Async XLA Ops:
  0.6 21.6 %copy-start.2 = (s32[1,32]{1,0:T(1,128)S(1)}, s32[1,32]{1,0:T(1,128)}, u32[]{:S(2)}) copy-start(s32[1,32]{1,0:T(1,128)} %mask.3) | copy-start | bytes 388
  2.6 19.6 %copy-start.1 = (f32[5,16,2176]{2,1,0:T(8,128)S(1)}, f32[5,16,2176]{2,1,0:T(8,128)}, u32[]{:S(2)}) copy-start(f32[5,16,2176]{2,1,0:T(8,128)} %pack.1.packed_in) | copy-start | bytes 2088964
  2.6 2.6 %collective-permute-start = (f32[5,16,2176]{2,1,0:T(8,128)}, f32[5,16,2176]{2,1,0:T(8,128)S(1)}, u32[]{:S(2)}, u32[]{:S(2)}) collective-permute-start(f32[5,16,2176]{2,1,0:T(8,128)} %pack.1.packed_in), channel_id=1, source_target_pairs={{0,1},{1,0},{2,3},{3,2},{4,5},{5,4},{6,7},{7,6},{8,9},{9,8},{10,11... | collective-permute-start | bytes 2088968 | tf_op jit(solution)/shard_map/ppermute | solution.py:45
  3.1 19.1 %collective-permute-start.1 = (f32[5,16,2176]{2,1,0:T(8,128)}, f32[5,16,2176]{2,1,0:T(8,128)S(1)}, u32[]{:S(2)}, u32[]{:S(2)}) collective-permute-start(f32[5,16,2176]{2,1,0:T(8,128)} %pack.1.packed_in), channel_id=1, source_target_pairs={{1,2},{3,4},{5,6},{2,1},{4,3},{6,5},{9,10},{11,12},{13,14},{10,9},... | collective-permute-start | bytes 2088968 | tf_op jit(solution)/shard_map/ppermute | solution.py:51
  5.2 4.8 %collective-permute-start.2 = (f32[1,8,512]{2,1,0:T(8,128)}, f32[1,8,512]{2,1,0:T(8,128)S(1)}, u32[]{:S(2)}, u32[]{:S(2)}) collective-permute-start(f32[1,8,512]{2,1,0:T(8,128)} %bitcast.3), channel_id=1, source_target_pairs={{8,0},{0,8},{24,16},{16,24},{9,1},{1,9},{25,17},{17,25},{10,2},{2,... | collective-permute-start | bytes 49160 | tf_op jit(solution)/shard_map/ppermute | solution.py:24
  10.7 4.9 %collective-permute-start.3 = (f32[2,8,512]{2,1,0:T(8,128)S(1)}, f32[2,8,512]{2,1,0:T(8,128)S(1)}, u32[]{:S(2)}, u32[]{:S(2)}) collective-permute-start(f32[2,8,512]{2,1,0:T(8,128)S(1)} %pad_maximum_fusion.obs_near), channel_id=1, source_target_pairs={{16,0},{24,8},{0,16},{8,24},{17,1},{25,9},{1,17},{9,25},{18,2},{26... | collective-permute-start | bytes 98312 | tf_op jit(solution)/shard_map/ppermute | solution.py:24
  15.5 14.0 %copy-start = (f32[1,3,16,4096]{3,2,1,0:T(8,128)S(1)}, f32[1,3,16,4096]{3,2,1,0:T(8,128)}, u32[]{:S(2)}) copy-start(f32[1,3,16,4096]{3,2,1,0:T(8,128)} %heads.7) | copy-start | bytes 2359300
  15.7 13.9 %collective-permute-start.4 = (f32[3,16,2176]{2,1,0:T(8,128)}, f32[3,16,2176]{2,1,0:T(8,128)S(1)}, u32[]{:S(2)}, u32[]{:S(2)}) collective-permute-start(f32[3,16,2176]{2,1,0:T(8,128)} %heads.4), channel_id=1, source_target_pairs={{8,0},{0,8},{24,16},{16,24},{9,1},{1,9},{25,17},{17,25},{10,2},{2,... | collective-permute-start | bytes 1253384 | tf_op jit(solution)/shard_map/ppermute | solution.py:24
  29.9 16.8 %collective-permute-start.9 = (f32[2,16,2048]{2,1,0:T(8,128)S(1)}, f32[2,16,2048]{2,1,0:T(8,128)S(1)}, u32[]{:S(2)}, u32[]{:S(2)}) collective-permute-start(f32[2,16,2048]{2,1,0:T(8,128)S(1)} %get-tuple-element.39), channel_id=1, source_target_pairs={{8,0},{0,8},{24,16},{16,24},{9,1},{1,9},{25,17},{17,25},{10,2},{2,... | collective-permute-start | bytes 786440 | tf_op jit(solution)/shard_map/ppermute | solution.py:24
  30.6 3.9 %collective-permute-start.5 = (f32[8,128]{1,0:T(8,128)S(1)}, f32[8,128]{1,0:T(8,128)S(1)}, u32[]{:S(2)}, u32[]{:S(2)}) collective-permute-start(f32[8,128]{1,0:T(8,128)S(1)} %storage.1), channel_id=1, source_target_pairs={{1,0},{0,1},{3,2},{2,3},{5,4},{4,5},{7,6},{6,7},{9,8},{8,9},{11,10... | collective-permute-start | bytes 12296 | tf_op jit(solution)/shard_map/ppermute | solution.py:24
  34.5 3.6 %collective-permute-start.6 = (f32[8,128]{1,0:T(8,128)S(1)}, f32[8,128]{1,0:T(8,128)S(1)}, u32[]{:S(2)}, u32[]{:S(2)}) collective-permute-start(f32[8,128]{1,0:T(8,128)S(1)} %add.23), channel_id=1, source_target_pairs={{2,0},{3,1},{0,2},{1,3},{6,4},{7,5},{4,6},{5,7},{10,8},{11,9},{8,1... | collective-permute-start | bytes 12296 | tf_op jit(solution)/shard_map/ppermute | solution.py:24
  38.1 11.3 %collective-permute-start.10 = (f32[16,1024]{1,0:T(8,128)S(1)}, f32[16,1024]{1,0:T(8,128)S(1)}, u32[]{:S(2)}, u32[]{:S(2)}) collective-permute-start(f32[16,1024]{1,0:T(8,128)S(1)} %get-tuple-element.41), channel_id=1, source_target_pairs={{0,0},{8,16},{16,8},{24,24},{1,1},{9,17},{17,9},{25,25},{2,2},{10,... | collective-permute-start | bytes 196616 | tf_op jit(solution)/shard_map/ppermute | solution.py:484
  38.8 4.0 %collective-permute-start.7 = (f32[8,128]{1,0:T(8,128)S(1)}, f32[8,128]{1,0:T(8,128)S(1)}, u32[]{:S(2)}, u32[]{:S(2)}) collective-permute-start(f32[8,128]{1,0:T(8,128)S(1)} %add.24), channel_id=1, source_target_pairs={{4,0},{5,1},{6,2},{7,3},{0,4},{1,5},{2,6},{3,7},{12,8},{13,9},{14,... | collective-permute-start | bytes 12296 | tf_op jit(solution)/shard_map/ppermute | solution.py:24
  42.7 4.0 %collective-permute-start.8 = (f32[8,128]{1,0:T(8,128)S(1)}, f32[8,128]{1,0:T(8,128)S(1)}, u32[]{:S(2)}, u32[]{:S(2)}) collective-permute-start(f32[8,128]{1,0:T(8,128)S(1)} %add.25), channel_id=1, source_target_pairs={{8,0},{0,8},{24,16},{16,24},{9,1},{1,9},{25,17},{17,25},{10,2},{2,... | collective-permute-start | bytes 12296 | tf_op jit(solution)/shard_map/ppermute | solution.py:24
  44.7 5.5 %collective-permute-start.11 = (f32[16,1024]{1,0:T(8,128)S(1)}, f32[16,1024]{1,0:T(8,128)S(1)}, u32[]{:S(2)}, u32[]{:S(2)}) collective-permute-start(f32[16,1024]{1,0:T(8,128)S(1)} %get-tuple-element.45), channel_id=1, source_target_pairs={{0,8},{8,24},{16,0},{24,16},{1,9},{9,25},{17,1},{25,17},{2,10},{10... | collective-permute-start | bytes 196616 | tf_op jit(solution)/shard_map/ppermute | solution.py:484
  46.8 4.5 %collective-permute-start.12 = (f32[8,128]{1,0:T(8,128)S(1)}, f32[8,128]{1,0:T(8,128)S(1)}, u32[]{:S(2)}, u32[]{:S(2)}) collective-permute-start(f32[8,128]{1,0:T(8,128)S(1)} %add.26), channel_id=1, source_target_pairs={{16,0},{24,8},{0,16},{8,24},{17,1},{25,9},{1,17},{9,25},{18,2},{26... | collective-permute-start | bytes 12296 | tf_op jit(solution)/shard_map/ppermute | solution.py:24
